TPU v7x, 128 devices: a whole 4x4x4 slice. The times are simulated.
128 devices in a mesh: date: 4 (over z), row: 8 (over x, y_hi), col: 4 (over y_lo, core).
Axes of the slice: x: 4, y: 4 (y_hi: 2, y_lo: 2; y = y_hi * 2 + y_lo), z: 4, core: 2. Of those that a mesh axis runs over, the one named last changes fastest.
Arguments:
- pixels: bfloat16 [16, 64, 64, 704], P('date', 'row', 'col'), may hold values from -8 to 8
- window_query_key_value_weight: bfloat16 [704, 2112], replicated, may hold values from -1 to 1
- head_logit_scale: float32 [22], replicated, may hold values from 5 to 100
- bias_network_first: float32 [2, 512], replicated, may hold values from -4 to 4
- bias_network_second: float32 [512, 22], replicated, may hold values from -0.25 to 0.25
- window_output_weight: bfloat16 [704, 704], replicated, may hold values from -0.21875 to 0.21875
- attention_norm_gain: float32 [704], replicated, may hold values from 0.5 to 1.5
- feedforward_up_weight: bfloat16 [704, 2816], replicated, may hold values from -0.21875 to 0.21875
- feedforward_down_weight: bfloat16 [2816, 704], replicated, may hold values from -0.109375 to 0.109375
- feedforward_norm_gain: float32 [704], replicated, may hold values from 0.5 to 1.5
- temporal_norm_gain: float32 [704], replicated, may hold values from 0.5 to 8
- date_rank_embedding: float32 [16, 704], replicated, may hold values from -3 to 3
- acquisition_rank: int32 [16], replicated, may hold values from 0 to 15, each once
- temporal_query_key_value_weight: bfloat16 [704, 2112], replicated, may hold values from -1 to 1
- temporal_output_weight: bfloat16 [704, 704], replicated, may hold values from -0.21875 to 0.21875
Outputs:
- refined: bfloat16 [16, 64, 64, 704], P('date', 'row', 'col')
Inputs may be any that keep to these rules, and one draw needn't show every extreme that they name: `acquisition_rank`: each of the 16 ranks appears once.
All inputs are finite; a program needn't handle non-finite values.
Results may differ from a plain program's by a relative error of at most 0.02.
Values may be sent and summed in bfloat16 or wider, within the bound.
No kernel may reach another device: no remote copies, remote signals or barrier semaphores. Data moves between devices by JAX's collectives and lax.ppermute only.
A program may use at most 192 MiB of HBM per device.

v0:
```python
import functools
import math

import jax
import jax.numpy as jnp
from jax import lax
from jax.experimental import pallas as pl
from jax.experimental.pallas import tpu as pltpu
from jax.sharding import PartitionSpec as P

WINDOW = 8
SHIFT = 4
POSITIONS = WINDOW * WINDOW
PAIR = 2 * POSITIONS
MASKED = -1000000000.0
FULL_PRECISION = lax.Precision.HIGHEST
BF16 = jnp.bfloat16
F32 = jnp.float32
MIB = 1024 * 1024

VMEM = pl.BlockSpec(memory_space=pltpu.VMEM)
SMEM = pl.BlockSpec(memory_space=pltpu.SMEM)
ANY = pl.BlockSpec(memory_space=pl.ANY)


def dot(a, b):
    return jnp.dot(a, b, preferred_element_type=F32)


def dot_first(a, b):
    return lax.dot_general(a, b, (((0,), (0,)), ((), ())), preferred_element_type=F32)


def dot_last(a, b):
    return lax.dot_general(a, b, (((1,), (1,)), ((), ())), preferred_element_type=F32)


def layer_norm(vector, gain):
    average = jnp.mean(vector, axis=-1, keepdims=True)
    centred = vector - average
    variance = jnp.mean(centred * centred, axis=-1, keepdims=True)
    return centred * lax.rsqrt(variance + 1e-05) * gain


def gelu(x):
    return 0.5 * x * (1.0 + lax.erf(x * math.sqrt(0.5)))


def column_blocks(total, width):
    return [(start, min(start + width, total)) for start in range(0, total, width)]


def project(tokens, weight, queries, keys, values):
    features = weight.shape[0]
    lead = features // 128 * 128
    edge = 2 * features
    for first, last in column_blocks(weight.shape[1], 256):
        block = dot(tokens, weight[:, first:last]).astype(BF16)
        if first < features:
            stop = min(last, features)
            queries[first:stop, :] = block.T[: stop - first]
        start, stop = max(first, lead), min(last, edge)
        if start < stop:
            keys[:, start - lead : stop - lead] = block[:, start - first : stop - first]
        if last > edge:
            start = max(first, edge)
            values[start - edge : last - edge, :] = block[:, start - first :].T


def head_blocks(heads, size, features):
    offset = features % 128
    blocks = []
    for start in range(0, heads * size + offset, 128):
        blocks.append(
            [
                (h, offset + h * size - start)
                for h in range(heads)
                if start <= offset + h * size < start + 128
            ]
        )
    return blocks


def spread_queries(queries, block, size, span):
    columns = []
    for h, start in block:
        parts = [queries[h * size : (h + 1) * size, span]]
        if start:
            parts.insert(0, jnp.zeros((start, 128), BF16))
        if start + size < 128:
            parts.append(jnp.zeros((128 - size - start, 128), BF16))
        columns.append(jnp.concatenate(parts, axis=0))
    return jnp.concatenate(columns, axis=1)


def staggered(units, early, late):
    ready = early(units[0])
    for i, unit in enumerate(units):
        held = ready
        if i + 1 < len(units):
            ready = early(units[i + 1])
        late(unit, held)


def pack(pixels, low, high, low_right, high_right, work):
    dates, rows, cols, features = pixels.shape
    half = rows // 2
    for d in range(dates):
        work[...] = pixels[d].astype(F32)
        for first, out, right in ((half, low, low_right), (0, high, high_right)):
            lines = range(first, first + half)
            inner = [work[i, SHIFT : SHIFT + WINDOW, :] for i in lines]
            outer = [work[i, cols - SHIFT : cols, :] for i in lines]
            out[d] = jnp.concatenate(inner + outer, axis=0).astype(BF16)
            right[d] = jnp.concatenate([work[i, :SHIFT, :] for i in lines], axis=0).astype(BF16)


def bias_kernel(first, second, out, table):
    units = first.shape[1]
    heads = second.shape[0]
    layer = jnp.concatenate([first[...], jnp.zeros((6, units), F32)], axis=0).T
    lane = lax.broadcasted_iota(jnp.int32, (1, 128), 1)

    def mapped(offset):
        distance = offset.astype(F32) * (8.0 / (WINDOW - 1))
        size = jnp.log(jnp.abs(distance) + 1.0) * (1.0 / (3.0 * math.log(2.0)))
        return jnp.where(distance < 0, -size, size)

    row_part = layer[:, 0:1] * mapped(lax.shift_right_logical(lane, 3) - (WINDOW - 1))
    col_weight = jnp.broadcast_to(layer[:, 1:2], (units, 128))
    for col in range(WINDOW):
        hidden = jnp.maximum(row_part + col_weight * mapped((lane & 7) - col), 0.0)
        logits = jnp.dot(second[...], hidden, precision=FULL_PRECISION, preferred_element_type=F32)
        table[col * 32 : col * 32 + heads, :] = 16.0 / (1.0 + jnp.exp(-logits))
    wide = lax.broadcasted_iota(jnp.int32, (WINDOW, 128), 1)
    for h in range(heads):
        lines = table[pl.ds(h, WINDOW, stride=32), :]
        for row in range(WINDOW):
            start = (WINDOW - 1 - row) * WINDOW
            left = pltpu.roll(lines, (128 - start) % 128, 1)
            right = pltpu.roll(lines, POSITIONS - start, 1)
            out[h, row * WINDOW : (row + 1) * WINDOW, :] = jnp.where(wide < POSITIONS, left, right)


def window_kernel(straddle, *refs):
    meta, scale, low, high, *refs = refs
    if straddle:
        low_right, high_right, _, *refs = refs
    bias, qkv, lift, up, down, attention_gain, forward_gain, *refs = refs
    outs, token, refs = refs[:4], refs[4], refs[5:]
    queries, keys, low_keys, values, mixed_heads, work = refs
    features = qkv.shape[0]
    heads = bias.shape[0]
    size = features // heads
    dates = outs[0].shape[0]
    token_total = dates * POSITIONS
    half = WINDOW // 2
    inner_part = half * WINDOW
    z = meta[0]
    token[...] = jnp.zeros(token.shape, F32)
    if straddle:
        for side, (left, right) in enumerate(((low, low_right), (high, high_right))):
            for d in range(dates):
                left_rows = left[d, inner_part:, :].astype(F32)
                right_rows = right[d].astype(F32)
                for i in range(half):
                    base = d * POSITIONS + (side * half + i) * WINDOW
                    part = slice(i * SHIFT, (i + 1) * SHIFT)
                    work[base : base + SHIFT, :] = left_rows[part, :]
                    work[base + SHIFT : base + WINDOW, :] = right_rows[part, :]
        tokens = work[...].astype(BF16)
    else:
        tokens = jnp.concatenate([low[:, :inner_part], high[:, :inner_part]], axis=1)
        tokens = tokens.reshape(token_total, features)

    project(tokens, qkv, queries, keys, values)

    wide_keys = keys[...].astype(F32)
    column = lax.broadcasted_iota(jnp.int32, (wide_keys.shape[1], 128), 0) - features % 128
    owner = lax.broadcasted_iota(jnp.int32, (wide_keys.shape[1], 128), 1)
    member = jnp.where((column >= owner * size) & (column < (owner + 1) * size), 1.0, 0.0)
    member = member.astype(BF16)

    def halves(x):
        top = x.astype(BF16)
        return top, (x - top.astype(F32)).astype(BF16)

    squares, rest = halves(wide_keys * wide_keys)
    norms = dot(squares, member) + dot(rest, member)
    shrink, rest = halves(lax.rsqrt(jnp.maximum(norms, 1.0)))
    shrink = dot_last(shrink, member) + dot_last(rest, member)
    keys[...], low_keys[...] = halves(wide_keys * shrink)

    lane = lax.broadcasted_iota(jnp.int32, (POSITIONS, PAIR), 1)
    line = lax.broadcasted_iota(jnp.int32, (POSITIONS, PAIR), 0)
    first_window = lane < POSITIONS
    apart = (((lane ^ line) & 32) != 0) & (meta[1] != 0)
    if straddle:
        apart = apart | ((((lane ^ line) & 4) != 0) & (meta[2] != 0))
    closed = jnp.where(apart, MASKED, 0.0)
    keep_first = jnp.where(first_window, 1.0, 0.0).astype(BF16)
    keep_second = jnp.where(first_window, 0.0, 1.0).astype(BF16)
    blocks = head_blocks(heads, size, features)

    def early(unit):
        b, p = unit
        span = slice(p * PAIR, (p + 1) * PAIR)
        columns = slice(b * 128, (b + 1) * 128)
        left = jnp.concatenate([keys[span, columns], low_keys[span, columns]], axis=1)
        right = spread_queries(queries, blocks[b], size, span)
        return dot(left, jnp.concatenate([right, right], axis=0))

    def late(unit, both):
        b, p = unit
        span = slice(p * PAIR, (p + 1) * PAIR)
        held = []
        for i, (h, _) in enumerate(blocks[b]):
            query = queries[h * size : (h + 1) * size, span].astype(F32)
            factor = scale[h] * lax.rsqrt(
                jnp.maximum(jnp.sum(query * query, axis=0, keepdims=True), 1.0)
            )
            mine = both[:, i * PAIR : (i + 1) * PAIR]
            scores = jnp.where(first_window, mine[:POSITIONS], mine[POSITIONS:])
            scores = scores * factor + (bias[h] + closed)
            weight = jnp.exp(scores - jnp.max(scores, axis=0, keepdims=True))
            total = jnp.sum(weight, axis=0, keepdims=True)
            narrow = weight.astype(BF16)
            spread = jnp.concatenate([narrow * keep_first, narrow * keep_second], axis=0)
            held.append((h, spread, 1.0 / total))
        for h, spread, inverse in held:
            result = dot(values[h * size : (h + 1) * size, span], spread) * inverse
            mixed_heads[h * size : (h + 1) * size, span] = result.astype(BF16)

    units = [(b, p) for b in range(len(blocks)) for p in range(token_total // PAIR)]
    staggered(units, early, late)

    projected = dot_first(mixed_heads[...], lift[...])
    gain = attention_gain[...].reshape(1, features)
    resid = (tokens.astype(F32) + layer_norm(projected, gain)).astype(BF16)

    lowered = jnp.zeros((token_total, features), F32)
    for first, last in column_blocks(up.shape[1], 512):
        hidden = gelu(dot(resid, up[:, first:last])).astype(BF16)
        lowered = lowered + dot_last(hidden, down[:, first:last])
    mixed = resid.astype(F32) + layer_norm(lowered, forward_gain[...].reshape(1, features))

    part = POSITIONS // 4
    if straddle:
        work[...] = mixed
    else:
        narrow = mixed.astype(BF16).reshape(dates, 4, part, features)
    for q in range(4):
        if straddle:
            quarter = []
            for d in range(dates):
                lines = []
                for i in range(half):
                    base = d * POSITIONS + ((q // 2) * half + i) * WINDOW + (q % 2) * SHIFT
                    lines.append(work[base : base + SHIFT, :])
                quarter.append(jnp.concatenate(lines, axis=0).astype(BF16)[None])
            quarter = jnp.concatenate(quarter, axis=0)
        else:
            quarter = narrow[:, q]
        for k in range(4):

            @pl.when((z + k) % 4 == q)
            def _(quarter=quarter, k=k):
                outs[k][...] = quarter


def time_kernel(size, meta, rank, *refs):
    pieces, refs = refs[:4], refs[4:]
    _, embedding, time_gain, qkv, lift, *refs = refs
    outs, token, refs = refs[:4], refs[4], refs[5:]
    queries, keys, values, mixed_heads = refs
    features = qkv.shape[0]
    heads = features // size
    z = meta[0]
    own, pixel_count, _ = pieces[0].shape
    dates = 4 * own
    group = 128 // dates
    groups = pixel_count // group
    token[...] = jnp.zeros(token.shape, F32)

    gain = time_gain[...].reshape(1, 1, features)
    wide = []
    normed = []
    for k in range(4):
        block = pieces[k][...].astype(F32)
        source = (z + 4 - k) % 4
        lines = layer_norm(block, gain)
        for i in range(own):
            line = embedding[pl.ds(rank[source * own + i], 1), :]
            normed.append((lines[i] + line)[None])
        wide.append(block)
    normed = jnp.concatenate(normed, axis=0)
    tokens = jnp.concatenate(
        [
            normed[:, g * group : (g + 1) * group, :].reshape(128, features).astype(BF16)
            for g in range(groups)
        ],
        axis=0,
    )
    project(tokens, qkv, queries, keys, values)

    lane = lax.broadcasted_iota(jnp.int32, (group, 128), 1)
    line = lax.broadcasted_iota(jnp.int32, (group, 128), 0)
    same = jnp.where((lane & (group - 1)) == line, 1.0, 0.0)
    shrink = size ** (-0.5)
    blocks = head_blocks(heads, size, features)

    def early(unit):
        b, g = unit
        span = slice(g * 128, (g + 1) * 128)
        right = spread_queries(queries, blocks[b], size, span)
        return dot(keys[span, b * 128 : (b + 1) * 128], right)

    def late(unit, both):
        b, g = unit
        span = slice(g * 128, (g + 1) * 128)
        held = []
        for i, (h, _) in enumerate(blocks[b]):
            scores = both[:, i * 128 : (i + 1) * 128].reshape(dates, group, 128)
            weight = jnp.exp((scores - jnp.max(scores, axis=0, keepdims=True)) * shrink)
            inverse = same / jnp.sum(weight, axis=0)
            held.append((h, (weight * inverse[None]).reshape(128, 128).astype(BF16)))
        for h, probs in held:
            result = dot(values[h * size : (h + 1) * size, span], probs)
            mixed_heads[h * size : (h + 1) * size, span] = result.astype(BF16)

    units = [(b, g) for b in range(len(blocks)) for g in range(groups)]
    staggered(units, early, late)

    lifted = dot_first(mixed_heads[...], lift[...])
    for k in range(4):
        parts = [
            lifted[g * 128 : (g + 1) * 128].reshape(dates, group, features)[k * own : (k + 1) * own]
            for g in range(groups)
        ]
        outs[k][...] = (wide[k] + jnp.concatenate(parts, axis=1)).astype(BF16)


def assemble(meta, *refs):
    inner, straddle, (out, work) = refs[:4], refs[4:8], refs[8:]
    dates, rows, cols, features = out.shape
    half = rows // 2
    z = meta[0]
    for k in range(4):
        q = (z + k) % 4
        block = inner[k][...].astype(F32)
        top = (2 * q + half) % rows
        for d in range(dates):
            for j in range(2):
                work[d, top + j, SHIFT : SHIFT + WINDOW, :] = block[d, j * WINDOW : (j + 1) * WINDOW]
    for parity in range(2):

        @pl.when(z % 2 == parity)
        def _(parity=parity):
            for k in range(4):
                q = (z + k) % 4
                block = straddle[k][...].astype(F32)
                top = jnp.where(q < 2, half, 0)
                left = cols - SHIFT if (parity + k) % 2 == 0 else 0
                for d in range(dates):
                    for i in range(half):
                        work[d, top + i, left : left + SHIFT, :] = block[
                            d, i * SHIFT : (i + 1) * SHIFT
                        ]

    out[...] = work[...].astype(BF16)


def call(kernel, out_shape, in_specs, scratch, flops, moved, name, room=8):
    return pl.pallas_call(
        kernel,
        out_shape=out_shape,
        in_specs=in_specs,
        out_specs=jax.tree.map(lambda _: VMEM, out_shape),
        scratch_shapes=scratch,
        compiler_params=pltpu.CompilerParams(vmem_limit_bytes=room * MIB),
        cost_estimate=pl.CostEstimate(flops=flops, bytes_accessed=moved, transcendentals=0),
        name=name,
    )


def local(
    routes,
    pixels,
    window_query_key_value_weight,
    head_logit_scale,
    bias_network_first,
    bias_network_second,
    window_output_weight,
    attention_norm_gain,
    feedforward_up_weight,
    feedforward_down_weight,
    feedforward_norm_gain,
    temporal_norm_gain,
    date_rank_embedding,
    acquisition_rank,
    temporal_query_key_value_weight,
    temporal_output_weight,
):
    dates, rows, cols, features = pixels.shape
    heads = head_logit_scale.shape[0]
    hidden = feedforward_up_weight.shape[1]
    plane = ("row", "col")
    space = ("date", "row", "col")
    token_total = dates * POSITIONS
    part = POSITIONS // 4
    date_axis = lax.axis_size("date")
    z = lax.axis_index("date")
    last_row, last_col = routes["last"](lax.axis_index("row"), lax.axis_index("col"))
    meta = jnp.stack([z, last_row, last_col]).astype(jnp.int32)

    piece_shape = jax.ShapeDtypeStruct((dates, POSITIONS // 2 + part, features), BF16)
    part_shape = jax.ShapeDtypeStruct((dates, part, features), BF16)
    token_shape = jax.ShapeDtypeStruct((8, 128), F32)
    key_columns = -(-(features % 128 + features) // 128) * 128
    tile_bytes = pixels.size * 2

    packed = call(
        pack,
        [piece_shape] * 2 + [part_shape] * 2,
        [VMEM],
        [pltpu.VMEM(pixels.shape[1:], F32)],
        10**10,
        tile_bytes * 2,
        "pack",
    )(pixels)
    low, high, low_right, high_right = (
        lax.ppermute(piece, plane, routes[name])
        for piece, name in zip(packed, ("low", "high", "low_right", "high_right"))
    )
    bias = call(
        bias_kernel,
        jax.ShapeDtypeStruct((heads, POSITIONS, PAIR), F32),
        [VMEM, VMEM],
        [pltpu.VMEM((WINDOW * 32, 128), F32)],
        10**9,
        10**6,
        "position_bias",
    )(bias_network_first, bias_network_second.T)

    projected = [
        pltpu.VMEM((features, token_total), BF16),
        pltpu.VMEM((token_total, key_columns), BF16),
        pltpu.VMEM((token_total, key_columns), BF16),
        pltpu.VMEM((features, token_total), BF16),
        pltpu.VMEM((features, token_total), BF16),
    ]

    def window_layer(straddle, inputs):
        return call(
            functools.partial(window_kernel, straddle),
            [part_shape] * 4 + [token_shape],
            [SMEM, SMEM]
            + [VMEM] * 2
            + ([VMEM] * 2 + [ANY] if straddle else [])
            + [VMEM] * 7,
            projected + [pltpu.VMEM((token_total, features), F32)],
            2 * token_total * features * (4 * features + 2 * hidden),
            12 * 10**6,
            "window_straddle" if straddle else "window_inner",
            24,
        )(
            meta,
            head_logit_scale,
            *inputs,
            bias,
            window_query_key_value_weight,
            window_output_weight,
            feedforward_up_weight,
            feedforward_down_weight.T,
            attention_norm_gain,
            feedforward_norm_gain,
        )

    def time_layer(pieces, token):
        return call(
            functools.partial(time_kernel, features // heads),
            [part_shape] * 4 + [token_shape],
            [SMEM, SMEM] + [VMEM] * 4 + [ANY] + [VMEM] * 4,
            projected[:2] + projected[3:],
            2 * token_total * features * 4 * features,
            5 * 10**6,
            "time_layer",
            14,
        )(
            meta,
            acquisition_rank,
            *pieces,
            token,
            date_rank_embedding,
            temporal_norm_gain,
            temporal_query_key_value_weight,
            temporal_output_weight,
        )

    def to_dates(pieces, kind):
        return [lax.ppermute(piece, space, routes[kind][k]) for k, piece in enumerate(pieces)]

    def to_home(pieces):
        return [
            piece
            if k == 0
            else lax.ppermute(piece, "date", [(i, (i - k) % date_axis) for i in range(date_axis)])
            for k, piece in enumerate(pieces)
        ]

    *inner, token = window_layer(False, [low, high])
    inner = to_dates(inner, "inner")
    *straddle, token = window_layer(True, [low, high, low_right, high_right, token])
    straddle = to_dates(straddle, "straddle")
    *inner, token = time_layer(inner, token)
    inner = to_home(inner)
    *straddle, token = time_layer(straddle, token)
    straddle = to_home(straddle)
    return call(
        assemble,
        jax.ShapeDtypeStruct(pixels.shape, BF16),
        [SMEM] + [VMEM] * 8,
        [pltpu.VMEM(pixels.shape, F32)],
        0,
        tile_bytes * 2,
        "assemble",
    )(meta, *inner, *straddle)


def plan(mesh):
    dates, rows, cols = (mesh.shape[name] for name in ("date", "row", "col"))
    high, low, core = 2, cols // 2, 2
    reach = high * low

    def place(r, c):
        x, y = r // high, (r % high) * low + c // core
        y = (y + 1) % reach
        return x * high + y // low, (y % low) * core + c % core

    def flat(r, c):
        return (r % rows) * cols + c % cols

    def spot(z, r, c):
        return (z % dates) * rows * cols + flat(r, c)

    tiles = [(r, c) for r in range(rows) for c in range(cols)]

    def route(down, right):
        return [(flat(r + down, c + right), flat(*place(r, c))) for r, c in tiles]

    def forward(kind, k):
        pairs = []
        for z in range(dates):
            q = (z + k) % dates
            right = q % 2 if kind == "straddle" else 0
            for r, c in tiles:
                pairs.append((spot(z, *place(r, c)), spot(q, r + q // 2, c + right)))
        return pairs

    def last(row, col):
        y = (row % high) * low + col // core
        y = (y + reach - 1) % reach
        r = (row // high) * high + y // low
        c = (y % low) * core + col % core
        return (r == rows - 1).astype(jnp.int32), (c == cols - 1).astype(jnp.int32)

    return {
        "low": route(0, 0),
        "high": route(1, 0),
        "low_right": route(0, 1),
        "high_right": route(1, 1),
        "inner": [forward("inner", k) for k in range(dates)],
        "straddle": [forward("straddle", k) for k in range(dates)],
        "last": last,
    }


def solution(mesh):
    placed = (P("date", "row", "col", None),) + (P(),) * 14
    return jax.shard_map(
        functools.partial(local, plan(mesh)),
        mesh=mesh,
        in_specs=placed,
        out_specs=P("date", "row", "col", None),
        check_vma=False,
    )
```

profile of v0, /device:TPU:0, one launch (start us, length us, event | category | flops | bytes accessed | tf_op | source)
XLA Modules:
  0.0 81.4 jit_solution(11107592926592945341)
XLA Ops:
  0.0 1.1 %copy-done.13 = bf16[4,8,16,704]{3,2,1,0:T(8,128)(2,1)S(1)} copy-done((bf16[4,8,16,704]{3,2,1,0:T(8,128)(2,1)S(1)}, bf16[4,8,16,704]{3,2,1,0:T(8,128)(2,1)}, u32[]{:S(2)}) %copy-start.13) | copy-done | bytes 720920
  1.1 1.1 %pack.1 = (bf16[4,48,704]{2,1,0:T(8,128)(2,1)}, bf16[4,48,704]{2,1,0:T(8,128)(2,1)}, bf16[4,16,704]{2,1,0:T(8,128)(2,1)}, bf16[4,16,704]{2,1,0:T(8,128)(2,1)}) custom-call(bf16[4,8,16,704]{3,2,1,0:T(8,128)(2,1)S(1)} %copy-done.13), custom_call_target="tpu_custom_call" | custom-call | flops 10000000000 | bytes 1441792 | tf_op jit(solution)/shard_map/pack/pallas_call | solution.py:422
  2.2 1.7 %collective-permute-start = (bf16[4,48,704]{2,1,0:T(8,128)(2,1)}, bf16[4,48,704]{2,1,0:T(8,128)(2,1)S(1)}, u32[]{:S(2)}, u32[]{:S(2)}) collective-permute-start(bf16[4,48,704]{2,1,0:T(8,128)(2,1)} %get-tuple-element.28), channel_id=1, source_target_pairs={{0,2},{1,3},{2,4},{3,5},{4,6},{5,7},{6,0},{7,1},{8,10},{9,11},{10,... | collective-permute-start | bytes 811016 | tf_op jit(solution)/shard_map/ppermute | solution.py:432
  3.9 3.9 %collective-permute-start.1 = (bf16[4,48,704]{2,1,0:T(8,128)(2,1)}, bf16[4,48,704]{2,1,0:T(8,128)(2,1)}, u32[]{:S(2)}, u32[]{:S(2)}) collective-permute-start(bf16[4,48,704]{2,1,0:T(8,128)(2,1)} %get-tuple-element.29), channel_id=1, source_target_pairs={{4,2},{5,3},{6,4},{7,5},{8,6},{9,7},{10,0},{11,1},{12,10},{13,11},... | collective-permute-start | bytes 811016 | tf_op jit(solution)/shard_map/ppermute | solution.py:432
  7.7 0.0 collective-permute-start.6
  7.7 0.9 %collective-permute-start.7 = (bf16[4,16,704]{2,1,0:T(8,128)(2,1)}, bf16[4,16,704]{2,1,0:T(8,128)(2,1)S(1)}, u32[]{:S(2)}, u32[]{:S(2)}) collective-permute-start(bf16[4,16,704]{2,1,0:T(8,128)(2,1)} %get-tuple-element.35), channel_id=1, source_target_pairs={{5,2},{6,3},{7,4},{4,5},{9,6},{10,7},{11,0},{8,1},{13,10},{14,11},... | collective-permute-start | bytes 270344 | tf_op jit(solution)/shard_map/ppermute | solution.py:432
  8.7 0.8 %copy-done.14 = f32[512,22]{0,1:T(8,128)S(1)} copy-done((f32[512,22]{0,1:T(8,128)S(1)}, f32[512,22]{0,1:T(8,128)}, u32[]{:S(2)}) %copy-start.14) | copy-done | bytes 45080
  9.5 0.7 copy-done.15
  10.2 1.8 %position_bias.1.refs_4_.refs_7_ = f32[22,64,128]{2,1,0:T(8,128)S(1)} custom-call(f32[2,512]{1,0:T(2,128)S(1)} %copy-done.15, f32[22,512]{1,0:T(8,128)S(1)} %bitcast.7), custom_call_target="tpu_custom_call" | custom-call | flops 1000000000 | bytes 1000000 | tf_op jit(solution)/shard_map/position_bias/pallas_call | solution.py:435
  12.0 0.1 pad_add_fusion.refs_0_.meta
  12.1 0.7 collective-permute-done.refs_2_
  12.9 2.3 %collective-permute-done.1.refs_3_ = bf16[4,48,704]{2,1,0:T(8,128)(2,1)} collective-permute-done((bf16[4,48,704]{2,1,0:T(8,128)(2,1)}, bf16[4,48,704]{2,1,0:T(8,128)(2,1)}, u32[]{:S(2)}, u32[]{:S(2)}) %collective-permute-start.1) | collective-permute-done | bytes 270368 | tf_op jit(solution)/shard_map/ppermute | solution.py:432
  15.2 0.0 copy-done.2
  15.2 0.0 copy-done.8
  15.2 0.0 copy-done.9
  15.2 0.0 copy-done.11
  15.2 0.0 copy-start
  15.2 2.1 %copy-done = bf16[704,2816]{1,0:T(8,128)(2,1)S(1)} copy-done((bf16[704,2816]{1,0:T(8,128)(2,1)S(1)}, bf16[704,2816]{1,0:T(8,128)(2,1)}, u32[]{:S(2)}) %copy-start) | copy-done | bytes 3964952
  17.3 2.1 %copy-done.1 = bf16[2816,704]{0,1:T(8,128)(2,1)S(1)} copy-done((bf16[2816,704]{0,1:T(8,128)(2,1)S(1)}, bf16[2816,704]{0,1:T(8,128)(2,1)}, u32[]{:S(2)}) %copy-start.1) | copy-done | bytes 3964952
  19.5 1.2 %copy-done.4 = bf16[704,704]{1,0:T(8,128)(2,1)S(1)} copy-done((bf16[704,704]{1,0:T(8,128)(2,1)S(1)}, bf16[704,704]{1,0:T(8,128)(2,1)}, u32[]{:S(2)}) %copy-start.4) | copy-done | bytes 991256
  20.7 8.5 %window_inner.1 = (bf16[4,16,704]{2,1,0:T(8,128)(2,1)S(1)}, bf16[4,16,704]{2,1,0:T(8,128)(2,1)S(1)}, bf16[4,16,704]{2,1,0:T(8,128)(2,1)S(1)}, bf16[4,16,704]{2,1,0:T(8,128)(2,1)S(1)}, f32[8,128]{1,0:T(8,128)S(1)}) custom-call(s32[3]{0:T(128)S(1)} %pad_add_fusion.refs_0_.meta, f32[22]{0:T(128)S(1)} %copy-done.11, ...), custom_call_target="tpu_custom_call" | custom-call | flops 3045064704 | bytes 12000000 | tf_op jit(solution)/shard_map/window_inner/pallas_call | solution.py:454
  29.2 2.8 %collective-permute-start.2 = (bf16[4,16,704]{2,1,0:T(8,128)(2,1)S(1)}, bf16[4,16,704]{2,1,0:T(8,128)(2,1)S(1)}, u32[]{:S(2)}, u32[]{:S(2)}) collective-permute-start(bf16[4,16,704]{2,1,0:T(8,128)(2,1)S(1)} %get-tuple-element.30), channel_id=1, source_target_pairs={{2,0},{3,1},{4,2},{5,3},{6,4},{7,5},{0,6},{1,7},{10,8},{11,9},{12,... | collective-permute-start | bytes 270344 | tf_op jit(solution)/shard_map/ppermute | solution.py:501
  32.0 1.4 %collective-permute-start.3 = (bf16[4,16,704]{2,1,0:T(8,128)(2,1)S(1)}, bf16[4,16,704]{2,1,0:T(8,128)(2,1)S(1)}, u32[]{:S(2)}, u32[]{:S(2)}) collective-permute-start(bf16[4,16,704]{2,1,0:T(8,128)(2,1)S(1)} %get-tuple-element.31), channel_id=1, source_target_pairs={{2,32},{3,33},{4,34},{5,35},{6,36},{7,37},{0,38},{1,39},{10,40},{1... | collective-permute-start | bytes 270344 | tf_op jit(solution)/shard_map/ppermute | solution.py:501
  33.4 5.3 %collective-permute-start.4 = (bf16[4,16,704]{2,1,0:T(8,128)(2,1)S(1)}, bf16[4,16,704]{2,1,0:T(8,128)(2,1)S(1)}, u32[]{:S(2)}, u32[]{:S(2)}) collective-permute-start(bf16[4,16,704]{2,1,0:T(8,128)(2,1)S(1)} %get-tuple-element.32), channel_id=1, source_target_pairs={{2,68},{3,69},{4,70},{5,71},{6,72},{7,73},{0,74},{1,75},{10,76},{1... | collective-permute-start | bytes 270344 | tf_op jit(solution)/shard_map/ppermute | solution.py:501
  38.7 0.0 collective-permute-done.6.refs_4_
  38.7 0.7 collective-permute-start.5
  39.4 0.0 collective-permute-done.7.refs_5_
  39.4 0.0 copy-done.5
  39.4 0.0 copy-start.7
  39.4 0.0 copy-start.10
  39.4 0.0 copy-start.12
  39.4 8.6 %window_straddle.1 = (bf16[4,16,704]{2,1,0:T(8,128)(2,1)S(1)}, bf16[4,16,704]{2,1,0:T(8,128)(2,1)S(1)}, bf16[4,16,704]{2,1,0:T(8,128)(2,1)S(1)}, bf16[4,16,704]{2,1,0:T(8,128)(2,1)S(1)}, f32[8,128]{1,0:T(8,128)S(1)}) custom-call(s32[3]{0:T(128)S(1)} %pad_add_fusion.refs_0_.meta, f32[22]{0:T(128)S(1)} %copy-done.11, ...), custom_call_target="tpu_custom_call" | custom-call | flops 3045064704 | bytes 12000000 | tf_op jit(solution)/shard_map/window_straddle/pallas_call | solution.py:454
  48.1 3.9 %collective-permute-start.11 = (bf16[4,16,704]{2,1,0:T(8,128)(2,1)S(1)}, bf16[4,16,704]{2,1,0:T(8,128)(2,1)S(1)}, u32[]{:S(2)}, u32[]{:S(2)}) collective-permute-start(bf16[4,16,704]{2,1,0:T(8,128)(2,1)S(1)} %get-tuple-element.42), channel_id=1, source_target_pairs={{2,0},{3,1},{4,2},{5,3},{6,4},{7,5},{0,6},{1,7},{10,8},{11,9},{12,... | collective-permute-start | bytes 270344 | tf_op jit(solution)/shard_map/ppermute | solution.py:501
  51.9 0.0 collective-permute-done.2.refs_0_
  51.9 0.0 collective-permute-start.12
  52.0 0.0 collective-permute-done.3.refs_1_
  52.0 0.1 collective-permute-start.13
  52.0 0.0 collective-permute-done.4.refs_2_
  52.0 1.9 %collective-permute-start.14 = (bf16[4,16,704]{2,1,0:T(8,128)(2,1)S(1)}, bf16[4,16,704]{2,1,0:T(8,128)(2,1)S(1)}, u32[]{:S(2)}, u32[]{:S(2)}) collective-permute-start(bf16[4,16,704]{2,1,0:T(8,128)(2,1)S(1)} %get-tuple-element.45), channel_id=1, source_target_pairs={{2,101},{3,102},{4,103},{5,100},{6,105},{7,106},{0,107},{1,104},{1... | collective-permute-start | bytes 270344 | tf_op jit(solution)/shard_map/ppermute | solution.py:501
  53.9 0.0 collective-permute-done.5.refs_3_
  53.9 0.0 copy-done.3
  53.9 0.0 copy-done.6
  53.9 0.0 copy-done.7
  53.9 0.0 copy-done.10
  53.9 0.0 copy-done.12
  54.0 3.8 %time_layer.2 = (bf16[4,16,704]{2,1,0:T(8,128)(2,1)S(1)}, bf16[4,16,704]{2,1,0:T(8,128)(2,1)S(1)}, bf16[4,16,704]{2,1,0:T(8,128)(2,1)S(1)}, bf16[4,16,704]{2,1,0:T(8,128)(2,1)S(1)}, f32[8,128]{1,0:T(8,128)S(1)}) custom-call(s32[3]{0:T(128)S(1)} %pad_add_fusion.refs_0_.meta, s32[16]{0:T(128)S(1)} %copy-done.12, ...), custom_call_target="tpu_custom_call" | custom-call | flops 1015021568 | bytes 5000000 | tf_op jit(solution)/shard_map/time_layer/pallas_call | solution.py:480
  57.8 3.8 %collective-permute-start.8 = (bf16[4,16,704]{2,1,0:T(8,128)(2,1)S(1)}, bf16[4,16,704]{2,1,0:T(8,128)(2,1)S(1)}, u32[]{:S(2)}, u32[]{:S(2)}) collective-permute-start(bf16[4,16,704]{2,1,0:T(8,128)(2,1)S(1)} %get-tuple-element.39), channel_id=1, source_target_pairs={{0,96},{32,0},{64,32},{96,64},{1,97},{33,1},{65,33},{97,65},{2,98}... | collective-permute-start | bytes 270344 | tf_op jit(solution)/shard_map/ppermute | solution.py:507
  61.6 0.0 collective-permute-done.11.refs_0_
  61.6 3.9 %collective-permute-start.9 = (bf16[4,16,704]{2,1,0:T(8,128)(2,1)S(1)}, bf16[4,16,704]{2,1,0:T(8,128)(2,1)S(1)}, u32[]{:S(2)}, u32[]{:S(2)}) collective-permute-start(bf16[4,16,704]{2,1,0:T(8,128)(2,1)S(1)} %get-tuple-element.40), channel_id=1, source_target_pairs={{0,64},{32,96},{64,0},{96,32},{1,65},{33,97},{65,1},{97,33},{2,66}... | collective-permute-start | bytes 270344 | tf_op jit(solution)/shard_map/ppermute | solution.py:507
  65.5 0.0 collective-permute-done.12.refs_1_
  65.5 1.3 %collective-permute-start.10 = (bf16[4,16,704]{2,1,0:T(8,128)(2,1)S(1)}, bf16[4,16,704]{2,1,0:T(8,128)(2,1)S(1)}, u32[]{:S(2)}, u32[]{:S(2)}) collective-permute-start(bf16[4,16,704]{2,1,0:T(8,128)(2,1)S(1)} %get-tuple-element.41), channel_id=1, source_target_pairs={{0,32},{32,64},{64,96},{96,0},{1,33},{33,65},{65,97},{97,1},{2,34}... | collective-permute-start | bytes 270344 | tf_op jit(solution)/shard_map/ppermute | solution.py:507
  66.8 0.0 collective-permute-done.13.refs_2_
  66.8 0.0 collective-permute-done.14.refs_3_
  66.8 3.8 %time_layer.3 = (bf16[4,16,704]{2,1,0:T(8,128)(2,1)S(1)}, bf16[4,16,704]{2,1,0:T(8,128)(2,1)S(1)}, bf16[4,16,704]{2,1,0:T(8,128)(2,1)S(1)}, bf16[4,16,704]{2,1,0:T(8,128)(2,1)S(1)}, f32[8,128]{1,0:T(8,128)}) custom-call(s32[3]{0:T(128)S(1)} %pad_add_fusion.refs_0_.meta, s32[16]{0:T(128)S(1)} %copy-done.12, ...), custom_call_target="tpu_custom_call" | custom-call | flops 1015021568 | bytes 5000000 | tf_op jit(solution)/shard_map/time_layer/pallas_call | solution.py:480
  70.7 2.0 %collective-permute-start.15 = (bf16[4,16,704]{2,1,0:T(8,128)(2,1)S(1)}, bf16[4,16,704]{2,1,0:T(8,128)(2,1)S(1)}, u32[]{:S(2)}, u32[]{:S(2)}) collective-permute-start(bf16[4,16,704]{2,1,0:T(8,128)(2,1)S(1)} %get-tuple-element.48), channel_id=1, source_target_pairs={{0,96},{32,0},{64,32},{96,64},{1,97},{33,1},{65,33},{97,65},{2,98}... | collective-permute-start | bytes 270344 | tf_op jit(solution)/shard_map/ppermute | solution.py:507
  72.6 0.2 collective-permute-start.16
  72.8 0.0 collective-permute-done.8.refs_1_
  72.8 0.8 collective-permute-start.17
  73.6 0.0 collective-permute-done.9.refs_2_
  73.6 0.0 collective-permute-done.10.refs_3_
  73.6 2.3 %collective-permute-done.15.refs_5_ = bf16[4,16,704]{2,1,0:T(8,128)(2,1)S(1)} collective-permute-done((bf16[4,16,704]{2,1,0:T(8,128)(2,1)S(1)}, bf16[4,16,704]{2,1,0:T(8,128)(2,1)S(1)}, u32[]{:S(2)}, u32[]{:S(2)}) %collective-permute-start.15) | collective-permute-done | bytes 90144 | tf_op jit(solution)/shard_map/ppermute | solution.py:507
  75.9 3.0 %collective-permute-done.16.refs_6_ = bf16[4,16,704]{2,1,0:T(8,128)(2,1)S(1)} collective-permute-done((bf16[4,16,704]{2,1,0:T(8,128)(2,1)S(1)}, bf16[4,16,704]{2,1,0:T(8,128)(2,1)S(1)}, u32[]{:S(2)}, u32[]{:S(2)}) %collective-permute-start.16) | collective-permute-done | bytes 90144 | tf_op jit(solution)/shard_map/ppermute | solution.py:507
  78.9 0.8 %collective-permute-done.17.refs_7_ = bf16[4,16,704]{2,1,0:T(8,128)(2,1)S(1)} collective-permute-done((bf16[4,16,704]{2,1,0:T(8,128)(2,1)S(1)}, bf16[4,16,704]{2,1,0:T(8,128)(2,1)S(1)}, u32[]{:S(2)}, u32[]{:S(2)}) %collective-permute-start.17) | collective-permute-done | bytes 90144 | tf_op jit(solution)/shard_map/ppermute | solution.py:507
  79.7 1.7 %assemble.1 = bf16[4,8,16,704]{3,2,1,0:T(8,128)(2,1)} custom-call(s32[3]{0:T(128)S(1)} %pad_add_fusion.refs_0_.meta, bf16[4,16,704]{2,1,0:T(8,128)(2,1)S(1)} %get-tuple-element.38.refs_0_, bf16[4,16,704]{2,1,0:T(8,128)(2,1)S(1)} %collective-permute-done.8.refs_1_, bf16[4,16,704]{2,1,0:T(8,128)(2,1)S(1)} %collective-permute-done.9.refs_2_, ...), custom_call_target="tpu_custom_call" | custom-call | bytes 1441792 | tf_op jit(solution)/shard_map/assemble/pallas_call | solution.py:519
  (12 shorter events, 0.0 us)
Async XLA Ops:
  0.0 1.1 %copy-start.13 = (bf16[4,8,16,704]{3,2,1,0:T(8,128)(2,1)S(1)}, bf16[4,8,16,704]{3,2,1,0:T(8,128)(2,1)}, u32[]{:S(2)}) copy-start(bf16[4,8,16,704]{3,2,1,0:T(8,128)(2,1)} %pixels.1) | copy-start | bytes 2162692
  2.2 13.0 %copy-start.2 = (bf16[704,2112]{1,0:T(8,128)(2,1)S(1)}, bf16[704,2112]{1,0:T(8,128)(2,1)}, u32[]{:S(2)}) copy-start(bf16[704,2112]{1,0:T(8,128)(2,1)} %refs_8_.3) | copy-start | bytes 8921092
  2.2 10.6 %collective-permute-start = (bf16[4,48,704]{2,1,0:T(8,128)(2,1)}, bf16[4,48,704]{2,1,0:T(8,128)(2,1)S(1)}, u32[]{:S(2)}, u32[]{:S(2)}) collective-permute-start(bf16[4,48,704]{2,1,0:T(8,128)(2,1)} %get-tuple-element.28), channel_id=1, source_target_pairs={{0,2},{1,3},{2,4},{3,5},{4,6},{5,7},{6,0},{7,1},{8,10},{9,11},{10,... | collective-permute-start | bytes 811016 | tf_op jit(solution)/shard_map/ppermute | solution.py:432
  3.9 11.3 %collective-permute-start.1 = (bf16[4,48,704]{2,1,0:T(8,128)(2,1)}, bf16[4,48,704]{2,1,0:T(8,128)(2,1)}, u32[]{:S(2)}, u32[]{:S(2)}) collective-permute-start(bf16[4,48,704]{2,1,0:T(8,128)(2,1)} %get-tuple-element.29), channel_id=1, source_target_pairs={{4,2},{5,3},{6,4},{7,5},{8,6},{9,7},{10,0},{11,1},{12,10},{13,11},... | collective-permute-start | bytes 811016 | tf_op jit(solution)/shard_map/ppermute | solution.py:432
  7.7 30.9 %collective-permute-start.6 = (bf16[4,16,704]{2,1,0:T(8,128)(2,1)}, bf16[4,16,704]{2,1,0:T(8,128)(2,1)S(1)}, u32[]{:S(2)}, u32[]{:S(2)}) collective-permute-start(bf16[4,16,704]{2,1,0:T(8,128)(2,1)} %get-tuple-element.34), channel_id=1, source_target_pairs={{1,2},{2,3},{3,4},{0,5},{5,6},{6,7},{7,0},{4,1},{9,10},{10,11},{11... | collective-permute-start | bytes 270344 | tf_op jit(solution)/shard_map/ppermute | solution.py:432
  7.7 31.6 %collective-permute-start.7 = (bf16[4,16,704]{2,1,0:T(8,128)(2,1)}, bf16[4,16,704]{2,1,0:T(8,128)(2,1)S(1)}, u32[]{:S(2)}, u32[]{:S(2)}) collective-permute-start(bf16[4,16,704]{2,1,0:T(8,128)(2,1)} %get-tuple-element.35), channel_id=1, source_target_pairs={{5,2},{6,3},{7,4},{4,5},{9,6},{10,7},{11,0},{8,1},{13,10},{14,11},... | collective-permute-start | bytes 270344 | tf_op jit(solution)/shard_map/ppermute | solution.py:432
  8.7 6.5 %copy-start.8 = (f32[704]{0:T(1024)S(1)}, f32[704]{0:T(1024)}, u32[]{:S(2)}) copy-start(f32[704]{0:T(1024)} %refs_12_.1) | copy-start | bytes 8452
  8.7 6.5 %copy-start.9 = (f32[704]{0:T(1024)S(1)}, f32[704]{0:T(1024)}, u32[]{:S(2)}) copy-start(f32[704]{0:T(1024)} %refs_13_.1) | copy-start | bytes 8452
  8.7 6.5 %copy-start.11 = (f32[22]{0:T(128)S(1)}, f32[22]{0:T(128)}, u32[]{:S(2)}) copy-start(f32[22]{0:T(128)} %refs_1_.3) | copy-start | bytes 268
  8.7 0.8 %copy-start.14 = (f32[512,22]{0,1:T(8,128)S(1)}, f32[512,22]{0,1:T(8,128)}, u32[]{:S(2)}) copy-start(f32[512,22]{0,1:T(8,128)} %param.19) | copy-start | bytes 135172
  9.5 0.7 copy-start.15
  15.2 2.1 %copy-start = (bf16[704,2816]{1,0:T(8,128)(2,1)S(1)}, bf16[704,2816]{1,0:T(8,128)(2,1)}, u32[]{:S(2)}) copy-start(bf16[704,2816]{1,0:T(8,128)(2,1)} %refs_10_.3) | copy-start | bytes 11894788
  17.3 2.1 %copy-start.1 = (bf16[2816,704]{0,1:T(8,128)(2,1)S(1)}, bf16[2816,704]{0,1:T(8,128)(2,1)}, u32[]{:S(2)}) copy-start(bf16[2816,704]{0,1:T(8,128)(2,1)} %param.23) | copy-start | bytes 11894788
  19.5 1.2 %copy-start.4 = (bf16[704,704]{1,0:T(8,128)(2,1)S(1)}, bf16[704,704]{1,0:T(8,128)(2,1)}, u32[]{:S(2)}) copy-start(bf16[704,704]{1,0:T(8,128)(2,1)} %refs_9_.3) | copy-start | bytes 2973700
  20.7 18.7 %copy-start.5 = (bf16[704,704]{1,0:T(8,128)(2,1)S(1)}, bf16[704,704]{1,0:T(8,128)(2,1)}, u32[]{:S(2)}) copy-start(bf16[704,704]{1,0:T(8,128)(2,1)} %refs_9_.3) | copy-start | bytes 2973700
  29.2 22.7 %collective-permute-start.2 = (bf16[4,16,704]{2,1,0:T(8,128)(2,1)S(1)}, bf16[4,16,704]{2,1,0:T(8,128)(2,1)S(1)}, u32[]{:S(2)}, u32[]{:S(2)}) collective-permute-start(bf16[4,16,704]{2,1,0:T(8,128)(2,1)S(1)} %get-tuple-element.30), channel_id=1, source_target_pairs={{2,0},{3,1},{4,2},{5,3},{6,4},{7,5},{0,6},{1,7},{10,8},{11,9},{12,... | collective-permute-start | bytes 270344 | tf_op jit(solution)/shard_map/ppermute | solution.py:501
  32.0 20.0 %collective-permute-start.3 = (bf16[4,16,704]{2,1,0:T(8,128)(2,1)S(1)}, bf16[4,16,704]{2,1,0:T(8,128)(2,1)S(1)}, u32[]{:S(2)}, u32[]{:S(2)}) collective-permute-start(bf16[4,16,704]{2,1,0:T(8,128)(2,1)S(1)} %get-tuple-element.31), channel_id=1, source_target_pairs={{2,32},{3,33},{4,34},{5,35},{6,36},{7,37},{0,38},{1,39},{10,40},{1... | collective-permute-start | bytes 270344 | tf_op jit(solution)/shard_map/ppermute | solution.py:501
  33.4 18.6 %collective-permute-start.4 = (bf16[4,16,704]{2,1,0:T(8,128)(2,1)S(1)}, bf16[4,16,704]{2,1,0:T(8,128)(2,1)S(1)}, u32[]{:S(2)}, u32[]{:S(2)}) collective-permute-start(bf16[4,16,704]{2,1,0:T(8,128)(2,1)S(1)} %get-tuple-element.32), channel_id=1, source_target_pairs={{2,68},{3,69},{4,70},{5,71},{6,72},{7,73},{0,74},{1,75},{10,76},{1... | collective-permute-start | bytes 270344 | tf_op jit(solution)/shard_map/ppermute | solution.py:501
  38.7 15.2 %collective-permute-start.5 = (bf16[4,16,704]{2,1,0:T(8,128)(2,1)S(1)}, bf16[4,16,704]{2,1,0:T(8,128)(2,1)S(1)}, u32[]{:S(2)}, u32[]{:S(2)}) collective-permute-start(bf16[4,16,704]{2,1,0:T(8,128)(2,1)S(1)} %get-tuple-element.33), channel_id=1, source_target_pairs={{2,100},{3,101},{4,102},{5,103},{6,104},{7,105},{0,106},{1,107},{1... | collective-permute-start | bytes 270344 | tf_op jit(solution)/shard_map/ppermute | solution.py:501
  39.4 14.5 %copy-start.3 = (bf16[704,2112]{1,0:T(8,128)(2,1)S(1)}, bf16[704,2112]{1,0:T(8,128)(2,1)}, u32[]{:S(2)}) copy-start(bf16[704,2112]{1,0:T(8,128)(2,1)} %refs_7_.5) | copy-start | bytes 8921092
  39.4 14.5 %copy-start.6 = (bf16[704,704]{1,0:T(8,128)(2,1)S(1)}, bf16[704,704]{1,0:T(8,128)(2,1)}, u32[]{:S(2)}) copy-start(bf16[704,704]{1,0:T(8,128)(2,1)} %refs_8_.5) | copy-start | bytes 2973700
  39.4 14.5 %copy-start.7 = (f32[16,704]{1,0:T(8,128)S(1)}, f32[16,704]{1,0:T(8,128)}, u32[]{:S(2)}) copy-start(f32[16,704]{1,0:T(8,128)} %refs_5_.5) | copy-start | bytes 135172
  39.4 14.5 %copy-start.10 = (f32[704]{0:T(1024)S(1)}, f32[704]{0:T(1024)}, u32[]{:S(2)}) copy-start(f32[704]{0:T(1024)} %refs_6_.5) | copy-start | bytes 8452
  39.4 14.5 %copy-start.12 = (s32[16]{0:T(128)S(1)}, s32[16]{0:T(128)}, u32[]{:S(2)}) copy-start(s32[16]{0:T(128)} %rank.3) | copy-start | bytes 196
  48.1 13.5 %collective-permute-start.11 = (bf16[4,16,704]{2,1,0:T(8,128)(2,1)S(1)}, bf16[4,16,704]{2,1,0:T(8,128)(2,1)S(1)}, u32[]{:S(2)}, u32[]{:S(2)}) collective-permute-start(bf16[4,16,704]{2,1,0:T(8,128)(2,1)S(1)} %get-tuple-element.42), channel_id=1, source_target_pairs={{2,0},{3,1},{4,2},{5,3},{6,4},{7,5},{0,6},{1,7},{10,8},{11,9},{12,... | collective-permute-start | bytes 270344 | tf_op jit(solution)/shard_map/ppermute | solution.py:501
  51.9 13.6 %collective-permute-start.12 = (bf16[4,16,704]{2,1,0:T(8,128)(2,1)S(1)}, bf16[4,16,704]{2,1,0:T(8,128)(2,1)S(1)}, u32[]{:S(2)}, u32[]{:S(2)}) collective-permute-start(bf16[4,16,704]{2,1,0:T(8,128)(2,1)S(1)} %get-tuple-element.43), channel_id=1, source_target_pairs={{2,33},{3,34},{4,35},{5,32},{6,37},{7,38},{0,39},{1,36},{10,41},{1... | collective-permute-start | bytes 270344 | tf_op jit(solution)/shard_map/ppermute | solution.py:501
  52.0 14.9 %collective-permute-start.13 = (bf16[4,16,704]{2,1,0:T(8,128)(2,1)S(1)}, bf16[4,16,704]{2,1,0:T(8,128)(2,1)S(1)}, u32[]{:S(2)}, u32[]{:S(2)}) collective-permute-start(bf16[4,16,704]{2,1,0:T(8,128)(2,1)S(1)} %get-tuple-element.44), channel_id=1, source_target_pairs={{2,68},{3,69},{4,70},{5,71},{6,72},{7,73},{0,74},{1,75},{10,76},{1... | collective-permute-start | bytes 270344 | tf_op jit(solution)/shard_map/ppermute | solution.py:501
  52.0 14.8 %collective-permute-start.14 = (bf16[4,16,704]{2,1,0:T(8,128)(2,1)S(1)}, bf16[4,16,704]{2,1,0:T(8,128)(2,1)S(1)}, u32[]{:S(2)}, u32[]{:S(2)}) collective-permute-start(bf16[4,16,704]{2,1,0:T(8,128)(2,1)S(1)} %get-tuple-element.45), channel_id=1, source_target_pairs={{2,101},{3,102},{4,103},{5,100},{6,105},{7,106},{0,107},{1,104},{1... | collective-permute-start | bytes 270344 | tf_op jit(solution)/shard_map/ppermute | solution.py:501
  57.8 15.0 %collective-permute-start.8 = (bf16[4,16,704]{2,1,0:T(8,128)(2,1)S(1)}, bf16[4,16,704]{2,1,0:T(8,128)(2,1)S(1)}, u32[]{:S(2)}, u32[]{:S(2)}) collective-permute-start(bf16[4,16,704]{2,1,0:T(8,128)(2,1)S(1)} %get-tuple-element.39), channel_id=1, source_target_pairs={{0,96},{32,0},{64,32},{96,64},{1,97},{33,1},{65,33},{97,65},{2,98}... | collective-permute-start | bytes 270344 | tf_op jit(solution)/shard_map/ppermute | solution.py:507
  61.6 12.0 %collective-permute-start.9 = (bf16[4,16,704]{2,1,0:T(8,128)(2,1)S(1)}, bf16[4,16,704]{2,1,0:T(8,128)(2,1)S(1)}, u32[]{:S(2)}, u32[]{:S(2)}) collective-permute-start(bf16[4,16,704]{2,1,0:T(8,128)(2,1)S(1)} %get-tuple-element.40), channel_id=1, source_target_pairs={{0,64},{32,96},{64,0},{96,32},{1,65},{33,97},{65,1},{97,33},{2,66}... | collective-permute-start | bytes 270344 | tf_op jit(solution)/shard_map/ppermute | solution.py:507
  65.5 8.1 %collective-permute-start.10 = (bf16[4,16,704]{2,1,0:T(8,128)(2,1)S(1)}, bf16[4,16,704]{2,1,0:T(8,128)(2,1)S(1)}, u32[]{:S(2)}, u32[]{:S(2)}) collective-permute-start(bf16[4,16,704]{2,1,0:T(8,128)(2,1)S(1)} %get-tuple-element.41), channel_id=1, source_target_pairs={{0,32},{32,64},{64,96},{96,0},{1,33},{33,65},{65,97},{97,1},{2,34}... | collective-permute-start | bytes 270344 | tf_op jit(solution)/shard_map/ppermute | solution.py:507
  70.7 5.2 %collective-permute-start.15 = (bf16[4,16,704]{2,1,0:T(8,128)(2,1)S(1)}, bf16[4,16,704]{2,1,0:T(8,128)(2,1)S(1)}, u32[]{:S(2)}, u32[]{:S(2)}) collective-permute-start(bf16[4,16,704]{2,1,0:T(8,128)(2,1)S(1)} %get-tuple-element.48), channel_id=1, source_target_pairs={{0,96},{32,0},{64,32},{96,64},{1,97},{33,1},{65,33},{97,65},{2,98}... | collective-permute-start | bytes 270344 | tf_op jit(solution)/shard_map/ppermute | solution.py:507
  72.6 6.2 %collective-permute-start.16 = (bf16[4,16,704]{2,1,0:T(8,128)(2,1)S(1)}, bf16[4,16,704]{2,1,0:T(8,128)(2,1)S(1)}, u32[]{:S(2)}, u32[]{:S(2)}) collective-permute-start(bf16[4,16,704]{2,1,0:T(8,128)(2,1)S(1)} %get-tuple-element.49), channel_id=1, source_target_pairs={{0,64},{32,96},{64,0},{96,32},{1,65},{33,97},{65,1},{97,33},{2,66}... | collective-permute-start | bytes 270344 | tf_op jit(solution)/shard_map/ppermute | solution.py:507
  72.8 6.9 %collective-permute-start.17 = (bf16[4,16,704]{2,1,0:T(8,128)(2,1)S(1)}, bf16[4,16,704]{2,1,0:T(8,128)(2,1)S(1)}, u32[]{:S(2)}, u32[]{:S(2)}) collective-permute-start(bf16[4,16,704]{2,1,0:T(8,128)(2,1)S(1)} %get-tuple-element.50), channel_id=1, source_target_pairs={{0,32},{32,64},{64,96},{96,0},{1,33},{33,65},{65,97},{97,1},{2,34}... | collective-permute-start | bytes 270344 | tf_op jit(solution)/shard_map/ppermute | solution.py:507
where the time goes:
time: 81.8 us; the launch traced here: 81.4 us
  starting transfers between devices  34.4 us (42%)
  Pallas kernels  29.4 us (36%)
  waiting for transfers between devices  9.21 us (11%)
  local copies, waits for them, and re-layouts  8.18 us (10%)
    pallas_call x2, Pallas kernels, window_layer(): call(functools.partial(window_kernel, straddle), [part_shape] * 4 + [toke...  17.1 us
    ppermute x8, starting transfers between devices, to_dates(): lax.ppermute(piece, space, routes[kind][k])  16 us
    ppermute x6, starting transfers between devices, to_home(): lax.ppermute(piece, 'date', [(i, (i - k) % date_axis) for i in range(date...  12 us
    unnamed x32, local copies, waits for them, and re-layouts  8.18 us
    pallas_call x2, Pallas kernels, time_layer(): call(functools.partial(time_kernel, features // heads), [part_shape] * 4...  7.64 us
    ppermute x4, starting transfers between devices, local(): lax.ppermute(piece, plane, routes[name])  6.43 us
    ppermute x6, waiting for transfers between devices, to_home(): lax.ppermute(piece, 'date', [(i, (i - k) % date_axis) for i in range(date...  6.1 us
    ppermute x4, waiting for transfers between devices, local(): lax.ppermute(piece, plane, routes[name])  3.09 us
  transfers between devices with their start and end apart: 18, of which 5 were waited for; matrix products, arithmetic and copies ran while one was open for 0% of the time, Pallas kernels for 33%

commit v1 on v0

--- a/solution.py
+++ b/solution.py
@@ -42,8 +42,24 @@
     return centred * lax.rsqrt(variance + 1e-05) * gain
 
 
+TAIL = (
+    3.309271834662358e-05,
+    -7.692189790236681e-04,
+    8.080714484816941e-03,
+    -5.3412101383958015e-02,
+    -4.587709752912628e-01,
+    -1.1512017013906806,
+    -9.999930610827096e-01,
+)
+
+
 def gelu(x):
-    return 0.5 * x * (1.0 + lax.erf(x * math.sqrt(0.5)))
+    size = jnp.abs(x)
+    a = jnp.minimum(size, 6.0)
+    power = TAIL[0]
+    for factor in TAIL[1:]:
+        power = power * a + factor
+    return jnp.maximum(x, 0.0) - size * jnp.exp2(power)
 
 
 def column_blocks(total, width):
@@ -142,37 +158,32 @@
             out[h, row * WINDOW : (row + 1) * WINDOW, :] = jnp.where(wide < POSITIONS, left, right)
 
 
-def window_kernel(straddle, *refs):
-    meta, scale, low, high, *refs = refs
-    if straddle:
-        low_right, high_right, _, *refs = refs
-    bias, qkv, lift, up, down, attention_gain, forward_gain, *refs = refs
-    outs, token, refs = refs[:4], refs[4], refs[5:]
-    queries, keys, low_keys, values, mixed_heads, work = refs
+def inner_tokens(low, high):
+    inner = WINDOW // 2 * WINDOW
+    tokens = jnp.concatenate([low[:, :inner], high[:, :inner]], axis=1)
+    return tokens.reshape(tokens.shape[0] * POSITIONS, tokens.shape[2])
+
+
+def straddle_tokens(low_left, high_left, low_right, high_right, work):
+    half = WINDOW // 2
+    for side, (left, right) in enumerate(((low_left, low_right), (high_left, high_right))):
+        for d in range(left.shape[0]):
+            left_rows = left[d, half * WINDOW :, :].astype(F32)
+            right_rows = right[d].astype(F32)
+            for i in range(half):
+                base = d * POSITIONS + (side * half + i) * WINDOW
+                part = slice(i * SHIFT, (i + 1) * SHIFT)
+                work[base : base + SHIFT, :] = left_rows[part, :]
+                work[base + SHIFT : base + WINDOW, :] = right_rows[part, :]
+    return work[...].astype(BF16)
+
+
+def attend(tokens, last_row, last_col, scale, bias, qkv, mixed_heads, scratch):
+    queries, keys, low_keys, values = scratch
     features = qkv.shape[0]
     heads = bias.shape[0]
     size = features // heads
-    dates = outs[0].shape[0]
-    token_total = dates * POSITIONS
-    half = WINDOW // 2
-    inner_part = half * WINDOW
-    z = meta[0]
-    token[...] = jnp.zeros(token.shape, F32)
-    if straddle:
-        for side, (left, right) in enumerate(((low, low_right), (high, high_right))):
-            for d in range(dates):
-                left_rows = left[d, inner_part:, :].astype(F32)
-                right_rows = right[d].astype(F32)
-                for i in range(half):
-                    base = d * POSITIONS + (side * half + i) * WINDOW
-                    part = slice(i * SHIFT, (i + 1) * SHIFT)
-                    work[base : base + SHIFT, :] = left_rows[part, :]
-                    work[base + SHIFT : base + WINDOW, :] = right_rows[part, :]
-        tokens = work[...].astype(BF16)
-    else:
-        tokens = jnp.concatenate([low[:, :inner_part], high[:, :inner_part]], axis=1)
-        tokens = tokens.reshape(token_total, features)
-
+    token_total = tokens.shape[0]
     project(tokens, qkv, queries, keys, values)
 
     wide_keys = keys[...].astype(F32)
@@ -194,9 +205,9 @@
     lane = lax.broadcasted_iota(jnp.int32, (POSITIONS, PAIR), 1)
     line = lax.broadcasted_iota(jnp.int32, (POSITIONS, PAIR), 0)
     first_window = lane < POSITIONS
-    apart = (((lane ^ line) & 32) != 0) & (meta[1] != 0)
-    if straddle:
-        apart = apart | ((((lane ^ line) & 4) != 0) & (meta[2] != 0))
+    apart = (((lane ^ line) & 32) != 0) & (last_row[0] != 0)
+    if last_col is not None:
+        apart = apart | ((((lane ^ line) & 4) != 0) & (last_col[0] != 0))
     closed = jnp.where(apart, MASKED, 0.0)
     keep_first = jnp.where(first_window, 1.0, 0.0).astype(BF16)
     keep_second = jnp.where(first_window, 0.0, 1.0).astype(BF16)
@@ -234,48 +245,79 @@
     units = [(b, p) for b in range(len(blocks)) for p in range(token_total // PAIR)]
     staggered(units, early, late)
 
+def settle(tokens, mixed_heads, lift, up, down, attention_gain, forward_gain):
+    features = tokens.shape[1]
     projected = dot_first(mixed_heads[...], lift[...])
     gain = attention_gain[...].reshape(1, features)
     resid = (tokens.astype(F32) + layer_norm(projected, gain)).astype(BF16)
 
-    lowered = jnp.zeros((token_total, features), F32)
-    for first, last in column_blocks(up.shape[1], 512):
-        hidden = gelu(dot(resid, up[:, first:last])).astype(BF16)
-        lowered = lowered + dot_last(hidden, down[:, first:last])
-    mixed = resid.astype(F32) + layer_norm(lowered, forward_gain[...].reshape(1, features))
-
-    part = POSITIONS // 4
-    if straddle:
-        work[...] = mixed
-    else:
-        narrow = mixed.astype(BF16).reshape(dates, 4, part, features)
-    for q in range(4):
-        if straddle:
-            quarter = []
-            for d in range(dates):
-                lines = []
-                for i in range(half):
-                    base = d * POSITIONS + ((q // 2) * half + i) * WINDOW + (q % 2) * SHIFT
-                    lines.append(work[base : base + SHIFT, :])
-                quarter.append(jnp.concatenate(lines, axis=0).astype(BF16)[None])
-            quarter = jnp.concatenate(quarter, axis=0)
-        else:
-            quarter = narrow[:, q]
+    parts = []
+
+    def raise_block(span):
+        return dot(resid, up[:, slice(*span)])
+
+    def lower_block(span, raised):
+        parts.append(dot_last(gelu(raised).astype(BF16), down[:, slice(*span)]))
+        if len(parts) > 1:
+            parts[:] = [parts[0] + parts[1]]
+
+    staggered(column_blocks(up.shape[1], 512), raise_block, lower_block)
+    (lowered,) = parts
+    return resid.astype(F32) + layer_norm(lowered, forward_gain[...].reshape(1, features))
+
+
+def send_quarters(quarters, place, outs):
+    for q, quarter in enumerate(quarters):
         for k in range(4):
 
-            @pl.when((z + k) % 4 == q)
+            @pl.when((place[0] + k) % 4 == q)
             def _(quarter=quarter, k=k):
                 outs[k][...] = quarter
 
 
-def time_kernel(size, meta, rank, *refs):
+def inner_attention(low, high, last_row, scale, bias, qkv, mixed_heads, *scratch):
+    attend(inner_tokens(low, high), last_row, None, scale, bias, qkv, mixed_heads, scratch)
+
+
+def inner_settle(place, low, high, mixed_heads, lift, up, down, gain, forward_gain, *outs):
+    *outs, token = outs
+    token[...] = jnp.zeros(token.shape, F32)
+    tokens = inner_tokens(low, high)
+    mixed = settle(tokens, mixed_heads, lift, up, down, gain, forward_gain)
+    narrow = mixed.astype(BF16).reshape(low.shape[0], 4, POSITIONS // 4, low.shape[2])
+    send_quarters([narrow[:, q] for q in range(4)], place, outs)
+
+
+def straddle_window(place, last_row, last_col, scale, *refs):
+    corners, _, bias, qkv, *refs = refs[:4], *refs[4:]
+    lift, up, down, attention_gain, forward_gain, *refs = refs
+    outs, token, scratch, mixed_heads, work = refs[:4], refs[4], refs[5:9], refs[9], refs[10]
+    token[...] = jnp.zeros(token.shape, F32)
+    tokens = straddle_tokens(*corners, work)
+    attend(tokens, last_row, last_col, scale, bias, qkv, mixed_heads, scratch)
+    work[...] = settle(tokens, mixed_heads, lift, up, down, attention_gain, forward_gain)
+    half = WINDOW // 2
+    quarters = []
+    for q in range(4):
+        quarter = []
+        for d in range(corners[0].shape[0]):
+            lines = []
+            for i in range(half):
+                base = d * POSITIONS + ((q // 2) * half + i) * WINDOW + (q % 2) * SHIFT
+                lines.append(work[base : base + SHIFT, :])
+            quarter.append(jnp.concatenate(lines, axis=0).astype(BF16)[None])
+        quarters.append(jnp.concatenate(quarter, axis=0))
+    send_quarters(quarters, place, outs)
+
+
+def time_kernel(size, place, rank, *refs):
     pieces, refs = refs[:4], refs[4:]
     _, embedding, time_gain, qkv, lift, *refs = refs
     outs, token, refs = refs[:4], refs[4], refs[5:]
     queries, keys, values, mixed_heads = refs
     features = qkv.shape[0]
     heads = features // size
-    z = meta[0]
+    z = place[0]
     own, pixel_count, _ = pieces[0].shape
     dates = 4 * own
     group = 128 // dates
@@ -340,11 +382,11 @@
         outs[k][...] = (wide[k] + jnp.concatenate(parts, axis=1)).astype(BF16)
 
 
-def assemble(meta, *refs):
+def assemble(place, *refs):
     inner, straddle, (out, work) = refs[:4], refs[4:8], refs[8:]
     dates, rows, cols, features = out.shape
     half = rows // 2
-    z = meta[0]
+    z = place[0]
     for k in range(4):
         q = (z + k) % 4
         block = inner[k][...].astype(F32)
@@ -411,7 +453,8 @@
     date_axis = lax.axis_size("date")
     z = lax.axis_index("date")
     last_row, last_col = routes["last"](lax.axis_index("row"), lax.axis_index("col"))
-    meta = jnp.stack([z, last_row, last_col]).astype(jnp.int32)
+    z = z.astype(jnp.int32).reshape(1)
+    last_row, last_col = last_row.reshape(1), last_col.reshape(1)
 
     piece_shape = jax.ShapeDtypeStruct((dates, POSITIONS // 2 + part, features), BF16)
     part_shape = jax.ShapeDtypeStruct((dates, part, features), BF16)
@@ -450,30 +493,58 @@
         pltpu.VMEM((features, token_total), BF16),
     ]
 
-    def window_layer(straddle, inputs):
+    weights = (
+        window_output_weight,
+        feedforward_up_weight,
+        feedforward_down_weight.T,
+        attention_norm_gain,
+        feedforward_norm_gain,
+    )
+    settle_flops = 2 * token_total * features * (features + 2 * hidden)
+    attend_flops = 2 * token_total * features * 3 * features * 2
+
+    def inner_layer(low, high):
+        mixed_heads = call(
+            inner_attention,
+            jax.ShapeDtypeStruct((features, token_total), BF16),
+            [VMEM] * 2 + [SMEM] * 2 + [VMEM] * 2,
+            projected[:4],
+            attend_flops,
+            4 * 10**6,
+            "inner_attention",
+            14,
+        )(low, high, last_row, head_logit_scale, bias, window_query_key_value_weight)
         return call(
-            functools.partial(window_kernel, straddle),
+            inner_settle,
             [part_shape] * 4 + [token_shape],
-            [SMEM, SMEM]
-            + [VMEM] * 2
-            + ([VMEM] * 2 + [ANY] if straddle else [])
-            + [VMEM] * 7,
+            [SMEM] + [VMEM] * 8,
+            [],
+            settle_flops,
+            9 * 10**6,
+            "inner_settle",
+            20,
+        )(z, low, high, mixed_heads, *weights)
+
+    def straddle_layer(corners, token):
+        return call(
+            straddle_window,
+            [part_shape] * 4 + [token_shape],
+            [SMEM] * 4 + [VMEM] * 4 + [ANY] + [VMEM] * 7,
             projected + [pltpu.VMEM((token_total, features), F32)],
-            2 * token_total * features * (4 * features + 2 * hidden),
-            12 * 10**6,
-            "window_straddle" if straddle else "window_inner",
+            attend_flops + settle_flops,
+            13 * 10**6,
+            "straddle_window",
             24,
         )(
-            meta,
+            z,
+            last_row,
+            last_col,
             head_logit_scale,
-            *inputs,
+            *corners,
+            token,
             bias,
             window_query_key_value_weight,
-            window_output_weight,
-            feedforward_up_weight,
-            feedforward_down_weight.T,
-            attention_norm_gain,
-            feedforward_norm_gain,
+            *weights,
         )
 
     def time_layer(pieces, token):
@@ -487,7 +558,7 @@
             "time_layer",
             14,
         )(
-            meta,
+            z,
             acquisition_rank,
             *pieces,
             token,
@@ -508,9 +579,9 @@
             for k, piece in enumerate(pieces)
         ]
 
-    *inner, token = window_layer(False, [low, high])
+    *inner, token = inner_layer(low, high)
     inner = to_dates(inner, "inner")
-    *straddle, token = window_layer(True, [low, high, low_right, high_right, token])
+    *straddle, token = straddle_layer([low, high, low_right, high_right], token)
     straddle = to_dates(straddle, "straddle")
     *inner, token = time_layer(inner, token)
     inner = to_home(inner)
@@ -524,7 +595,7 @@
         0,
         tile_bytes * 2,
         "assemble",
-    )(meta, *inner, *straddle)
+    )(z, *inner, *straddle)
 
 
 def plan(mesh):

time: 81.8 us -> 76.7 us (0.938)
  local copies, waits for them, and re-layouts: 8.18 us -> 3.08 us
  Pallas kernels: 29.4 us -> 28.3 us
  waiting for transfers between devices: 9.21 us -> 10.3 us
    unnamed x32, local copies, waits for them, and re-layouts: 8.18 us -> 3.08 us
    ppermute x4, waiting for transfers between devices: 3.09 us -> 4.38 us  [local(): lax.ppermute(piece, plane, routes[name])]
    pallas_call x2 -> x3, Pallas kernels: 17.1 us -> 17.4 us  [the longest x1 8.64 us: straddle_layer(): call(straddle_window, [part_shape] * 4 + [token_shape], [SMEM] * 4 + [VME...]
  transfers between devices with their start and end apart: 18 -> 18, of which waited for: 5 -> 5; matrix products, arithmetic and copies ran while one was open for 0% -> 0% of each run, Pallas kernels for 33% -> 35%
where the time goes in v1:
time: 76.7 us; the launch traced here: 76.5 us
  starting transfers between devices  34.6 us (45%)
  Pallas kernels  28.3 us (37%)
  waiting for transfers between devices  10.3 us (13%)
  local copies, waits for them, and re-layouts  3.08 us (4%)
    ppermute x8, starting transfers between devices, to_dates(): lax.ppermute(piece, space, routes[kind][k])  16 us
    ppermute x6, starting transfers between devices, to_home(): lax.ppermute(piece, 'date', [(i, (i - k) % date_axis) for i in range(date...  12.1 us
    pallas_call x1, Pallas kernels, straddle_layer(): call(straddle_window, [part_shape] * 4 + [token_shape], [SMEM] * 4 + [VME...  8.64 us
    pallas_call x2, Pallas kernels, time_layer(): call(functools.partial(time_kernel, features // heads), [part_shape] * 4...  7.63 us
    ppermute x4, starting transfers between devices, local(): lax.ppermute(piece, plane, routes[name])  6.5 us
    ppermute x6, waiting for transfers between devices, to_home(): lax.ppermute(piece, 'date', [(i, (i - k) % date_axis) for i in range(date...  5.93 us
    pallas_call x1, Pallas kernels, inner_layer(): call(inner_settle, [part_shape] * 4 + [token_shape], [SMEM] + [VMEM] * 8,...  4.86 us
    ppermute x4, waiting for transfers between devices, local(): lax.ppermute(piece, plane, routes[name])  4.38 us
  transfers between devices with their start and end apart: 18, of which 5 were waited for; matrix products, arithmetic and copies ran while one was open for 0% of the time, Pallas kernels for 35%

profile of v1, /device:TPU:0, one launch (start us, length us, event | category | flops | bytes accessed | tf_op | source)
XLA Modules:
  0.0 76.5 jit_solution(6868582307753934283)
XLA Ops:
  0.0 1.1 %copy-done.12 = bf16[4,8,16,704]{3,2,1,0:T(8,128)(2,1)S(1)} copy-done((bf16[4,8,16,704]{3,2,1,0:T(8,128)(2,1)S(1)}, bf16[4,8,16,704]{3,2,1,0:T(8,128)(2,1)}, u32[]{:S(2)}) %copy-start.12) | copy-done | bytes 720920
  1.1 0.3 pack.1
  1.5 0.0 copy-start.15
  1.5 1.7 %collective-permute-start = (bf16[4,48,704]{2,1,0:T(8,128)(2,1)S(1)}, bf16[4,48,704]{2,1,0:T(8,128)(2,1)S(1)}, u32[]{:S(2)}, u32[]{:S(2)}) collective-permute-start(bf16[4,48,704]{2,1,0:T(8,128)(2,1)S(1)} %get-tuple-element.28), channel_id=1, source_target_pairs={{0,2},{1,3},{2,4},{3,5},{4,6},{5,7},{6,0},{7,1},{8,10},{9,11},{10,... | collective-permute-start | bytes 811016 | tf_op jit(solution)/shard_map/ppermute | solution.py:475
  3.2 3.9 %collective-permute-start.1 = (bf16[4,48,704]{2,1,0:T(8,128)(2,1)S(1)}, bf16[4,48,704]{2,1,0:T(8,128)(2,1)S(1)}, u32[]{:S(2)}, u32[]{:S(2)}) collective-permute-start(bf16[4,48,704]{2,1,0:T(8,128)(2,1)S(1)} %get-tuple-element.29), channel_id=1, source_target_pairs={{4,2},{5,3},{6,4},{7,5},{8,6},{9,7},{10,0},{11,1},{12,10},{13,11},... | collective-permute-start | bytes 811016 | tf_op jit(solution)/shard_map/ppermute | solution.py:475
  7.1 0.0 collective-permute-start.6
  7.1 0.9 %collective-permute-start.7 = (bf16[4,16,704]{2,1,0:T(8,128)(2,1)S(1)}, bf16[4,16,704]{2,1,0:T(8,128)(2,1)S(1)}, u32[]{:S(2)}, u32[]{:S(2)}) collective-permute-start(bf16[4,16,704]{2,1,0:T(8,128)(2,1)S(1)} %get-tuple-element.35), channel_id=1, source_target_pairs={{5,2},{6,3},{7,4},{4,5},{9,6},{10,7},{11,0},{8,1},{13,10},{14,11},... | collective-permute-start | bytes 270344 | tf_op jit(solution)/shard_map/ppermute | solution.py:475
  8.0 0.0 copy-done.13
  8.0 0.0 copy-done.14
  8.0 1.8 %position_bias.1.bias.refs_5_ = f32[22,64,128]{2,1,0:T(8,128)S(1)} custom-call(f32[2,512]{1,0:T(2,128)S(1)} %copy-done.14, f32[22,512]{1,0:T(8,128)S(1)} %bitcast.7), custom_call_target="tpu_custom_call" | custom-call | flops 1000000000 | bytes 1000000 | tf_op jit(solution)/shard_map/position_bias/pallas_call | solution.py:478
  9.8 0.0 copy-start.2
  9.8 0.0 copy-start.4
  9.8 0.0 copy-start.7
  9.9 0.0 copy-start.8
  9.9 2.1 %collective-permute-done.low.refs_0_ = bf16[4,48,704]{2,1,0:T(8,128)(2,1)S(1)} collective-permute-done((bf16[4,48,704]{2,1,0:T(8,128)(2,1)S(1)}, bf16[4,48,704]{2,1,0:T(8,128)(2,1)S(1)}, u32[]{:S(2)}, u32[]{:S(2)}) %collective-permute-start) | collective-permute-done | bytes 270368 | tf_op jit(solution)/shard_map/ppermute | solution.py:475
  12.0 2.3 %collective-permute-done.1.high.refs_1_ = bf16[4,48,704]{2,1,0:T(8,128)(2,1)S(1)} collective-permute-done((bf16[4,48,704]{2,1,0:T(8,128)(2,1)S(1)}, bf16[4,48,704]{2,1,0:T(8,128)(2,1)S(1)}, u32[]{:S(2)}, u32[]{:S(2)}) %collective-permute-start.1) | collective-permute-done | bytes 270368 | tf_op jit(solution)/shard_map/ppermute | solution.py:475
  14.2 0.0 copy-done.15
  14.2 1.9 %copy-done.10 = bf16[704,2112]{1,0:T(8,128)(2,1)S(1)} copy-done((bf16[704,2112]{1,0:T(8,128)(2,1)S(1)}, bf16[704,2112]{1,0:T(8,128)(2,1)}, u32[]{:S(2)}) %copy-start.10) | copy-done | bytes 2973720
  16.1 3.8 %inner_attention.1.mixed_heads = bf16[704,256]{1,0:T(8,128)(2,1)S(1)} custom-call(bf16[4,48,704]{2,1,0:T(8,128)(2,1)S(1)} %collective-permute-done.low.refs_0_, bf16[4,48,704]{2,1,0:T(8,128)(2,1)S(1)} %collective-permute-done.1.high.refs_1_, s32[1]{0:T(128)} %bitcast.1.last_row, f32[22]{0:T(128)S(1)} %copy-done.15, ...), custom_call_target="tpu_custom_call" | custom-call | flops 1522532352 | bytes 4000000 | tf_op jit(solution)/shard_map/inner_attention/pallas_call | solution.py:507
  20.0 0.0 copy-done.3
  20.0 0.0 copy-done.2
  20.0 0.0 copy-done.4
  20.0 0.0 copy-done.7
  20.0 0.0 copy-done.8
  20.0 0.0 copy-start.11
  20.0 4.9 %inner_settle.1 = (bf16[4,16,704]{2,1,0:T(8,128)(2,1)S(1)}, bf16[4,16,704]{2,1,0:T(8,128)(2,1)S(1)}, bf16[4,16,704]{2,1,0:T(8,128)(2,1)S(1)}, bf16[4,16,704]{2,1,0:T(8,128)(2,1)S(1)}, f32[8,128]{1,0:T(8,128)S(1)}) custom-call(s32[1]{0:T(128)} %bitcast.place, bf16[4,48,704]{2,1,0:T(8,128)(2,1)S(1)} %collective-permute-done.low.refs_0_, ...), custom_call_target="tpu_custom_call" | custom-call | flops 2283798528 | bytes 9000000 | tf_op jit(solution)/shard_map/inner_settle/pallas_call | solution.py:517
  24.9 2.8 %collective-permute-start.2 = (bf16[4,16,704]{2,1,0:T(8,128)(2,1)S(1)}, bf16[4,16,704]{2,1,0:T(8,128)(2,1)S(1)}, u32[]{:S(2)}, u32[]{:S(2)}) collective-permute-start(bf16[4,16,704]{2,1,0:T(8,128)(2,1)S(1)} %get-tuple-element.30), channel_id=1, source_target_pairs={{2,0},{3,1},{4,2},{5,3},{6,4},{7,5},{0,6},{1,7},{10,8},{11,9},{12,... | collective-permute-start | bytes 270344 | tf_op jit(solution)/shard_map/ppermute | solution.py:572
  27.7 1.4 %collective-permute-start.3 = (bf16[4,16,704]{2,1,0:T(8,128)(2,1)S(1)}, bf16[4,16,704]{2,1,0:T(8,128)(2,1)S(1)}, u32[]{:S(2)}, u32[]{:S(2)}) collective-permute-start(bf16[4,16,704]{2,1,0:T(8,128)(2,1)S(1)} %get-tuple-element.31), channel_id=1, source_target_pairs={{2,32},{3,33},{4,34},{5,35},{6,36},{7,37},{0,38},{1,39},{10,40},{1... | collective-permute-start | bytes 270344 | tf_op jit(solution)/shard_map/ppermute | solution.py:572
  29.1 5.3 %collective-permute-start.4 = (bf16[4,16,704]{2,1,0:T(8,128)(2,1)S(1)}, bf16[4,16,704]{2,1,0:T(8,128)(2,1)S(1)}, u32[]{:S(2)}, u32[]{:S(2)}) collective-permute-start(bf16[4,16,704]{2,1,0:T(8,128)(2,1)S(1)} %get-tuple-element.32), channel_id=1, source_target_pairs={{2,68},{3,69},{4,70},{5,71},{6,72},{7,73},{0,74},{1,75},{10,76},{1... | collective-permute-start | bytes 270344 | tf_op jit(solution)/shard_map/ppermute | solution.py:572
  34.4 0.0 collective-permute-done.6.refs_2_
  34.4 0.6 collective-permute-start.5
  35.1 0.0 collective-permute-done.7.refs_3_
  35.1 0.0 copy-start.5
  35.1 0.0 copy-start.6
  35.1 0.0 copy-start.9
  35.1 8.6 %straddle_window.1 = (bf16[4,16,704]{2,1,0:T(8,128)(2,1)S(1)}, bf16[4,16,704]{2,1,0:T(8,128)(2,1)S(1)}, bf16[4,16,704]{2,1,0:T(8,128)(2,1)S(1)}, bf16[4,16,704]{2,1,0:T(8,128)(2,1)S(1)}, f32[8,128]{1,0:T(8,128)S(1)}) custom-call(s32[1]{0:T(128)} %bitcast.place, s32[1]{0:T(128)} %bitcast.1.last_row, s32[1]{0:T(128)} %bitcast.4.last_col, f32[22]{0:T(128)S(1)} %copy-done.15, ...), custom_call_target="tpu_custom_call" | custom-call | flops 3806330880 | bytes 13000000 | tf_op jit(solution)/shard_map/straddle_window/pallas_call | solution.py:529
  43.8 3.8 %collective-permute-start.11 = (bf16[4,16,704]{2,1,0:T(8,128)(2,1)S(1)}, bf16[4,16,704]{2,1,0:T(8,128)(2,1)S(1)}, u32[]{:S(2)}, u32[]{:S(2)}) collective-permute-start(bf16[4,16,704]{2,1,0:T(8,128)(2,1)S(1)} %get-tuple-element.42), channel_id=1, source_target_pairs={{2,0},{3,1},{4,2},{5,3},{6,4},{7,5},{0,6},{1,7},{10,8},{11,9},{12,... | collective-permute-start | bytes 270344 | tf_op jit(solution)/shard_map/ppermute | solution.py:572
  47.6 0.0 collective-permute-done.2.refs_0_
  47.6 0.0 collective-permute-start.12
  47.6 0.0 collective-permute-done.3.refs_1_
  47.6 0.1 collective-permute-start.13
  47.7 0.0 collective-permute-done.4.refs_2_
  47.7 1.9 %collective-permute-start.14 = (bf16[4,16,704]{2,1,0:T(8,128)(2,1)S(1)}, bf16[4,16,704]{2,1,0:T(8,128)(2,1)S(1)}, u32[]{:S(2)}, u32[]{:S(2)}) collective-permute-start(bf16[4,16,704]{2,1,0:T(8,128)(2,1)S(1)} %get-tuple-element.45), channel_id=1, source_target_pairs={{2,101},{3,102},{4,103},{5,100},{6,105},{7,106},{0,107},{1,104},{1... | collective-permute-start | bytes 270344 | tf_op jit(solution)/shard_map/ppermute | solution.py:572
  49.6 0.0 collective-permute-done.5.refs_3_
  49.6 0.0 copy-done.1
  49.7 3.8 %time_layer.2 = (bf16[4,16,704]{2,1,0:T(8,128)(2,1)S(1)}, bf16[4,16,704]{2,1,0:T(8,128)(2,1)S(1)}, bf16[4,16,704]{2,1,0:T(8,128)(2,1)S(1)}, bf16[4,16,704]{2,1,0:T(8,128)(2,1)S(1)}, f32[8,128]{1,0:T(8,128)S(1)}) custom-call(s32[1]{0:T(128)} %bitcast.place, s32[16]{0:T(128)S(1)} %copy-done.9, bf16[4,16,704]{2,1,0:T(8,128)(2,1)S(1)} %collective-permute-done.2.refs_0_, ...), custom_call_target="tpu_custom_call" | custom-call | flops 1015021568 | bytes 5000000 | tf_op jit(solution)/shard_map/time_layer/pallas_call | solution.py:551
  53.5 3.7 %collective-permute-start.8 = (bf16[4,16,704]{2,1,0:T(8,128)(2,1)S(1)}, bf16[4,16,704]{2,1,0:T(8,128)(2,1)S(1)}, u32[]{:S(2)}, u32[]{:S(2)}) collective-permute-start(bf16[4,16,704]{2,1,0:T(8,128)(2,1)S(1)} %get-tuple-element.39), channel_id=1, source_target_pairs={{0,96},{32,0},{64,32},{96,64},{1,97},{33,1},{65,33},{97,65},{2,98}... | collective-permute-start | bytes 270344 | tf_op jit(solution)/shard_map/ppermute | solution.py:578
  57.2 0.0 collective-permute-done.11.refs_0_
  57.2 4.2 %collective-permute-start.9 = (bf16[4,16,704]{2,1,0:T(8,128)(2,1)S(1)}, bf16[4,16,704]{2,1,0:T(8,128)(2,1)S(1)}, u32[]{:S(2)}, u32[]{:S(2)}) collective-permute-start(bf16[4,16,704]{2,1,0:T(8,128)(2,1)S(1)} %get-tuple-element.40), channel_id=1, source_target_pairs={{0,64},{32,96},{64,0},{96,32},{1,65},{33,97},{65,1},{97,33},{2,66}... | collective-permute-start | bytes 270344 | tf_op jit(solution)/shard_map/ppermute | solution.py:578
  61.4 0.0 collective-permute-done.12.refs_1_
  61.4 1.1 %collective-permute-start.10 = (bf16[4,16,704]{2,1,0:T(8,128)(2,1)S(1)}, bf16[4,16,704]{2,1,0:T(8,128)(2,1)S(1)}, u32[]{:S(2)}, u32[]{:S(2)}) collective-permute-start(bf16[4,16,704]{2,1,0:T(8,128)(2,1)S(1)} %get-tuple-element.41), channel_id=1, source_target_pairs={{0,32},{32,64},{64,96},{96,0},{1,33},{33,65},{65,97},{97,1},{2,34}... | collective-permute-start | bytes 270344 | tf_op jit(solution)/shard_map/ppermute | solution.py:578
  62.5 0.0 collective-permute-done.13.refs_2_
  62.5 0.0 collective-permute-done.14.refs_3_
  62.5 3.8 %time_layer.3 = (bf16[4,16,704]{2,1,0:T(8,128)(2,1)S(1)}, bf16[4,16,704]{2,1,0:T(8,128)(2,1)S(1)}, bf16[4,16,704]{2,1,0:T(8,128)(2,1)S(1)}, bf16[4,16,704]{2,1,0:T(8,128)(2,1)S(1)}, f32[8,128]{1,0:T(8,128)}) custom-call(s32[1]{0:T(128)} %bitcast.place, s32[16]{0:T(128)S(1)} %copy-done.9, bf16[4,16,704]{2,1,0:T(8,128)(2,1)S(1)} %collective-permute-done.11.refs_0_, ...), custom_call_target="tpu_custom_call" | custom-call | flops 1015021568 | bytes 5000000 | tf_op jit(solution)/shard_map/time_layer/pallas_call | solution.py:551
  66.3 2.2 %collective-permute-start.15 = (bf16[4,16,704]{2,1,0:T(8,128)(2,1)S(1)}, bf16[4,16,704]{2,1,0:T(8,128)(2,1)S(1)}, u32[]{:S(2)}, u32[]{:S(2)}) collective-permute-start(bf16[4,16,704]{2,1,0:T(8,128)(2,1)S(1)} %get-tuple-element.48), channel_id=1, source_target_pairs={{0,96},{32,0},{64,32},{96,64},{1,97},{33,1},{65,33},{97,65},{2,98}... | collective-permute-start | bytes 270344 | tf_op jit(solution)/shard_map/ppermute | solution.py:578
  68.5 0.0 collective-permute-start.16
  68.5 0.0 collective-permute-done.8.refs_1_
  68.5 0.9 %collective-permute-start.17 = (bf16[4,16,704]{2,1,0:T(8,128)(2,1)S(1)}, bf16[4,16,704]{2,1,0:T(8,128)(2,1)S(1)}, u32[]{:S(2)}, u32[]{:S(2)}) collective-permute-start(bf16[4,16,704]{2,1,0:T(8,128)(2,1)S(1)} %get-tuple-element.50), channel_id=1, source_target_pairs={{0,32},{32,64},{64,96},{96,0},{1,33},{33,65},{65,97},{97,1},{2,34}... | collective-permute-start | bytes 270344 | tf_op jit(solution)/shard_map/ppermute | solution.py:578
  69.5 0.0 collective-permute-done.9.refs_2_
  69.5 0.0 collective-permute-done.10.refs_3_
  69.5 2.3 %collective-permute-done.15.refs_5_ = bf16[4,16,704]{2,1,0:T(8,128)(2,1)S(1)} collective-permute-done((bf16[4,16,704]{2,1,0:T(8,128)(2,1)S(1)}, bf16[4,16,704]{2,1,0:T(8,128)(2,1)S(1)}, u32[]{:S(2)}, u32[]{:S(2)}) %collective-permute-start.15) | collective-permute-done | bytes 90144 | tf_op jit(solution)/shard_map/ppermute | solution.py:578
  71.7 3.0 %collective-permute-done.16.refs_6_ = bf16[4,16,704]{2,1,0:T(8,128)(2,1)S(1)} collective-permute-done((bf16[4,16,704]{2,1,0:T(8,128)(2,1)S(1)}, bf16[4,16,704]{2,1,0:T(8,128)(2,1)S(1)}, u32[]{:S(2)}, u32[]{:S(2)}) %collective-permute-start.16) | collective-permute-done | bytes 90144 | tf_op jit(solution)/shard_map/ppermute | solution.py:578
  74.7 0.7 collective-permute-done.17.refs_7_
  75.4 1.1 %assemble.1 = bf16[4,8,16,704]{3,2,1,0:T(8,128)(2,1)} custom-call(s32[1]{0:T(128)} %bitcast.place, bf16[4,16,704]{2,1,0:T(8,128)(2,1)S(1)} %get-tuple-element.38.refs_0_, bf16[4,16,704]{2,1,0:T(8,128)(2,1)S(1)} %collective-permute-done.8.refs_1_, bf16[4,16,704]{2,1,0:T(8,128)(2,1)S(1)} %collective-permute-done.9.refs_2_, ...), custom_call_target="tpu_custom_call" | custom-call | bytes 1441792 | tf_op jit(solution)/shard_map/assemble/pallas_call | solution.py:590
  (12 shorter events, 0.0 us)
Async XLA Ops:
  0.0 1.1 %copy-start.12 = (bf16[4,8,16,704]{3,2,1,0:T(8,128)(2,1)S(1)}, bf16[4,8,16,704]{3,2,1,0:T(8,128)(2,1)}, u32[]{:S(2)}) copy-start(bf16[4,8,16,704]{3,2,1,0:T(8,128)(2,1)} %pixels.1) | copy-start | bytes 2162692
  1.1 6.8 %copy-start.13 = (f32[512,22]{0,1:T(8,128)S(1)}, f32[512,22]{0,1:T(8,128)}, u32[]{:S(2)}) copy-start(f32[512,22]{0,1:T(8,128)} %param.19) | copy-start | bytes 135172
  1.1 6.8 %copy-start.14 = (f32[2,512]{1,0:T(2,128)S(1)}, f32[2,512]{1,0:T(2,128)}, u32[]{:S(2)}) copy-start(f32[2,512]{1,0:T(2,128)} %first.1) | copy-start | bytes 12292
  1.5 12.8 %copy-start.15 = (f32[22]{0:T(128)S(1)}, f32[22]{0:T(128)}, u32[]{:S(2)}) copy-start(f32[22]{0:T(128)} %scale.3) | copy-start | bytes 268
  1.5 10.5 %collective-permute-start = (bf16[4,48,704]{2,1,0:T(8,128)(2,1)S(1)}, bf16[4,48,704]{2,1,0:T(8,128)(2,1)S(1)}, u32[]{:S(2)}, u32[]{:S(2)}) collective-permute-start(bf16[4,48,704]{2,1,0:T(8,128)(2,1)S(1)} %get-tuple-element.28), channel_id=1, source_target_pairs={{0,2},{1,3},{2,4},{3,5},{4,6},{5,7},{6,0},{7,1},{8,10},{9,11},{10,... | collective-permute-start | bytes 811016 | tf_op jit(solution)/shard_map/ppermute | solution.py:475
  3.2 11.0 %collective-permute-start.1 = (bf16[4,48,704]{2,1,0:T(8,128)(2,1)S(1)}, bf16[4,48,704]{2,1,0:T(8,128)(2,1)S(1)}, u32[]{:S(2)}, u32[]{:S(2)}) collective-permute-start(bf16[4,48,704]{2,1,0:T(8,128)(2,1)S(1)} %get-tuple-element.29), channel_id=1, source_target_pairs={{4,2},{5,3},{6,4},{7,5},{8,6},{9,7},{10,0},{11,1},{12,10},{13,11},... | collective-permute-start | bytes 811016 | tf_op jit(solution)/shard_map/ppermute | solution.py:475
  7.1 27.4 %collective-permute-start.6 = (bf16[4,16,704]{2,1,0:T(8,128)(2,1)S(1)}, bf16[4,16,704]{2,1,0:T(8,128)(2,1)S(1)}, u32[]{:S(2)}, u32[]{:S(2)}) collective-permute-start(bf16[4,16,704]{2,1,0:T(8,128)(2,1)S(1)} %get-tuple-element.34), channel_id=1, source_target_pairs={{1,2},{2,3},{3,4},{0,5},{5,6},{6,7},{7,0},{4,1},{9,10},{10,11},{11... | collective-permute-start | bytes 270344 | tf_op jit(solution)/shard_map/ppermute | solution.py:475
  7.1 28.0 %collective-permute-start.7 = (bf16[4,16,704]{2,1,0:T(8,128)(2,1)S(1)}, bf16[4,16,704]{2,1,0:T(8,128)(2,1)S(1)}, u32[]{:S(2)}, u32[]{:S(2)}) collective-permute-start(bf16[4,16,704]{2,1,0:T(8,128)(2,1)S(1)} %get-tuple-element.35), channel_id=1, source_target_pairs={{5,2},{6,3},{7,4},{4,5},{9,6},{10,7},{11,0},{8,1},{13,10},{14,11},... | collective-permute-start | bytes 270344 | tf_op jit(solution)/shard_map/ppermute | solution.py:475
  8.0 12.0 %copy-start.3 = (bf16[2816,704]{0,1:T(8,128)(2,1)S(1)}, bf16[2816,704]{0,1:T(8,128)(2,1)}, u32[]{:S(2)}) copy-start(bf16[2816,704]{0,1:T(8,128)(2,1)} %param.23) | copy-start | bytes 11894788
  9.8 10.2 %copy-start.2 = (bf16[704,2816]{1,0:T(8,128)(2,1)S(1)}, bf16[704,2816]{1,0:T(8,128)(2,1)}, u32[]{:S(2)}) copy-start(bf16[704,2816]{1,0:T(8,128)(2,1)} %refs_8_.3) | copy-start | bytes 11894788
  9.8 10.1 %copy-start.4 = (bf16[704,704]{1,0:T(8,128)(2,1)S(1)}, bf16[704,704]{1,0:T(8,128)(2,1)}, u32[]{:S(2)}) copy-start(bf16[704,704]{1,0:T(8,128)(2,1)} %refs_7_.3) | copy-start | bytes 2973700
  9.8 10.1 %copy-start.7 = (f32[704]{0:T(1024)S(1)}, f32[704]{0:T(1024)}, u32[]{:S(2)}) copy-start(f32[704]{0:T(1024)} %refs_10_.1) | copy-start | bytes 8452
  9.9 10.1 %copy-start.8 = (f32[704]{0:T(1024)S(1)}, f32[704]{0:T(1024)}, u32[]{:S(2)}) copy-start(f32[704]{0:T(1024)} %refs_11_.1) | copy-start | bytes 8452
  14.2 1.9 %copy-start.10 = (bf16[704,2112]{1,0:T(8,128)(2,1)S(1)}, bf16[704,2112]{1,0:T(8,128)(2,1)}, u32[]{:S(2)}) copy-start(bf16[704,2112]{1,0:T(8,128)(2,1)} %refs_6_.3) | copy-start | bytes 8921092
  20.0 15.1 %copy-start.11 = (bf16[704,2112]{1,0:T(8,128)(2,1)S(1)}, bf16[704,2112]{1,0:T(8,128)(2,1)}, u32[]{:S(2)}) copy-start(bf16[704,2112]{1,0:T(8,128)(2,1)} %refs_6_.3) | copy-start | bytes 8921092
  24.9 22.7 %collective-permute-start.2 = (bf16[4,16,704]{2,1,0:T(8,128)(2,1)S(1)}, bf16[4,16,704]{2,1,0:T(8,128)(2,1)S(1)}, u32[]{:S(2)}, u32[]{:S(2)}) collective-permute-start(bf16[4,16,704]{2,1,0:T(8,128)(2,1)S(1)} %get-tuple-element.30), channel_id=1, source_target_pairs={{2,0},{3,1},{4,2},{5,3},{6,4},{7,5},{0,6},{1,7},{10,8},{11,9},{12,... | collective-permute-start | bytes 270344 | tf_op jit(solution)/shard_map/ppermute | solution.py:572
  27.7 19.9 %collective-permute-start.3 = (bf16[4,16,704]{2,1,0:T(8,128)(2,1)S(1)}, bf16[4,16,704]{2,1,0:T(8,128)(2,1)S(1)}, u32[]{:S(2)}, u32[]{:S(2)}) collective-permute-start(bf16[4,16,704]{2,1,0:T(8,128)(2,1)S(1)} %get-tuple-element.31), channel_id=1, source_target_pairs={{2,32},{3,33},{4,34},{5,35},{6,36},{7,37},{0,38},{1,39},{10,40},{1... | collective-permute-start | bytes 270344 | tf_op jit(solution)/shard_map/ppermute | solution.py:572
  29.1 18.5 %collective-permute-start.4 = (bf16[4,16,704]{2,1,0:T(8,128)(2,1)S(1)}, bf16[4,16,704]{2,1,0:T(8,128)(2,1)S(1)}, u32[]{:S(2)}, u32[]{:S(2)}) collective-permute-start(bf16[4,16,704]{2,1,0:T(8,128)(2,1)S(1)} %get-tuple-element.32), channel_id=1, source_target_pairs={{2,68},{3,69},{4,70},{5,71},{6,72},{7,73},{0,74},{1,75},{10,76},{1... | collective-permute-start | bytes 270344 | tf_op jit(solution)/shard_map/ppermute | solution.py:572
  34.4 15.2 %collective-permute-start.5 = (bf16[4,16,704]{2,1,0:T(8,128)(2,1)S(1)}, bf16[4,16,704]{2,1,0:T(8,128)(2,1)S(1)}, u32[]{:S(2)}, u32[]{:S(2)}) collective-permute-start(bf16[4,16,704]{2,1,0:T(8,128)(2,1)S(1)} %get-tuple-element.33), channel_id=1, source_target_pairs={{2,100},{3,101},{4,102},{5,103},{6,104},{7,105},{0,106},{1,107},{1... | collective-permute-start | bytes 270344 | tf_op jit(solution)/shard_map/ppermute | solution.py:572
  35.1 14.6 %copy-start = (bf16[704,2112]{1,0:T(8,128)(2,1)S(1)}, bf16[704,2112]{1,0:T(8,128)(2,1)}, u32[]{:S(2)}) copy-start(bf16[704,2112]{1,0:T(8,128)(2,1)} %refs_7_.5) | copy-start | bytes 8921092
  35.1 14.6 %copy-start.1 = (bf16[704,704]{1,0:T(8,128)(2,1)S(1)}, bf16[704,704]{1,0:T(8,128)(2,1)}, u32[]{:S(2)}) copy-start(bf16[704,704]{1,0:T(8,128)(2,1)} %refs_8_.5) | copy-start | bytes 2973700
  35.1 14.6 %copy-start.5 = (f32[16,704]{1,0:T(8,128)S(1)}, f32[16,704]{1,0:T(8,128)}, u32[]{:S(2)}) copy-start(f32[16,704]{1,0:T(8,128)} %refs_5_.3) | copy-start | bytes 135172
  35.1 14.6 %copy-start.6 = (f32[704]{0:T(1024)S(1)}, f32[704]{0:T(1024)}, u32[]{:S(2)}) copy-start(f32[704]{0:T(1024)} %refs_6_.5) | copy-start | bytes 8452
  35.1 14.6 %copy-start.9 = (s32[16]{0:T(128)S(1)}, s32[16]{0:T(128)}, u32[]{:S(2)}) copy-start(s32[16]{0:T(128)} %rank.3) | copy-start | bytes 196
  43.8 13.4 %collective-permute-start.11 = (bf16[4,16,704]{2,1,0:T(8,128)(2,1)S(1)}, bf16[4,16,704]{2,1,0:T(8,128)(2,1)S(1)}, u32[]{:S(2)}, u32[]{:S(2)}) collective-permute-start(bf16[4,16,704]{2,1,0:T(8,128)(2,1)S(1)} %get-tuple-element.42), channel_id=1, source_target_pairs={{2,0},{3,1},{4,2},{5,3},{6,4},{7,5},{0,6},{1,7},{10,8},{11,9},{12,... | collective-permute-start | bytes 270344 | tf_op jit(solution)/shard_map/ppermute | solution.py:572
  47.6 13.8 %collective-permute-start.12 = (bf16[4,16,704]{2,1,0:T(8,128)(2,1)S(1)}, bf16[4,16,704]{2,1,0:T(8,128)(2,1)S(1)}, u32[]{:S(2)}, u32[]{:S(2)}) collective-permute-start(bf16[4,16,704]{2,1,0:T(8,128)(2,1)S(1)} %get-tuple-element.43), channel_id=1, source_target_pairs={{2,33},{3,34},{4,35},{5,32},{6,37},{7,38},{0,39},{1,36},{10,41},{1... | collective-permute-start | bytes 270344 | tf_op jit(solution)/shard_map/ppermute | solution.py:572
  47.6 14.9 %collective-permute-start.13 = (bf16[4,16,704]{2,1,0:T(8,128)(2,1)S(1)}, bf16[4,16,704]{2,1,0:T(8,128)(2,1)S(1)}, u32[]{:S(2)}, u32[]{:S(2)}) collective-permute-start(bf16[4,16,704]{2,1,0:T(8,128)(2,1)S(1)} %get-tuple-element.44), channel_id=1, source_target_pairs={{2,68},{3,69},{4,70},{5,71},{6,72},{7,73},{0,74},{1,75},{10,76},{1... | collective-permute-start | bytes 270344 | tf_op jit(solution)/shard_map/ppermute | solution.py:572
  47.7 14.8 %collective-permute-start.14 = (bf16[4,16,704]{2,1,0:T(8,128)(2,1)S(1)}, bf16[4,16,704]{2,1,0:T(8,128)(2,1)S(1)}, u32[]{:S(2)}, u32[]{:S(2)}) collective-permute-start(bf16[4,16,704]{2,1,0:T(8,128)(2,1)S(1)} %get-tuple-element.45), channel_id=1, source_target_pairs={{2,101},{3,102},{4,103},{5,100},{6,105},{7,106},{0,107},{1,104},{1... | collective-permute-start | bytes 270344 | tf_op jit(solution)/shard_map/ppermute | solution.py:572
  53.5 15.0 %collective-permute-start.8 = (bf16[4,16,704]{2,1,0:T(8,128)(2,1)S(1)}, bf16[4,16,704]{2,1,0:T(8,128)(2,1)S(1)}, u32[]{:S(2)}, u32[]{:S(2)}) collective-permute-start(bf16[4,16,704]{2,1,0:T(8,128)(2,1)S(1)} %get-tuple-element.39), channel_id=1, source_target_pairs={{0,96},{32,0},{64,32},{96,64},{1,97},{33,1},{65,33},{97,65},{2,98}... | collective-permute-start | bytes 270344 | tf_op jit(solution)/shard_map/ppermute | solution.py:578
  57.2 12.3 %collective-permute-start.9 = (bf16[4,16,704]{2,1,0:T(8,128)(2,1)S(1)}, bf16[4,16,704]{2,1,0:T(8,128)(2,1)S(1)}, u32[]{:S(2)}, u32[]{:S(2)}) collective-permute-start(bf16[4,16,704]{2,1,0:T(8,128)(2,1)S(1)} %get-tuple-element.40), channel_id=1, source_target_pairs={{0,64},{32,96},{64,0},{96,32},{1,65},{33,97},{65,1},{97,33},{2,66}... | collective-permute-start | bytes 270344 | tf_op jit(solution)/shard_map/ppermute | solution.py:578
  61.4 8.1 %collective-permute-start.10 = (bf16[4,16,704]{2,1,0:T(8,128)(2,1)S(1)}, bf16[4,16,704]{2,1,0:T(8,128)(2,1)S(1)}, u32[]{:S(2)}, u32[]{:S(2)}) collective-permute-start(bf16[4,16,704]{2,1,0:T(8,128)(2,1)S(1)} %get-tuple-element.41), channel_id=1, source_target_pairs={{0,32},{32,64},{64,96},{96,0},{1,33},{33,65},{65,97},{97,1},{2,34}... | collective-permute-start | bytes 270344 | tf_op jit(solution)/shard_map/ppermute | solution.py:578
  66.3 5.4 %collective-permute-start.15 = (bf16[4,16,704]{2,1,0:T(8,128)(2,1)S(1)}, bf16[4,16,704]{2,1,0:T(8,128)(2,1)S(1)}, u32[]{:S(2)}, u32[]{:S(2)}) collective-permute-start(bf16[4,16,704]{2,1,0:T(8,128)(2,1)S(1)} %get-tuple-element.48), channel_id=1, source_target_pairs={{0,96},{32,0},{64,32},{96,64},{1,97},{33,1},{65,33},{97,65},{2,98}... | collective-permute-start | bytes 270344 | tf_op jit(solution)/shard_map/ppermute | solution.py:578
  68.5 6.2 %collective-permute-start.16 = (bf16[4,16,704]{2,1,0:T(8,128)(2,1)S(1)}, bf16[4,16,704]{2,1,0:T(8,128)(2,1)S(1)}, u32[]{:S(2)}, u32[]{:S(2)}) collective-permute-start(bf16[4,16,704]{2,1,0:T(8,128)(2,1)S(1)} %get-tuple-element.49), channel_id=1, source_target_pairs={{0,64},{32,96},{64,0},{96,32},{1,65},{33,97},{65,1},{97,33},{2,66}... | collective-permute-start | bytes 270344 | tf_op jit(solution)/shard_map/ppermute | solution.py:578
  68.5 6.9 %collective-permute-start.17 = (bf16[4,16,704]{2,1,0:T(8,128)(2,1)S(1)}, bf16[4,16,704]{2,1,0:T(8,128)(2,1)S(1)}, u32[]{:S(2)}, u32[]{:S(2)}) collective-permute-start(bf16[4,16,704]{2,1,0:T(8,128)(2,1)S(1)} %get-tuple-element.50), channel_id=1, source_target_pairs={{0,32},{32,64},{64,96},{96,0},{1,33},{33,65},{65,97},{97,1},{2,34}... | collective-permute-start | bytes 270344 | tf_op jit(solution)/shard_map/ppermute | solution.py:578

commit v2 on v1

--- a/solution.py
+++ b/solution.py
@@ -42,24 +42,8 @@
     return centred * lax.rsqrt(variance + 1e-05) * gain
 
 
-TAIL = (
-    3.309271834662358e-05,
-    -7.692189790236681e-04,
-    8.080714484816941e-03,
-    -5.3412101383958015e-02,
-    -4.587709752912628e-01,
-    -1.1512017013906806,
-    -9.999930610827096e-01,
-)
-
-
 def gelu(x):
-    size = jnp.abs(x)
-    a = jnp.minimum(size, 6.0)
-    power = TAIL[0]
-    for factor in TAIL[1:]:
-        power = power * a + factor
-    return jnp.maximum(x, 0.0) - size * jnp.exp2(power)
+    return 0.5 * x * (1.0 + lax.erf(x * math.sqrt(0.5)))
 
 
 def column_blocks(total, width):
@@ -131,7 +115,7 @@
             right[d] = jnp.concatenate([work[i, :SHIFT, :] for i in lines], axis=0).astype(BF16)
 
 
-def bias_kernel(first, second, out, table):
+def bias_kernel(first, second, _, out, table):
     units = first.shape[1]
     heads = second.shape[0]
     layer = jnp.concatenate([first[...], jnp.zeros((6, units), F32)], axis=0).T
@@ -247,7 +231,7 @@
 
 def settle(tokens, mixed_heads, lift, up, down, attention_gain, forward_gain):
     features = tokens.shape[1]
-    projected = dot_first(mixed_heads[...], lift[...])
+    projected = dot_first(mixed_heads, lift[...])
     gain = attention_gain[...].reshape(1, features)
     resid = (tokens.astype(F32) + layer_norm(projected, gain)).astype(BF16)
 
@@ -279,38 +263,41 @@
     attend(inner_tokens(low, high), last_row, None, scale, bias, qkv, mixed_heads, scratch)
 
 
-def inner_settle(place, low, high, mixed_heads, lift, up, down, gain, forward_gain, *outs):
-    *outs, token = outs
-    token[...] = jnp.zeros(token.shape, F32)
-    tokens = inner_tokens(low, high)
-    mixed = settle(tokens, mixed_heads, lift, up, down, gain, forward_gain)
-    narrow = mixed.astype(BF16).reshape(low.shape[0], 4, POSITIONS // 4, low.shape[2])
-    send_quarters([narrow[:, q] for q in range(4)], place, outs)
-
-
-def straddle_window(place, last_row, last_col, scale, *refs):
-    corners, _, bias, qkv, *refs = refs[:4], *refs[4:]
-    lift, up, down, attention_gain, forward_gain, *refs = refs
-    outs, token, scratch, mixed_heads, work = refs[:4], refs[4], refs[5:9], refs[9], refs[10]
-    token[...] = jnp.zeros(token.shape, F32)
+def straddle_attention(*refs):
+    corners, (_, last_row, last_col, scale, bias, qkv, mixed_heads) = refs[:4], refs[4:11]
+    *scratch, work = refs[11:]
     tokens = straddle_tokens(*corners, work)
     attend(tokens, last_row, last_col, scale, bias, qkv, mixed_heads, scratch)
-    work[...] = settle(tokens, mixed_heads, lift, up, down, attention_gain, forward_gain)
+
+
+def settle_all(place, *refs):
+    corners, (inner_heads, straddle_heads, *weights), refs = refs[:4], refs[4:11], refs[11:]
+    outs, token, work = refs[:4], refs[4], refs[5]
+    token[...] = jnp.zeros(token.shape, F32)
+    dates, _, features = corners[0].shape
     half = WINDOW // 2
+    inner_total = dates * POSITIONS
+    tokens = jnp.concatenate(
+        [inner_tokens(*corners[:2]), straddle_tokens(*corners, work)], axis=0
+    )
+    mixed_heads = jnp.concatenate([inner_heads[...], straddle_heads[...]], axis=1)
+    mixed = settle(tokens, mixed_heads, *weights)
+    work[...] = mixed[inner_total:]
+    narrow = mixed[:inner_total].astype(BF16).reshape(dates, 4, POSITIONS // 4, features)
     quarters = []
     for q in range(4):
         quarter = []
-        for d in range(corners[0].shape[0]):
+        for d in range(dates):
             lines = []
             for i in range(half):
                 base = d * POSITIONS + ((q // 2) * half + i) * WINDOW + (q % 2) * SHIFT
                 lines.append(work[base : base + SHIFT, :])
             quarter.append(jnp.concatenate(lines, axis=0).astype(BF16)[None])
-        quarters.append(jnp.concatenate(quarter, axis=0))
+        quarters.append(jnp.concatenate([narrow[:, q], jnp.concatenate(quarter, axis=0)], axis=1))
     send_quarters(quarters, place, outs)
 
 
-def time_kernel(size, place, rank, *refs):
+def time_kernel(size, pixel_start, place, rank, *refs):
     pieces, refs = refs[:4], refs[4:]
     _, embedding, time_gain, qkv, lift, *refs = refs
     outs, token, refs = refs[:4], refs[4], refs[5:]
@@ -318,7 +305,7 @@
     features = qkv.shape[0]
     heads = features // size
     z = place[0]
-    own, pixel_count, _ = pieces[0].shape
+    own, pixel_count, _ = outs[0].shape
     dates = 4 * own
     group = 128 // dates
     groups = pixel_count // group
@@ -328,7 +315,7 @@
     wide = []
     normed = []
     for k in range(4):
-        block = pieces[k][...].astype(F32)
+        block = pieces[k][:, pixel_start : pixel_start + pixel_count, :].astype(F32)
         source = (z + 4 - k) % 4
         lines = layer_norm(block, gain)
         for i in range(own):
@@ -450,7 +437,6 @@
     space = ("date", "row", "col")
     token_total = dates * POSITIONS
     part = POSITIONS // 4
-    date_axis = lax.axis_size("date")
     z = lax.axis_index("date")
     last_row, last_col = routes["last"](lax.axis_index("row"), lax.axis_index("col"))
     z = z.astype(jnp.int32).reshape(1)
@@ -478,12 +464,12 @@
     bias = call(
         bias_kernel,
         jax.ShapeDtypeStruct((heads, POSITIONS, PAIR), F32),
-        [VMEM, VMEM],
+        [VMEM] * 3,
         [pltpu.VMEM((WINDOW * 32, 128), F32)],
         10**9,
         10**6,
         "position_bias",
-    )(bias_network_first, bias_network_second.T)
+    )(bias_network_first, bias_network_second.T, window_query_key_value_weight)
 
     projected = [
         pltpu.VMEM((features, token_total), BF16),
@@ -503,53 +489,45 @@
     settle_flops = 2 * token_total * features * (features + 2 * hidden)
     attend_flops = 2 * token_total * features * 3 * features * 2
 
-    def inner_layer(low, high):
-        mixed_heads = call(
+    heads_shape = jax.ShapeDtypeStruct((features, token_total), BF16)
+    attention = (head_logit_scale, bias, window_query_key_value_weight)
+    work = pltpu.VMEM((token_total, features), F32)
+
+    def window_layer(low, high, *rights):
+        inner_heads = call(
             inner_attention,
-            jax.ShapeDtypeStruct((features, token_total), BF16),
+            heads_shape,
             [VMEM] * 2 + [SMEM] * 2 + [VMEM] * 2,
             projected[:4],
             attend_flops,
             4 * 10**6,
             "inner_attention",
             14,
-        )(low, high, last_row, head_logit_scale, bias, window_query_key_value_weight)
+        )(low, high, last_row, *attention)
+        straddle_heads = call(
+            straddle_attention,
+            heads_shape,
+            [VMEM] * 4 + [ANY] + [SMEM] * 3 + [VMEM] * 2,
+            projected[:4] + [work],
+            attend_flops,
+            4 * 10**6,
+            "straddle_attention",
+            14,
+        )(low, high, *rights, inner_heads, last_row, last_col, *attention)
         return call(
-            inner_settle,
-            [part_shape] * 4 + [token_shape],
-            [SMEM] + [VMEM] * 8,
-            [],
-            settle_flops,
+            settle_all,
+            [jax.ShapeDtypeStruct((dates, 2 * part, features), BF16)] * 4 + [token_shape],
+            [SMEM] + [VMEM] * 11,
+            [work],
+            2 * settle_flops,
             9 * 10**6,
-            "inner_settle",
-            20,
-        )(z, low, high, mixed_heads, *weights)
-
-    def straddle_layer(corners, token):
+            "settle",
+            28,
+        )(z, low, high, *rights, inner_heads, straddle_heads, *weights)
+
+    def time_layer(pixel_start, pieces, token):
         return call(
-            straddle_window,
-            [part_shape] * 4 + [token_shape],
-            [SMEM] * 4 + [VMEM] * 4 + [ANY] + [VMEM] * 7,
-            projected + [pltpu.VMEM((token_total, features), F32)],
-            attend_flops + settle_flops,
-            13 * 10**6,
-            "straddle_window",
-            24,
-        )(
-            z,
-            last_row,
-            last_col,
-            head_logit_scale,
-            *corners,
-            token,
-            bias,
-            window_query_key_value_weight,
-            *weights,
-        )
-
-    def time_layer(pieces, token):
-        return call(
-            functools.partial(time_kernel, features // heads),
+            functools.partial(time_kernel, features // heads, pixel_start),
             [part_shape] * 4 + [token_shape],
             [SMEM, SMEM] + [VMEM] * 4 + [ANY] + [VMEM] * 4,
             projected[:2] + projected[3:],
@@ -568,25 +546,15 @@
             temporal_output_weight,
         )
 
-    def to_dates(pieces, kind):
-        return [lax.ppermute(piece, space, routes[kind][k]) for k, piece in enumerate(pieces)]
-
-    def to_home(pieces):
-        return [
-            piece
-            if k == 0
-            else lax.ppermute(piece, "date", [(i, (i - k) % date_axis) for i in range(date_axis)])
-            for k, piece in enumerate(pieces)
-        ]
-
-    *inner, token = inner_layer(low, high)
-    inner = to_dates(inner, "inner")
-    *straddle, token = straddle_layer([low, high, low_right, high_right], token)
-    straddle = to_dates(straddle, "straddle")
-    *inner, token = time_layer(inner, token)
-    inner = to_home(inner)
-    *straddle, token = time_layer(straddle, token)
-    straddle = to_home(straddle)
+    def moved(pieces, kind):
+        return [lax.ppermute(piece, space, route) for piece, route in zip(pieces, routes[kind])]
+
+    *mixed, token = window_layer(low, high, low_right, high_right)
+    mixed = moved(mixed, "forward")
+    *inner, token = time_layer(0, mixed, token)
+    inner = inner[:1] + moved(inner[1:], "inner")
+    *straddle, token = time_layer(part, mixed, token)
+    straddle = moved(straddle, "straddle")
     return call(
         assemble,
         jax.ShapeDtypeStruct(pixels.shape, BF16),
@@ -619,14 +587,17 @@
     def route(down, right):
         return [(flat(r + down, c + right), flat(*place(r, c))) for r, c in tiles]
 
-    def forward(kind, k):
+    spots = [(z, r, c) for z in range(dates) for r, c in tiles]
+
+    def forward(k):
         pairs = []
-        for z in range(dates):
+        for z, r, c in spots:
             q = (z + k) % dates
-            right = q % 2 if kind == "straddle" else 0
-            for r, c in tiles:
-                pairs.append((spot(z, *place(r, c)), spot(q, r + q // 2, c + right)))
+            pairs.append((spot(z, *place(r, c)), spot(q, r + q // 2, c)))
         return pairs
+
+    def back(k, right):
+        return [(spot(z, r, c), spot(z - k, r, c + right * (z % 2))) for z, r, c in spots]
 
     def last(row, col):
         y = (row % high) * low + col // core
@@ -640,8 +611,9 @@
         "high": route(1, 0),
         "low_right": route(0, 1),
         "high_right": route(1, 1),
-        "inner": [forward("inner", k) for k in range(dates)],
-        "straddle": [forward("straddle", k) for k in range(dates)],
+        "forward": [forward(k) for k in range(dates)],
+        "inner": [back(k, 0) for k in range(1, dates)],
+        "straddle": [back(k, 1) for k in range(dates)],
         "last": last,
     }
 

time: 76.7 us -> 79.4 us (1.035); the launches traced: 76.5 us -> 77.8 us
  waiting for transfers between devices: 10.3 us -> 18.4 us
  starting transfers between devices: 34.6 us -> 28.4 us
  local copies, waits for them, and re-layouts: 3.08 us -> 1.36 us
  Pallas kernels: 28.3 us -> 29.4 us
    ppermute x14 -> x11, waiting for transfers between devices: 5.95 us -> 13.7 us  [moved(): lax.ppermute(piece, space, route)]
    ppermute x14 -> x11, starting transfers between devices: 28.1 us -> 22 us  [moved(): lax.ppermute(piece, space, route)]
    unnamed x32 -> x30, local copies, waits for them, and re-layouts: 3.08 us -> 1.36 us
  transfers between devices with their start and end apart: 18 -> 15, of which waited for: 5 -> 8; matrix products, arithmetic and copies ran while one was open for 0% -> 0% of each run, Pallas kernels for 35% -> 13%
where the time goes in v2:
time: 79.4 us; the launch traced here: 77.8 us
  Pallas kernels  29.4 us (37%)
  starting transfers between devices  28.4 us (36%)
  waiting for transfers between devices  18.4 us (23%)
  local copies, waits for them, and re-layouts  1.36 us (2%)
    ppermute x11, starting transfers between devices, moved(): lax.ppermute(piece, space, route)  22 us
    ppermute x11, waiting for transfers between devices, moved(): lax.ppermute(piece, space, route)  13.7 us
    pallas_call x1, Pallas kernels, window_layer(): call(settle_all, [jax.ShapeDtypeStruct((dates, 2 * part, features), BF16)...  8.86 us
    pallas_call x2, Pallas kernels, time_layer(): call(functools.partial(time_kernel, features // heads, pixel_start), [par...  7.63 us
    ppermute x4, starting transfers between devices, local(): lax.ppermute(piece, plane, routes[name])  6.43 us
    ppermute x4, waiting for transfers between devices, local(): lax.ppermute(piece, plane, routes[name])  4.7 us
    pallas_call x1, Pallas kernels, window_layer(): call(straddle_attention, heads_shape, [VMEM] * 4 + [ANY] + [SMEM] * 3 + [...  4.48 us
    pallas_call x1, Pallas kernels, window_layer(): call(inner_attention, heads_shape, [VMEM] * 2 + [SMEM] * 2 + [VMEM] * 2,...  4.43 us
  transfers between devices with their start and end apart: 15, of which 8 were waited for; matrix products, arithmetic and copies ran while one was open for 0% of the time, Pallas kernels for 13%

profile of v2, /device:TPU:0, one launch (start us, length us, event | category | flops | bytes accessed | tf_op | source)
XLA Modules:
  0.0 77.8 jit_solution(9199826733247357691)
XLA Ops:
  0.0 0.0 copy-start.2
  0.0 0.0 copy-start.4
  0.0 0.0 copy-start.11
  0.0 1.3 %copy-done.11 = bf16[4,8,16,704]{3,2,1,0:T(8,128)(2,1)S(1)} copy-done((bf16[4,8,16,704]{3,2,1,0:T(8,128)(2,1)S(1)}, bf16[4,8,16,704]{3,2,1,0:T(8,128)(2,1)}, u32[]{:S(2)}) %copy-start.11) | copy-done | bytes 720920
  1.3 1.1 %pack.1 = (bf16[4,48,704]{2,1,0:T(8,128)(2,1)}, bf16[4,48,704]{2,1,0:T(8,128)(2,1)}, bf16[4,16,704]{2,1,0:T(8,128)(2,1)}, bf16[4,16,704]{2,1,0:T(8,128)(2,1)}) custom-call(bf16[4,8,16,704]{3,2,1,0:T(8,128)(2,1)S(1)} %copy-done.11), custom_call_target="tpu_custom_call" | custom-call | flops 10000000000 | bytes 1441792 | tf_op jit(solution)/shard_map/pack/pallas_call | solution.py:451
  2.4 1.7 %collective-permute-start = (bf16[4,48,704]{2,1,0:T(8,128)(2,1)}, bf16[4,48,704]{2,1,0:T(8,128)(2,1)S(1)}, u32[]{:S(2)}, u32[]{:S(2)}) collective-permute-start(bf16[4,48,704]{2,1,0:T(8,128)(2,1)} %get-tuple-element.23), channel_id=1, source_target_pairs={{0,2},{1,3},{2,4},{3,5},{4,6},{5,7},{6,0},{7,1},{8,10},{9,11},{10,... | collective-permute-start | bytes 811016 | tf_op jit(solution)/shard_map/ppermute | solution.py:461
  4.0 3.9 %collective-permute-start.1 = (bf16[4,48,704]{2,1,0:T(8,128)(2,1)}, bf16[4,48,704]{2,1,0:T(8,128)(2,1)}, u32[]{:S(2)}, u32[]{:S(2)}) collective-permute-start(bf16[4,48,704]{2,1,0:T(8,128)(2,1)} %get-tuple-element.24), channel_id=1, source_target_pairs={{4,2},{5,3},{6,4},{7,5},{8,6},{9,7},{10,0},{11,1},{12,10},{13,11},... | collective-permute-start | bytes 811016 | tf_op jit(solution)/shard_map/ppermute | solution.py:461
  7.9 0.0 collective-permute-start.2
  7.9 0.9 %collective-permute-start.3 = (bf16[4,16,704]{2,1,0:T(8,128)(2,1)}, bf16[4,16,704]{2,1,0:T(8,128)(2,1)}, u32[]{:S(2)}, u32[]{:S(2)}) collective-permute-start(bf16[4,16,704]{2,1,0:T(8,128)(2,1)} %get-tuple-element.26), channel_id=1, source_target_pairs={{5,2},{6,3},{7,4},{4,5},{9,6},{10,7},{11,0},{8,1},{13,10},{14,11},... | collective-permute-start | bytes 270344 | tf_op jit(solution)/shard_map/ppermute | solution.py:461
  8.8 0.0 copy-done.2
  8.8 0.0 copy-done.4
  8.8 0.0 copy-done.6
  8.8 1.8 %position_bias.1.bias.refs_8_ = f32[22,64,128]{2,1,0:T(8,128)S(1)} custom-call(f32[2,512]{1,0:T(2,128)S(1)} %copy-done.6, f32[22,512]{1,0:T(8,128)S(1)} %bitcast.5, bf16[704,2112]{1,0:T(8,128)(2,1)S(1)} %copy-done.2), custom_call_target="tpu_custom_call" | custom-call | flops 1000000000 | bytes 1000000 | tf_op jit(solution)/shard_map/position_bias/pallas_call | solution.py:464
  10.7 2.4 %collective-permute-done.low.refs_0_ = bf16[4,48,704]{2,1,0:T(8,128)(2,1)S(1)} collective-permute-done((bf16[4,48,704]{2,1,0:T(8,128)(2,1)}, bf16[4,48,704]{2,1,0:T(8,128)(2,1)S(1)}, u32[]{:S(2)}, u32[]{:S(2)}) %collective-permute-start) | collective-permute-done | bytes 270368 | tf_op jit(solution)/shard_map/ppermute | solution.py:461
  13.0 2.3 %collective-permute-done.1.high.refs_1_ = bf16[4,48,704]{2,1,0:T(8,128)(2,1)} collective-permute-done((bf16[4,48,704]{2,1,0:T(8,128)(2,1)}, bf16[4,48,704]{2,1,0:T(8,128)(2,1)}, u32[]{:S(2)}, u32[]{:S(2)}) %collective-permute-start.1) | collective-permute-done | bytes 270368 | tf_op jit(solution)/shard_map/ppermute | solution.py:461
  15.3 0.0 copy-done.14
  15.4 4.4 %inner_attention.1.refs_4_ = bf16[704,256]{1,0:T(8,128)(2,1)S(1)} custom-call(bf16[4,48,704]{2,1,0:T(8,128)(2,1)S(1)} %collective-permute-done.low.refs_0_, bf16[4,48,704]{2,1,0:T(8,128)(2,1)} %collective-permute-done.1.high.refs_1_, s32[1]{0:T(128)} %bitcast.1.last_row.refs_5_, f32[22]{0:T(128)S(1)} %copy-done.14, ...), custom_call_target="tpu_custom_call" | custom-call | flops 1522532352 | bytes 4000000 | tf_op jit(solution)/shard_map/inner_attention/pallas_call | solution.py:497
  19.8 0.0 copy-start.10
  19.8 0.0 copy-start.12
  19.8 0.0 copy-start.13
  19.8 0.0 collective-permute-done.2.refs_2_
  19.8 0.0 collective-permute-done.3.refs_3_
  19.8 4.5 %straddle_attention.1.refs_5_ = bf16[704,256]{1,0:T(8,128)(2,1)S(1)} custom-call(bf16[4,48,704]{2,1,0:T(8,128)(2,1)S(1)} %collective-permute-done.low.refs_0_, bf16[4,48,704]{2,1,0:T(8,128)(2,1)} %collective-permute-done.1.high.refs_1_, bf16[4,16,704]{2,1,0:T(8,128)(2,1)S(1)} %collective-permute-done.2.refs_2_, ...), custom_call_target="tpu_custom_call" | custom-call | flops 1522532352 | bytes 4000000 | tf_op jit(solution)/shard_map/straddle_attention/pallas_call | solution.py:507
  24.3 0.0 copy-done.9
  24.3 0.0 copy-done.8
  24.3 0.0 copy-done.10
  24.4 0.0 copy-done.12
  24.4 0.0 copy-done.13
  24.4 0.0 copy-start
  24.4 0.0 copy-start.1
  24.4 0.0 copy-start.3
  24.4 0.0 copy-start.5
  24.4 0.0 copy-start.7
  24.4 8.9 %settle.1 = (bf16[4,32,704]{2,1,0:T(8,128)(2,1)S(1)}, bf16[4,32,704]{2,1,0:T(8,128)(2,1)S(1)}, bf16[4,32,704]{2,1,0:T(8,128)(2,1)S(1)}, bf16[4,32,704]{2,1,0:T(8,128)(2,1)S(1)}, f32[8,128]{1,0:T(8,128)S(1)}) custom-call(s32[1]{0:T(128)} %bitcast.place, bf16[4,48,704]{2,1,0:T(8,128)(2,1)S(1)} %collective-permute-done.low.refs_0_, ...), custom_call_target="tpu_custom_call" | custom-call | flops 4567597056 | bytes 9000000 | tf_op jit(solution)/shard_map/settle/pallas_call | solution.py:517
  33.3 2.8 %collective-permute-start.4 = (bf16[4,32,704]{2,1,0:T(8,128)(2,1)S(1)}, bf16[4,32,704]{2,1,0:T(8,128)(2,1)S(1)}, u32[]{:S(2)}, u32[]{:S(2)}) collective-permute-start(bf16[4,32,704]{2,1,0:T(8,128)(2,1)S(1)} %get-tuple-element.27), channel_id=1, source_target_pairs={{2,0},{3,1},{4,2},{5,3},{6,4},{7,5},{0,6},{1,7},{10,8},{11,9},{12,... | collective-permute-start | bytes 540680 | tf_op jit(solution)/shard_map/ppermute | solution.py:550
  36.1 1.4 %collective-permute-start.5 = (bf16[4,32,704]{2,1,0:T(8,128)(2,1)S(1)}, bf16[4,32,704]{2,1,0:T(8,128)(2,1)S(1)}, u32[]{:S(2)}, u32[]{:S(2)}) collective-permute-start(bf16[4,32,704]{2,1,0:T(8,128)(2,1)S(1)} %get-tuple-element.28), channel_id=1, source_target_pairs={{2,32},{3,33},{4,34},{5,35},{6,36},{7,37},{0,38},{1,39},{10,40},{1... | collective-permute-start | bytes 540680 | tf_op jit(solution)/shard_map/ppermute | solution.py:550
  37.5 5.3 %collective-permute-start.6 = (bf16[4,32,704]{2,1,0:T(8,128)(2,1)S(1)}, bf16[4,32,704]{2,1,0:T(8,128)(2,1)S(1)}, u32[]{:S(2)}, u32[]{:S(2)}) collective-permute-start(bf16[4,32,704]{2,1,0:T(8,128)(2,1)S(1)} %get-tuple-element.29), channel_id=1, source_target_pairs={{2,68},{3,69},{4,70},{5,71},{6,72},{7,73},{0,74},{1,75},{10,76},{1... | collective-permute-start | bytes 540680 | tf_op jit(solution)/shard_map/ppermute | solution.py:550
  42.8 0.7 collective-permute-start.7
  43.5 0.0 collective-permute-done.4.refs_0_
  43.5 1.2 %collective-permute-done.5.refs_1_ = bf16[4,32,704]{2,1,0:T(8,128)(2,1)S(1)} collective-permute-done((bf16[4,32,704]{2,1,0:T(8,128)(2,1)S(1)}, bf16[4,32,704]{2,1,0:T(8,128)(2,1)S(1)}, u32[]{:S(2)}, u32[]{:S(2)}) %collective-permute-start.5) | collective-permute-done | bytes 180256 | tf_op jit(solution)/shard_map/ppermute | solution.py:550
  44.7 2.7 %collective-permute-done.6.refs_2_ = bf16[4,32,704]{2,1,0:T(8,128)(2,1)S(1)} collective-permute-done((bf16[4,32,704]{2,1,0:T(8,128)(2,1)S(1)}, bf16[4,32,704]{2,1,0:T(8,128)(2,1)S(1)}, u32[]{:S(2)}, u32[]{:S(2)}) %collective-permute-start.6) | collective-permute-done | bytes 180256 | tf_op jit(solution)/shard_map/ppermute | solution.py:550
  47.4 3.5 %collective-permute-done.7.refs_3_ = bf16[4,32,704]{2,1,0:T(8,128)(2,1)S(1)} collective-permute-done((bf16[4,32,704]{2,1,0:T(8,128)(2,1)S(1)}, bf16[4,32,704]{2,1,0:T(8,128)(2,1)S(1)}, u32[]{:S(2)}, u32[]{:S(2)}) %collective-permute-start.7) | collective-permute-done | bytes 180256 | tf_op jit(solution)/shard_map/ppermute | solution.py:550
  50.9 0.0 copy-done
  50.9 0.0 copy-done.1
  50.9 0.0 copy-done.3
  50.9 0.0 copy-done.5
  50.9 0.0 copy-done.7
  50.9 3.8 %time_layer.2 = (bf16[4,16,704]{2,1,0:T(8,128)(2,1)S(1)}, bf16[4,16,704]{2,1,0:T(8,128)(2,1)S(1)}, bf16[4,16,704]{2,1,0:T(8,128)(2,1)S(1)}, bf16[4,16,704]{2,1,0:T(8,128)(2,1)S(1)}, f32[8,128]{1,0:T(8,128)S(1)}) custom-call(s32[1]{0:T(128)} %bitcast.place, s32[16]{0:T(128)S(1)} %copy-done.7, bf16[4,32,704]{2,1,0:T(8,128)(2,1)S(1)} %collective-permute-done.4.refs_0_, ...), custom_call_target="tpu_custom_call" | custom-call | flops 1015021568 | bytes 5000000 | tf_op jit(solution)/shard_map/time_layer/pallas_call | solution.py:529
  54.7 4.3 %collective-permute-start.8 = (bf16[4,16,704]{2,1,0:T(8,128)(2,1)S(1)}, bf16[4,16,704]{2,1,0:T(8,128)(2,1)S(1)}, u32[]{:S(2)}, u32[]{:S(2)}) collective-permute-start(bf16[4,16,704]{2,1,0:T(8,128)(2,1)S(1)} %get-tuple-element.33), channel_id=1, source_target_pairs={{0,96},{1,97},{2,98},{3,99},{4,100},{5,101},{6,102},{7,103},{8,104... | collective-permute-start | bytes 270344 | tf_op jit(solution)/shard_map/ppermute | solution.py:550
  59.0 0.0 collective-permute-start.9
  59.0 0.9 %collective-permute-start.10 = (bf16[4,16,704]{2,1,0:T(8,128)(2,1)S(1)}, bf16[4,16,704]{2,1,0:T(8,128)(2,1)S(1)}, u32[]{:S(2)}, u32[]{:S(2)}) collective-permute-start(bf16[4,16,704]{2,1,0:T(8,128)(2,1)S(1)} %get-tuple-element.35), channel_id=1, source_target_pairs={{0,32},{1,33},{2,34},{3,35},{4,36},{5,37},{6,38},{7,39},{8,40},{9,... | collective-permute-start | bytes 270344 | tf_op jit(solution)/shard_map/ppermute | solution.py:550
  60.0 3.8 %time_layer.3 = (bf16[4,16,704]{2,1,0:T(8,128)(2,1)S(1)}, bf16[4,16,704]{2,1,0:T(8,128)(2,1)S(1)}, bf16[4,16,704]{2,1,0:T(8,128)(2,1)S(1)}, bf16[4,16,704]{2,1,0:T(8,128)(2,1)S(1)}, f32[8,128]{1,0:T(8,128)}) custom-call(s32[1]{0:T(128)} %bitcast.place, s32[16]{0:T(128)S(1)} %copy-done.7, bf16[4,32,704]{2,1,0:T(8,128)(2,1)S(1)} %collective-permute-done.4.refs_0_, ...), custom_call_target="tpu_custom_call" | custom-call | flops 1015021568 | bytes 5000000 | tf_op jit(solution)/shard_map/time_layer/pallas_call | solution.py:529
  63.8 0.7 collective-permute-start.11
  64.5 3.6 %collective-permute-start.12 = (bf16[4,16,704]{2,1,0:T(8,128)(2,1)S(1)}, bf16[4,16,704]{2,1,0:T(8,128)(2,1)S(1)}, u32[]{:S(2)}, u32[]{:S(2)}) collective-permute-start(bf16[4,16,704]{2,1,0:T(8,128)(2,1)S(1)} %get-tuple-element.38), channel_id=1, source_target_pairs={{0,96},{1,97},{2,98},{3,99},{4,100},{5,101},{6,102},{7,103},{8,104... | collective-permute-start | bytes 270344 | tf_op jit(solution)/shard_map/ppermute | solution.py:550
  68.1 0.0 collective-permute-done.8.refs_1_
  68.1 2.3 %collective-permute-start.13 = (bf16[4,16,704]{2,1,0:T(8,128)(2,1)S(1)}, bf16[4,16,704]{2,1,0:T(8,128)(2,1)S(1)}, u32[]{:S(2)}, u32[]{:S(2)}) collective-permute-start(bf16[4,16,704]{2,1,0:T(8,128)(2,1)S(1)} %get-tuple-element.39), channel_id=1, source_target_pairs={{0,64},{1,65},{2,66},{3,67},{4,68},{5,69},{6,70},{7,71},{8,72},{9,... | collective-permute-start | bytes 270344 | tf_op jit(solution)/shard_map/ppermute | solution.py:550
  70.4 0.0 collective-permute-done.9.refs_2_
  70.4 0.0 collective-permute-start.14
  70.4 0.0 collective-permute-done.10.refs_3_
  70.4 0.0 collective-permute-done.11.refs_4_
  70.4 2.4 %collective-permute-done.12.refs_5_ = bf16[4,16,704]{2,1,0:T(8,128)(2,1)S(1)} collective-permute-done((bf16[4,16,704]{2,1,0:T(8,128)(2,1)S(1)}, bf16[4,16,704]{2,1,0:T(8,128)(2,1)S(1)}, u32[]{:S(2)}, u32[]{:S(2)}) %collective-permute-start.12) | collective-permute-done | bytes 90144 | tf_op jit(solution)/shard_map/ppermute | solution.py:550
  72.9 2.4 %collective-permute-done.13.refs_6_ = bf16[4,16,704]{2,1,0:T(8,128)(2,1)S(1)} collective-permute-done((bf16[4,16,704]{2,1,0:T(8,128)(2,1)S(1)}, bf16[4,16,704]{2,1,0:T(8,128)(2,1)S(1)}, u32[]{:S(2)}, u32[]{:S(2)}) %collective-permute-start.13) | collective-permute-done | bytes 90144 | tf_op jit(solution)/shard_map/ppermute | solution.py:550
  75.3 1.4 %collective-permute-done.14.refs_7_ = bf16[4,16,704]{2,1,0:T(8,128)(2,1)S(1)} collective-permute-done((bf16[4,16,704]{2,1,0:T(8,128)(2,1)S(1)}, bf16[4,16,704]{2,1,0:T(8,128)(2,1)S(1)}, u32[]{:S(2)}, u32[]{:S(2)}) %collective-permute-start.14) | collective-permute-done | bytes 90144 | tf_op jit(solution)/shard_map/ppermute | solution.py:550
  76.7 1.1 %assemble.1 = bf16[4,8,16,704]{3,2,1,0:T(8,128)(2,1)} custom-call(s32[1]{0:T(128)} %bitcast.place, bf16[4,16,704]{2,1,0:T(8,128)(2,1)S(1)} %get-tuple-element.32.refs_0_, bf16[4,16,704]{2,1,0:T(8,128)(2,1)S(1)} %collective-permute-done.8.refs_1_, bf16[4,16,704]{2,1,0:T(8,128)(2,1)S(1)} %collective-permute-done.9.refs_2_, ...), custom_call_target="tpu_custom_call" | custom-call | bytes 1441792 | tf_op jit(solution)/shard_map/assemble/pallas_call | solution.py:558
  (4 shorter events, 0.0 us)
Async XLA Ops:
  0.0 8.8 %copy-start.2 = (bf16[704,2112]{1,0:T(8,128)(2,1)S(1)}, bf16[704,2112]{1,0:T(8,128)(2,1)}, u32[]{:S(2)}) copy-start(bf16[704,2112]{1,0:T(8,128)(2,1)} %refs_9_.2) | copy-start | bytes 8921092
  0.0 8.8 %copy-start.4 = (f32[512,22]{0,1:T(8,128)S(1)}, f32[512,22]{0,1:T(8,128)}, u32[]{:S(2)}) copy-start(f32[512,22]{0,1:T(8,128)} %param.19) | copy-start | bytes 135172
  0.0 8.8 %copy-start.6 = (f32[2,512]{1,0:T(2,128)S(1)}, f32[2,512]{1,0:T(2,128)}, u32[]{:S(2)}) copy-start(f32[2,512]{1,0:T(2,128)} %first.1) | copy-start | bytes 12292
  0.0 1.3 %copy-start.11 = (bf16[4,8,16,704]{3,2,1,0:T(8,128)(2,1)S(1)}, bf16[4,8,16,704]{3,2,1,0:T(8,128)(2,1)}, u32[]{:S(2)}) copy-start(bf16[4,8,16,704]{3,2,1,0:T(8,128)(2,1)} %pixels.1) | copy-start | bytes 2162692
  2.4 13.0 %copy-start.14 = (f32[22]{0:T(128)S(1)}, f32[22]{0:T(128)}, u32[]{:S(2)}) copy-start(f32[22]{0:T(128)} %refs_7_.4) | copy-start | bytes 268
  2.4 10.6 %collective-permute-start = (bf16[4,48,704]{2,1,0:T(8,128)(2,1)}, bf16[4,48,704]{2,1,0:T(8,128)(2,1)S(1)}, u32[]{:S(2)}, u32[]{:S(2)}) collective-permute-start(bf16[4,48,704]{2,1,0:T(8,128)(2,1)} %get-tuple-element.23), channel_id=1, source_target_pairs={{0,2},{1,3},{2,4},{3,5},{4,6},{5,7},{6,0},{7,1},{8,10},{9,11},{10,... | collective-permute-start | bytes 811016 | tf_op jit(solution)/shard_map/ppermute | solution.py:461
  4.0 11.3 %collective-permute-start.1 = (bf16[4,48,704]{2,1,0:T(8,128)(2,1)}, bf16[4,48,704]{2,1,0:T(8,128)(2,1)}, u32[]{:S(2)}, u32[]{:S(2)}) collective-permute-start(bf16[4,48,704]{2,1,0:T(8,128)(2,1)} %get-tuple-element.24), channel_id=1, source_target_pairs={{4,2},{5,3},{6,4},{7,5},{8,6},{9,7},{10,0},{11,1},{12,10},{13,11},... | collective-permute-start | bytes 811016 | tf_op jit(solution)/shard_map/ppermute | solution.py:461
  7.9 11.9 %collective-permute-start.2 = (bf16[4,16,704]{2,1,0:T(8,128)(2,1)}, bf16[4,16,704]{2,1,0:T(8,128)(2,1)S(1)}, u32[]{:S(2)}, u32[]{:S(2)}) collective-permute-start(bf16[4,16,704]{2,1,0:T(8,128)(2,1)} %get-tuple-element.25), channel_id=1, source_target_pairs={{1,2},{2,3},{3,4},{0,5},{5,6},{6,7},{7,0},{4,1},{9,10},{10,11},{11... | collective-permute-start | bytes 270344 | tf_op jit(solution)/shard_map/ppermute | solution.py:461
  7.9 11.9 %collective-permute-start.3 = (bf16[4,16,704]{2,1,0:T(8,128)(2,1)}, bf16[4,16,704]{2,1,0:T(8,128)(2,1)}, u32[]{:S(2)}, u32[]{:S(2)}) collective-permute-start(bf16[4,16,704]{2,1,0:T(8,128)(2,1)} %get-tuple-element.26), channel_id=1, source_target_pairs={{5,2},{6,3},{7,4},{4,5},{9,6},{10,7},{11,0},{8,1},{13,10},{14,11},... | collective-permute-start | bytes 270344 | tf_op jit(solution)/shard_map/ppermute | solution.py:461
  15.4 9.0 %copy-start.9 = (bf16[2816,704]{0,1:T(8,128)(2,1)S(1)}, bf16[2816,704]{0,1:T(8,128)(2,1)}, u32[]{:S(2)}) copy-start(bf16[2816,704]{0,1:T(8,128)(2,1)} %param.23) | copy-start | bytes 11894788
  19.8 4.6 %copy-start.8 = (bf16[704,2816]{1,0:T(8,128)(2,1)S(1)}, bf16[704,2816]{1,0:T(8,128)(2,1)}, u32[]{:S(2)}) copy-start(bf16[704,2816]{1,0:T(8,128)(2,1)} %refs_7_.5) | copy-start | bytes 11894788
  19.8 4.6 %copy-start.10 = (bf16[704,704]{1,0:T(8,128)(2,1)S(1)}, bf16[704,704]{1,0:T(8,128)(2,1)}, u32[]{:S(2)}) copy-start(bf16[704,704]{1,0:T(8,128)(2,1)} %refs_6_.3) | copy-start | bytes 2973700
  19.8 4.6 %copy-start.12 = (f32[704]{0:T(1024)S(1)}, f32[704]{0:T(1024)}, u32[]{:S(2)}) copy-start(f32[704]{0:T(1024)} %refs_9_.3) | copy-start | bytes 8452
  19.8 4.6 %copy-start.13 = (f32[704]{0:T(1024)S(1)}, f32[704]{0:T(1024)}, u32[]{:S(2)}) copy-start(f32[704]{0:T(1024)} %refs_10_.1) | copy-start | bytes 8452
  24.4 26.5 %copy-start = (bf16[704,2112]{1,0:T(8,128)(2,1)S(1)}, bf16[704,2112]{1,0:T(8,128)(2,1)}, u32[]{:S(2)}) copy-start(bf16[704,2112]{1,0:T(8,128)(2,1)} %refs_7_.7) | copy-start | bytes 8921092
  24.4 26.5 %copy-start.1 = (bf16[704,704]{1,0:T(8,128)(2,1)S(1)}, bf16[704,704]{1,0:T(8,128)(2,1)}, u32[]{:S(2)}) copy-start(bf16[704,704]{1,0:T(8,128)(2,1)} %refs_8_.3) | copy-start | bytes 2973700
  24.4 26.5 %copy-start.3 = (f32[16,704]{1,0:T(8,128)S(1)}, f32[16,704]{1,0:T(8,128)}, u32[]{:S(2)}) copy-start(f32[16,704]{1,0:T(8,128)} %refs_5_.3) | copy-start | bytes 135172
  24.4 26.5 %copy-start.5 = (f32[704]{0:T(1024)S(1)}, f32[704]{0:T(1024)}, u32[]{:S(2)}) copy-start(f32[704]{0:T(1024)} %refs_6_.5) | copy-start | bytes 8452
  24.4 26.5 %copy-start.7 = (s32[16]{0:T(128)S(1)}, s32[16]{0:T(128)}, u32[]{:S(2)}) copy-start(s32[16]{0:T(128)} %rank.3) | copy-start | bytes 196
  33.3 10.2 %collective-permute-start.4 = (bf16[4,32,704]{2,1,0:T(8,128)(2,1)S(1)}, bf16[4,32,704]{2,1,0:T(8,128)(2,1)S(1)}, u32[]{:S(2)}, u32[]{:S(2)}) collective-permute-start(bf16[4,32,704]{2,1,0:T(8,128)(2,1)S(1)} %get-tuple-element.27), channel_id=1, source_target_pairs={{2,0},{3,1},{4,2},{5,3},{6,4},{7,5},{0,6},{1,7},{10,8},{11,9},{12,... | collective-permute-start | bytes 540680 | tf_op jit(solution)/shard_map/ppermute | solution.py:550
  36.1 8.6 %collective-permute-start.5 = (bf16[4,32,704]{2,1,0:T(8,128)(2,1)S(1)}, bf16[4,32,704]{2,1,0:T(8,128)(2,1)S(1)}, u32[]{:S(2)}, u32[]{:S(2)}) collective-permute-start(bf16[4,32,704]{2,1,0:T(8,128)(2,1)S(1)} %get-tuple-element.28), channel_id=1, source_target_pairs={{2,32},{3,33},{4,34},{5,35},{6,36},{7,37},{0,38},{1,39},{10,40},{1... | collective-permute-start | bytes 540680 | tf_op jit(solution)/shard_map/ppermute | solution.py:550
  37.5 9.9 %collective-permute-start.6 = (bf16[4,32,704]{2,1,0:T(8,128)(2,1)S(1)}, bf16[4,32,704]{2,1,0:T(8,128)(2,1)S(1)}, u32[]{:S(2)}, u32[]{:S(2)}) collective-permute-start(bf16[4,32,704]{2,1,0:T(8,128)(2,1)S(1)} %get-tuple-element.29), channel_id=1, source_target_pairs={{2,68},{3,69},{4,70},{5,71},{6,72},{7,73},{0,74},{1,75},{10,76},{1... | collective-permute-start | bytes 540680 | tf_op jit(solution)/shard_map/ppermute | solution.py:550
  42.8 8.1 %collective-permute-start.7 = (bf16[4,32,704]{2,1,0:T(8,128)(2,1)S(1)}, bf16[4,32,704]{2,1,0:T(8,128)(2,1)S(1)}, u32[]{:S(2)}, u32[]{:S(2)}) collective-permute-start(bf16[4,32,704]{2,1,0:T(8,128)(2,1)S(1)} %get-tuple-element.30), channel_id=1, source_target_pairs={{2,100},{3,101},{4,102},{5,103},{6,104},{7,105},{0,106},{1,107},{1... | collective-permute-start | bytes 540680 | tf_op jit(solution)/shard_map/ppermute | solution.py:550
  54.7 13.3 %collective-permute-start.8 = (bf16[4,16,704]{2,1,0:T(8,128)(2,1)S(1)}, bf16[4,16,704]{2,1,0:T(8,128)(2,1)S(1)}, u32[]{:S(2)}, u32[]{:S(2)}) collective-permute-start(bf16[4,16,704]{2,1,0:T(8,128)(2,1)S(1)} %get-tuple-element.33), channel_id=1, source_target_pairs={{0,96},{1,97},{2,98},{3,99},{4,100},{5,101},{6,102},{7,103},{8,104... | collective-permute-start | bytes 270344 | tf_op jit(solution)/shard_map/ppermute | solution.py:550
  59.0 11.4 %collective-permute-start.9 = (bf16[4,16,704]{2,1,0:T(8,128)(2,1)S(1)}, bf16[4,16,704]{2,1,0:T(8,128)(2,1)S(1)}, u32[]{:S(2)}, u32[]{:S(2)}) collective-permute-start(bf16[4,16,704]{2,1,0:T(8,128)(2,1)S(1)} %get-tuple-element.34), channel_id=1, source_target_pairs={{0,64},{1,65},{2,66},{3,67},{4,68},{5,69},{6,70},{7,71},{8,72},{9,... | collective-permute-start | bytes 270344 | tf_op jit(solution)/shard_map/ppermute | solution.py:550
  59.0 11.4 %collective-permute-start.10 = (bf16[4,16,704]{2,1,0:T(8,128)(2,1)S(1)}, bf16[4,16,704]{2,1,0:T(8,128)(2,1)S(1)}, u32[]{:S(2)}, u32[]{:S(2)}) collective-permute-start(bf16[4,16,704]{2,1,0:T(8,128)(2,1)S(1)} %get-tuple-element.35), channel_id=1, source_target_pairs={{0,32},{1,33},{2,34},{3,35},{4,36},{5,37},{6,38},{7,39},{8,40},{9,... | collective-permute-start | bytes 270344 | tf_op jit(solution)/shard_map/ppermute | solution.py:550
  63.8 6.6 %collective-permute-start.11 = (bf16[4,16,704]{2,1,0:T(8,128)(2,1)S(1)}, bf16[4,16,704]{2,1,0:T(8,128)(2,1)S(1)}, u32[]{:S(2)}, u32[]{:S(2)}) collective-permute-start(bf16[4,16,704]{2,1,0:T(8,128)(2,1)S(1)} %get-tuple-element.37), channel_id=1, source_target_pairs={{0,0},{1,1},{2,2},{3,3},{4,4},{5,5},{6,6},{7,7},{8,8},{9,9},{10,10... | collective-permute-start | bytes 270344 | tf_op jit(solution)/shard_map/ppermute | solution.py:550
  64.5 8.4 %collective-permute-start.12 = (bf16[4,16,704]{2,1,0:T(8,128)(2,1)S(1)}, bf16[4,16,704]{2,1,0:T(8,128)(2,1)S(1)}, u32[]{:S(2)}, u32[]{:S(2)}) collective-permute-start(bf16[4,16,704]{2,1,0:T(8,128)(2,1)S(1)} %get-tuple-element.38), channel_id=1, source_target_pairs={{0,96},{1,97},{2,98},{3,99},{4,100},{5,101},{6,102},{7,103},{8,104... | collective-permute-start | bytes 270344 | tf_op jit(solution)/shard_map/ppermute | solution.py:550
  68.1 7.2 %collective-permute-start.13 = (bf16[4,16,704]{2,1,0:T(8,128)(2,1)S(1)}, bf16[4,16,704]{2,1,0:T(8,128)(2,1)S(1)}, u32[]{:S(2)}, u32[]{:S(2)}) collective-permute-start(bf16[4,16,704]{2,1,0:T(8,128)(2,1)S(1)} %get-tuple-element.39), channel_id=1, source_target_pairs={{0,64},{1,65},{2,66},{3,67},{4,68},{5,69},{6,70},{7,71},{8,72},{9,... | collective-permute-start | bytes 270344 | tf_op jit(solution)/shard_map/ppermute | solution.py:550
  70.4 6.3 %collective-permute-start.14 = (bf16[4,16,704]{2,1,0:T(8,128)(2,1)S(1)}, bf16[4,16,704]{2,1,0:T(8,128)(2,1)S(1)}, u32[]{:S(2)}, u32[]{:S(2)}) collective-permute-start(bf16[4,16,704]{2,1,0:T(8,128)(2,1)S(1)} %get-tuple-element.40), channel_id=1, source_target_pairs={{0,32},{1,33},{2,34},{3,35},{4,36},{5,37},{6,38},{7,39},{8,40},{9,... | collective-permute-start | bytes 270344 | tf_op jit(solution)/shard_map/ppermute | solution.py:550

commit v3 on v1

--- a/solution.py
+++ b/solution.py
@@ -42,24 +42,8 @@
     return centred * lax.rsqrt(variance + 1e-05) * gain
 
 
-TAIL = (
-    3.309271834662358e-05,
-    -7.692189790236681e-04,
-    8.080714484816941e-03,
-    -5.3412101383958015e-02,
-    -4.587709752912628e-01,
-    -1.1512017013906806,
-    -9.999930610827096e-01,
-)
-
-
 def gelu(x):
-    size = jnp.abs(x)
-    a = jnp.minimum(size, 6.0)
-    power = TAIL[0]
-    for factor in TAIL[1:]:
-        power = power * a + factor
-    return jnp.maximum(x, 0.0) - size * jnp.exp2(power)
+    return 0.5 * x * (1.0 + lax.erf(x * math.sqrt(0.5)))
 
 
 def column_blocks(total, width):
@@ -131,7 +115,7 @@
             right[d] = jnp.concatenate([work[i, :SHIFT, :] for i in lines], axis=0).astype(BF16)
 
 
-def bias_kernel(first, second, out, table):
+def bias_kernel(first, second, _, out, table):
     units = first.shape[1]
     heads = second.shape[0]
     layer = jnp.concatenate([first[...], jnp.zeros((6, units), F32)], axis=0).T
@@ -251,17 +235,23 @@
     gain = attention_gain[...].reshape(1, features)
     resid = (tokens.astype(F32) + layer_norm(projected, gain)).astype(BF16)
 
-    parts = []
+    total = up.shape[1]
+    raised, parts = [], []
 
     def raise_block(span):
         return dot(resid, up[:, slice(*span)])
 
-    def lower_block(span, raised):
-        parts.append(dot_last(gelu(raised).astype(BF16), down[:, slice(*span)]))
-        if len(parts) > 1:
-            parts[:] = [parts[0] + parts[1]]
-
-    staggered(column_blocks(up.shape[1], 512), raise_block, lower_block)
+    def lower_block(span, block):
+        raised.append(gelu(block).astype(BF16))
+        if len(raised) == 2 or span[1] == total:
+            start = span[1] - 256 * len(raised)
+            hidden = jnp.concatenate(raised, axis=1)
+            parts.append(dot_last(hidden, down[:, start : span[1]]))
+            raised.clear()
+            if len(parts) > 1:
+                parts[:] = [parts[0] + parts[1]]
+
+    staggered(column_blocks(total, 256), raise_block, lower_block)
     (lowered,) = parts
     return resid.astype(F32) + layer_norm(lowered, forward_gain[...].reshape(1, features))
 
@@ -470,6 +460,7 @@
         10**10,
         tile_bytes * 2,
         "pack",
+        4,
     )(pixels)
     low, high, low_right, high_right = (
         lax.ppermute(piece, plane, routes[name])
@@ -478,12 +469,13 @@
     bias = call(
         bias_kernel,
         jax.ShapeDtypeStruct((heads, POSITIONS, PAIR), F32),
-        [VMEM, VMEM],
+        [VMEM] * 3,
         [pltpu.VMEM((WINDOW * 32, 128), F32)],
         10**9,
         10**6,
         "position_bias",
-    )(bias_network_first, bias_network_second.T)
+        6,
+    )(bias_network_first, bias_network_second.T, window_query_key_value_weight)
 
     projected = [
         pltpu.VMEM((features, token_total), BF16),

time: 76.7 us -> 75.9 us (0.990)
  local copies, waits for them, and re-layouts: 3.08 us -> 1.35 us
    unnamed x32 -> x30, local copies, waits for them, and re-layouts: 3.08 us -> 1.35 us
where the time goes in v3:
time: 75.9 us; the launch traced here: 75.7 us
  starting transfers between devices  34.4 us (45%)
  Pallas kernels  29 us (38%)
  waiting for transfers between devices  10.8 us (14%)
  local copies, waits for them, and re-layouts  1.35 us (2%)
    ppermute x8, starting transfers between devices, to_dates(): lax.ppermute(piece, space, routes[kind][k])  16 us
    ppermute x6, starting transfers between devices, to_home(): lax.ppermute(piece, 'date', [(i, (i - k) % date_axis) for i in range(date...  12 us
    pallas_call x1, Pallas kernels, straddle_layer(): call(straddle_window, [part_shape] * 4 + [token_shape], [SMEM] * 4 + [VME...  8.43 us
    pallas_call x2, Pallas kernels, time_layer(): call(functools.partial(time_kernel, features // heads), [part_shape] * 4...  7.62 us
    ppermute x4, starting transfers between devices, local(): lax.ppermute(piece, plane, routes[name])  6.43 us
    ppermute x6, waiting for transfers between devices, to_home(): lax.ppermute(piece, 'date', [(i, (i - k) % date_axis) for i in range(date...  6.1 us
    pallas_call x1, Pallas kernels, inner_layer(): call(inner_settle, [part_shape] * 4 + [token_shape], [SMEM] + [VMEM] * 8,...  4.67 us
    ppermute x4, waiting for transfers between devices, local(): lax.ppermute(piece, plane, routes[name])  4.65 us
  transfers between devices with their start and end apart: 18, of which 5 were waited for; matrix products, arithmetic and copies ran while one was open for 0% of the time, Pallas kernels for 35%

profile of v3, /device:TPU:0, one launch (start us, length us, event | category | flops | bytes accessed | tf_op | source)
XLA Modules:
  0.0 75.7 jit_solution(11400774402570319000)
XLA Ops:
  0.0 1.3 %copy-done.13 = bf16[4,8,16,704]{3,2,1,0:T(8,128)(2,1)S(1)} copy-done((bf16[4,8,16,704]{3,2,1,0:T(8,128)(2,1)S(1)}, bf16[4,8,16,704]{3,2,1,0:T(8,128)(2,1)}, u32[]{:S(2)}) %copy-start.13) | copy-done | bytes 720920
  1.3 1.1 %pack.1 = (bf16[4,48,704]{2,1,0:T(8,128)(2,1)}, bf16[4,48,704]{2,1,0:T(8,128)(2,1)}, bf16[4,16,704]{2,1,0:T(8,128)(2,1)}, bf16[4,16,704]{2,1,0:T(8,128)(2,1)}) custom-call(bf16[4,8,16,704]{3,2,1,0:T(8,128)(2,1)S(1)} %copy-done.13), custom_call_target="tpu_custom_call" | custom-call | flops 10000000000 | bytes 1441792 | tf_op jit(solution)/shard_map/pack/pallas_call | solution.py:455
  2.4 1.7 %collective-permute-start = (bf16[4,48,704]{2,1,0:T(8,128)(2,1)}, bf16[4,48,704]{2,1,0:T(8,128)(2,1)S(1)}, u32[]{:S(2)}, u32[]{:S(2)}) collective-permute-start(bf16[4,48,704]{2,1,0:T(8,128)(2,1)} %get-tuple-element.28), channel_id=1, source_target_pairs={{0,2},{1,3},{2,4},{3,5},{4,6},{5,7},{6,0},{7,1},{8,10},{9,11},{10,... | collective-permute-start | bytes 811016 | tf_op jit(solution)/shard_map/ppermute | solution.py:466
  4.0 3.9 %collective-permute-start.1 = (bf16[4,48,704]{2,1,0:T(8,128)(2,1)}, bf16[4,48,704]{2,1,0:T(8,128)(2,1)}, u32[]{:S(2)}, u32[]{:S(2)}) collective-permute-start(bf16[4,48,704]{2,1,0:T(8,128)(2,1)} %get-tuple-element.29), channel_id=1, source_target_pairs={{4,2},{5,3},{6,4},{7,5},{8,6},{9,7},{10,0},{11,1},{12,10},{13,11},... | collective-permute-start | bytes 811016 | tf_op jit(solution)/shard_map/ppermute | solution.py:466
  7.9 0.0 collective-permute-start.6
  7.9 0.9 %collective-permute-start.7 = (bf16[4,16,704]{2,1,0:T(8,128)(2,1)}, bf16[4,16,704]{2,1,0:T(8,128)(2,1)}, u32[]{:S(2)}, u32[]{:S(2)}) collective-permute-start(bf16[4,16,704]{2,1,0:T(8,128)(2,1)} %get-tuple-element.35), channel_id=1, source_target_pairs={{5,2},{6,3},{7,4},{4,5},{9,6},{10,7},{11,0},{8,1},{13,10},{14,11},... | collective-permute-start | bytes 270344 | tf_op jit(solution)/shard_map/ppermute | solution.py:466
  8.8 0.0 copy-done.9
  8.8 0.0 copy-done.7
  8.8 0.0 copy-done.4
  8.8 1.8 %position_bias.1.bias.refs_5_ = f32[22,64,128]{2,1,0:T(8,128)S(1)} custom-call(f32[2,512]{1,0:T(2,128)S(1)} %copy-done.9, f32[22,512]{1,0:T(8,128)S(1)} %bitcast.7, bf16[704,2112]{1,0:T(8,128)(2,1)S(1)} %copy-done.4), custom_call_target="tpu_custom_call" | custom-call | flops 1000000000 | bytes 1000000 | tf_op jit(solution)/shard_map/position_bias/pallas_call | solution.py:469
  10.7 0.0 copy-start.2
  10.7 0.0 copy-start.5
  10.7 0.0 copy-start.10
  10.7 0.0 copy-start.11
  10.7 2.3 %collective-permute-done.low.refs_0_ = bf16[4,48,704]{2,1,0:T(8,128)(2,1)S(1)} collective-permute-done((bf16[4,48,704]{2,1,0:T(8,128)(2,1)}, bf16[4,48,704]{2,1,0:T(8,128)(2,1)S(1)}, u32[]{:S(2)}, u32[]{:S(2)}) %collective-permute-start) | collective-permute-done | bytes 270368 | tf_op jit(solution)/shard_map/ppermute | solution.py:466
  13.0 2.3 %collective-permute-done.1.high.refs_1_ = bf16[4,48,704]{2,1,0:T(8,128)(2,1)} collective-permute-done((bf16[4,48,704]{2,1,0:T(8,128)(2,1)}, bf16[4,48,704]{2,1,0:T(8,128)(2,1)}, u32[]{:S(2)}, u32[]{:S(2)}) %collective-permute-start.1) | collective-permute-done | bytes 270368 | tf_op jit(solution)/shard_map/ppermute | solution.py:466
  15.3 0.0 copy-done.14
  15.3 4.3 %inner_attention.1.mixed_heads = bf16[704,256]{1,0:T(8,128)(2,1)S(1)} custom-call(bf16[4,48,704]{2,1,0:T(8,128)(2,1)S(1)} %collective-permute-done.low.refs_0_, bf16[4,48,704]{2,1,0:T(8,128)(2,1)} %collective-permute-done.1.high.refs_1_, s32[1]{0:T(128)} %bitcast.1.last_row, f32[22]{0:T(128)S(1)} %copy-done.14, ...), custom_call_target="tpu_custom_call" | custom-call | flops 1522532352 | bytes 4000000 | tf_op jit(solution)/shard_map/inner_attention/pallas_call | solution.py:499
  19.6 0.0 copy-done.3
  19.6 0.0 copy-done.2
  19.6 0.0 copy-done.5
  19.7 0.0 copy-done.10
  19.7 0.0 copy-done.11
  19.7 4.7 %inner_settle.1 = (bf16[4,16,704]{2,1,0:T(8,128)(2,1)S(1)}, bf16[4,16,704]{2,1,0:T(8,128)(2,1)S(1)}, bf16[4,16,704]{2,1,0:T(8,128)(2,1)S(1)}, bf16[4,16,704]{2,1,0:T(8,128)(2,1)S(1)}, f32[8,128]{1,0:T(8,128)S(1)}) custom-call(s32[1]{0:T(128)} %bitcast.place, bf16[4,48,704]{2,1,0:T(8,128)(2,1)S(1)} %collective-permute-done.low.refs_0_, ...), custom_call_target="tpu_custom_call" | custom-call | flops 2283798528 | bytes 9000000 | tf_op jit(solution)/shard_map/inner_settle/pallas_call | solution.py:509
  24.4 2.8 %collective-permute-start.2 = (bf16[4,16,704]{2,1,0:T(8,128)(2,1)S(1)}, bf16[4,16,704]{2,1,0:T(8,128)(2,1)S(1)}, u32[]{:S(2)}, u32[]{:S(2)}) collective-permute-start(bf16[4,16,704]{2,1,0:T(8,128)(2,1)S(1)} %get-tuple-element.30), channel_id=1, source_target_pairs={{2,0},{3,1},{4,2},{5,3},{6,4},{7,5},{0,6},{1,7},{10,8},{11,9},{12,... | collective-permute-start | bytes 270344 | tf_op jit(solution)/shard_map/ppermute | solution.py:564
  27.1 1.4 %collective-permute-start.3 = (bf16[4,16,704]{2,1,0:T(8,128)(2,1)S(1)}, bf16[4,16,704]{2,1,0:T(8,128)(2,1)S(1)}, u32[]{:S(2)}, u32[]{:S(2)}) collective-permute-start(bf16[4,16,704]{2,1,0:T(8,128)(2,1)S(1)} %get-tuple-element.31), channel_id=1, source_target_pairs={{2,32},{3,33},{4,34},{5,35},{6,36},{7,37},{0,38},{1,39},{10,40},{1... | collective-permute-start | bytes 270344 | tf_op jit(solution)/shard_map/ppermute | solution.py:564
  28.5 5.3 %collective-permute-start.4 = (bf16[4,16,704]{2,1,0:T(8,128)(2,1)S(1)}, bf16[4,16,704]{2,1,0:T(8,128)(2,1)S(1)}, u32[]{:S(2)}, u32[]{:S(2)}) collective-permute-start(bf16[4,16,704]{2,1,0:T(8,128)(2,1)S(1)} %get-tuple-element.32), channel_id=1, source_target_pairs={{2,68},{3,69},{4,70},{5,71},{6,72},{7,73},{0,74},{1,75},{10,76},{1... | collective-permute-start | bytes 270344 | tf_op jit(solution)/shard_map/ppermute | solution.py:564
  33.8 0.0 collective-permute-done.6.refs_2_
  33.8 0.7 collective-permute-start.5
  34.5 0.0 collective-permute-done.7.refs_3_
  34.5 0.0 copy-start.8
  34.5 0.0 copy-start.12
  34.5 8.4 %straddle_window.1 = (bf16[4,16,704]{2,1,0:T(8,128)(2,1)S(1)}, bf16[4,16,704]{2,1,0:T(8,128)(2,1)S(1)}, bf16[4,16,704]{2,1,0:T(8,128)(2,1)S(1)}, bf16[4,16,704]{2,1,0:T(8,128)(2,1)S(1)}, f32[8,128]{1,0:T(8,128)S(1)}) custom-call(s32[1]{0:T(128)} %bitcast.place, s32[1]{0:T(128)} %bitcast.1.last_row, s32[1]{0:T(128)} %bitcast.4.last_col, f32[22]{0:T(128)S(1)} %copy-done.14, ...), custom_call_target="tpu_custom_call" | custom-call | flops 3806330880 | bytes 13000000 | tf_op jit(solution)/shard_map/straddle_window/pallas_call | solution.py:521
  43.0 3.9 %collective-permute-start.11 = (bf16[4,16,704]{2,1,0:T(8,128)(2,1)S(1)}, bf16[4,16,704]{2,1,0:T(8,128)(2,1)S(1)}, u32[]{:S(2)}, u32[]{:S(2)}) collective-permute-start(bf16[4,16,704]{2,1,0:T(8,128)(2,1)S(1)} %get-tuple-element.42), channel_id=1, source_target_pairs={{2,0},{3,1},{4,2},{5,3},{6,4},{7,5},{0,6},{1,7},{10,8},{11,9},{12,... | collective-permute-start | bytes 270344 | tf_op jit(solution)/shard_map/ppermute | solution.py:564
  46.8 0.0 collective-permute-done.2.refs_0_
  46.8 0.0 collective-permute-start.12
  46.8 0.0 collective-permute-done.3.refs_1_
  46.9 0.1 collective-permute-start.13
  46.9 0.0 collective-permute-done.4.refs_2_
  46.9 1.9 %collective-permute-start.14 = (bf16[4,16,704]{2,1,0:T(8,128)(2,1)S(1)}, bf16[4,16,704]{2,1,0:T(8,128)(2,1)S(1)}, u32[]{:S(2)}, u32[]{:S(2)}) collective-permute-start(bf16[4,16,704]{2,1,0:T(8,128)(2,1)S(1)} %get-tuple-element.45), channel_id=1, source_target_pairs={{2,101},{3,102},{4,103},{5,100},{6,105},{7,106},{0,107},{1,104},{1... | collective-permute-start | bytes 270344 | tf_op jit(solution)/shard_map/ppermute | solution.py:564
  48.8 0.0 collective-permute-done.5.refs_3_
  48.8 0.0 copy-done
  48.8 0.0 copy-done.1
  48.8 0.0 copy-done.6
  48.8 0.0 copy-done.8
  48.9 3.8 %time_layer.2 = (bf16[4,16,704]{2,1,0:T(8,128)(2,1)S(1)}, bf16[4,16,704]{2,1,0:T(8,128)(2,1)S(1)}, bf16[4,16,704]{2,1,0:T(8,128)(2,1)S(1)}, bf16[4,16,704]{2,1,0:T(8,128)(2,1)S(1)}, f32[8,128]{1,0:T(8,128)S(1)}) custom-call(s32[1]{0:T(128)} %bitcast.place, s32[16]{0:T(128)S(1)} %copy-done.12, bf16[4,16,704]{2,1,0:T(8,128)(2,1)S(1)} %collective-permute-done.2.refs_0_, ...), custom_call_target="tpu_custom_call" | custom-call | flops 1015021568 | bytes 5000000 | tf_op jit(solution)/shard_map/time_layer/pallas_call | solution.py:543
  52.7 3.8 %collective-permute-start.8 = (bf16[4,16,704]{2,1,0:T(8,128)(2,1)S(1)}, bf16[4,16,704]{2,1,0:T(8,128)(2,1)S(1)}, u32[]{:S(2)}, u32[]{:S(2)}) collective-permute-start(bf16[4,16,704]{2,1,0:T(8,128)(2,1)S(1)} %get-tuple-element.39), channel_id=1, source_target_pairs={{0,96},{32,0},{64,32},{96,64},{1,97},{33,1},{65,33},{97,65},{2,98}... | collective-permute-start | bytes 270344 | tf_op jit(solution)/shard_map/ppermute | solution.py:570
  56.5 0.0 collective-permute-done.11.refs_0_
  56.5 3.9 %collective-permute-start.9 = (bf16[4,16,704]{2,1,0:T(8,128)(2,1)S(1)}, bf16[4,16,704]{2,1,0:T(8,128)(2,1)S(1)}, u32[]{:S(2)}, u32[]{:S(2)}) collective-permute-start(bf16[4,16,704]{2,1,0:T(8,128)(2,1)S(1)} %get-tuple-element.40), channel_id=1, source_target_pairs={{0,64},{32,96},{64,0},{96,32},{1,65},{33,97},{65,1},{97,33},{2,66}... | collective-permute-start | bytes 270344 | tf_op jit(solution)/shard_map/ppermute | solution.py:570
  60.4 0.0 collective-permute-done.12.refs_1_
  60.4 1.3 %collective-permute-start.10 = (bf16[4,16,704]{2,1,0:T(8,128)(2,1)S(1)}, bf16[4,16,704]{2,1,0:T(8,128)(2,1)S(1)}, u32[]{:S(2)}, u32[]{:S(2)}) collective-permute-start(bf16[4,16,704]{2,1,0:T(8,128)(2,1)S(1)} %get-tuple-element.41), channel_id=1, source_target_pairs={{0,32},{32,64},{64,96},{96,0},{1,33},{33,65},{65,97},{97,1},{2,34}... | collective-permute-start | bytes 270344 | tf_op jit(solution)/shard_map/ppermute | solution.py:570
  61.7 0.0 collective-permute-done.13.refs_2_
  61.7 0.0 collective-permute-done.14.refs_3_
  61.7 3.8 %time_layer.3 = (bf16[4,16,704]{2,1,0:T(8,128)(2,1)S(1)}, bf16[4,16,704]{2,1,0:T(8,128)(2,1)S(1)}, bf16[4,16,704]{2,1,0:T(8,128)(2,1)S(1)}, bf16[4,16,704]{2,1,0:T(8,128)(2,1)S(1)}, f32[8,128]{1,0:T(8,128)}) custom-call(s32[1]{0:T(128)} %bitcast.place, s32[16]{0:T(128)S(1)} %copy-done.12, bf16[4,16,704]{2,1,0:T(8,128)(2,1)S(1)} %collective-permute-done.11.refs_0_, ...), custom_call_target="tpu_custom_call" | custom-call | flops 1015021568 | bytes 5000000 | tf_op jit(solution)/shard_map/time_layer/pallas_call | solution.py:543
  65.5 2.0 %collective-permute-start.15 = (bf16[4,16,704]{2,1,0:T(8,128)(2,1)S(1)}, bf16[4,16,704]{2,1,0:T(8,128)(2,1)S(1)}, u32[]{:S(2)}, u32[]{:S(2)}) collective-permute-start(bf16[4,16,704]{2,1,0:T(8,128)(2,1)S(1)} %get-tuple-element.48), channel_id=1, source_target_pairs={{0,96},{32,0},{64,32},{96,64},{1,97},{33,1},{65,33},{97,65},{2,98}... | collective-permute-start | bytes 270344 | tf_op jit(solution)/shard_map/ppermute | solution.py:570
  67.5 0.2 collective-permute-start.16
  67.7 0.0 collective-permute-done.8.refs_1_
  67.7 0.8 %collective-permute-start.17 = (bf16[4,16,704]{2,1,0:T(8,128)(2,1)S(1)}, bf16[4,16,704]{2,1,0:T(8,128)(2,1)S(1)}, u32[]{:S(2)}, u32[]{:S(2)}) collective-permute-start(bf16[4,16,704]{2,1,0:T(8,128)(2,1)S(1)} %get-tuple-element.50), channel_id=1, source_target_pairs={{0,32},{32,64},{64,96},{96,0},{1,33},{33,65},{65,97},{97,1},{2,34}... | collective-permute-start | bytes 270344 | tf_op jit(solution)/shard_map/ppermute | solution.py:570
  68.5 0.0 collective-permute-done.9.refs_2_
  68.5 0.0 collective-permute-done.10.refs_3_
  68.5 2.3 %collective-permute-done.15.refs_5_ = bf16[4,16,704]{2,1,0:T(8,128)(2,1)S(1)} collective-permute-done((bf16[4,16,704]{2,1,0:T(8,128)(2,1)S(1)}, bf16[4,16,704]{2,1,0:T(8,128)(2,1)S(1)}, u32[]{:S(2)}, u32[]{:S(2)}) %collective-permute-start.15) | collective-permute-done | bytes 90144 | tf_op jit(solution)/shard_map/ppermute | solution.py:570
  70.7 3.0 %collective-permute-done.16.refs_6_ = bf16[4,16,704]{2,1,0:T(8,128)(2,1)S(1)} collective-permute-done((bf16[4,16,704]{2,1,0:T(8,128)(2,1)S(1)}, bf16[4,16,704]{2,1,0:T(8,128)(2,1)S(1)}, u32[]{:S(2)}, u32[]{:S(2)}) %collective-permute-start.16) | collective-permute-done | bytes 90144 | tf_op jit(solution)/shard_map/ppermute | solution.py:570
  73.8 0.8 %collective-permute-done.17.refs_7_ = bf16[4,16,704]{2,1,0:T(8,128)(2,1)S(1)} collective-permute-done((bf16[4,16,704]{2,1,0:T(8,128)(2,1)S(1)}, bf16[4,16,704]{2,1,0:T(8,128)(2,1)S(1)}, u32[]{:S(2)}, u32[]{:S(2)}) %collective-permute-start.17) | collective-permute-done | bytes 90144 | tf_op jit(solution)/shard_map/ppermute | solution.py:570
  74.6 1.1 %assemble.1 = bf16[4,8,16,704]{3,2,1,0:T(8,128)(2,1)} custom-call(s32[1]{0:T(128)} %bitcast.place, bf16[4,16,704]{2,1,0:T(8,128)(2,1)S(1)} %get-tuple-element.38.refs_0_, bf16[4,16,704]{2,1,0:T(8,128)(2,1)S(1)} %collective-permute-done.8.refs_1_, bf16[4,16,704]{2,1,0:T(8,128)(2,1)S(1)} %collective-permute-done.9.refs_2_, ...), custom_call_target="tpu_custom_call" | custom-call | bytes 1441792 | tf_op jit(solution)/shard_map/assemble/pallas_call | solution.py:582
  (10 shorter events, 0.0 us)
Async XLA Ops:
  0.0 8.8 %copy-start.9 = (f32[2,512]{1,0:T(2,128)S(1)}, f32[2,512]{1,0:T(2,128)}, u32[]{:S(2)}) copy-start(f32[2,512]{1,0:T(2,128)} %first.1) | copy-start | bytes 12292
  0.0 8.8 %copy-start.7 = (f32[512,22]{0,1:T(8,128)S(1)}, f32[512,22]{0,1:T(8,128)}, u32[]{:S(2)}) copy-start(f32[512,22]{0,1:T(8,128)} %param.19) | copy-start | bytes 135172
  0.0 8.8 %copy-start.4 = (bf16[704,2112]{1,0:T(8,128)(2,1)S(1)}, bf16[704,2112]{1,0:T(8,128)(2,1)}, u32[]{:S(2)}) copy-start(bf16[704,2112]{1,0:T(8,128)(2,1)} %refs_6_.3) | copy-start | bytes 8921092
  0.0 1.3 %copy-start.13 = (bf16[4,8,16,704]{3,2,1,0:T(8,128)(2,1)S(1)}, bf16[4,8,16,704]{3,2,1,0:T(8,128)(2,1)}, u32[]{:S(2)}) copy-start(bf16[4,8,16,704]{3,2,1,0:T(8,128)(2,1)} %pixels.1) | copy-start | bytes 2162692
  2.4 13.0 %copy-start.14 = (f32[22]{0:T(128)S(1)}, f32[22]{0:T(128)}, u32[]{:S(2)}) copy-start(f32[22]{0:T(128)} %scale.3) | copy-start | bytes 268
  2.4 10.6 %collective-permute-start = (bf16[4,48,704]{2,1,0:T(8,128)(2,1)}, bf16[4,48,704]{2,1,0:T(8,128)(2,1)S(1)}, u32[]{:S(2)}, u32[]{:S(2)}) collective-permute-start(bf16[4,48,704]{2,1,0:T(8,128)(2,1)} %get-tuple-element.28), channel_id=1, source_target_pairs={{0,2},{1,3},{2,4},{3,5},{4,6},{5,7},{6,0},{7,1},{8,10},{9,11},{10,... | collective-permute-start | bytes 811016 | tf_op jit(solution)/shard_map/ppermute | solution.py:466
  4.0 11.3 %collective-permute-start.1 = (bf16[4,48,704]{2,1,0:T(8,128)(2,1)}, bf16[4,48,704]{2,1,0:T(8,128)(2,1)}, u32[]{:S(2)}, u32[]{:S(2)}) collective-permute-start(bf16[4,48,704]{2,1,0:T(8,128)(2,1)} %get-tuple-element.29), channel_id=1, source_target_pairs={{4,2},{5,3},{6,4},{7,5},{8,6},{9,7},{10,0},{11,1},{12,10},{13,11},... | collective-permute-start | bytes 811016 | tf_op jit(solution)/shard_map/ppermute | solution.py:466
  7.9 25.9 %collective-permute-start.6 = (bf16[4,16,704]{2,1,0:T(8,128)(2,1)}, bf16[4,16,704]{2,1,0:T(8,128)(2,1)S(1)}, u32[]{:S(2)}, u32[]{:S(2)}) collective-permute-start(bf16[4,16,704]{2,1,0:T(8,128)(2,1)} %get-tuple-element.34), channel_id=1, source_target_pairs={{1,2},{2,3},{3,4},{0,5},{5,6},{6,7},{7,0},{4,1},{9,10},{10,11},{11... | collective-permute-start | bytes 270344 | tf_op jit(solution)/shard_map/ppermute | solution.py:466
  7.9 26.6 %collective-permute-start.7 = (bf16[4,16,704]{2,1,0:T(8,128)(2,1)}, bf16[4,16,704]{2,1,0:T(8,128)(2,1)}, u32[]{:S(2)}, u32[]{:S(2)}) collective-permute-start(bf16[4,16,704]{2,1,0:T(8,128)(2,1)} %get-tuple-element.35), channel_id=1, source_target_pairs={{5,2},{6,3},{7,4},{4,5},{9,6},{10,7},{11,0},{8,1},{13,10},{14,11},... | collective-permute-start | bytes 270344 | tf_op jit(solution)/shard_map/ppermute | solution.py:466
  8.8 10.8 %copy-start.3 = (bf16[2816,704]{0,1:T(8,128)(2,1)S(1)}, bf16[2816,704]{0,1:T(8,128)(2,1)}, u32[]{:S(2)}) copy-start(bf16[2816,704]{0,1:T(8,128)(2,1)} %param.23) | copy-start | bytes 11894788
  10.7 9.0 %copy-start.2 = (bf16[704,2816]{1,0:T(8,128)(2,1)S(1)}, bf16[704,2816]{1,0:T(8,128)(2,1)}, u32[]{:S(2)}) copy-start(bf16[704,2816]{1,0:T(8,128)(2,1)} %refs_8_.3) | copy-start | bytes 11894788
  10.7 9.0 %copy-start.5 = (bf16[704,704]{1,0:T(8,128)(2,1)S(1)}, bf16[704,704]{1,0:T(8,128)(2,1)}, u32[]{:S(2)}) copy-start(bf16[704,704]{1,0:T(8,128)(2,1)} %refs_7_.3) | copy-start | bytes 2973700
  10.7 9.0 %copy-start.10 = (f32[704]{0:T(1024)S(1)}, f32[704]{0:T(1024)}, u32[]{:S(2)}) copy-start(f32[704]{0:T(1024)} %refs_10_.1) | copy-start | bytes 8452
  10.7 9.0 %copy-start.11 = (f32[704]{0:T(1024)S(1)}, f32[704]{0:T(1024)}, u32[]{:S(2)}) copy-start(f32[704]{0:T(1024)} %refs_11_.1) | copy-start | bytes 8452
  24.4 22.5 %collective-permute-start.2 = (bf16[4,16,704]{2,1,0:T(8,128)(2,1)S(1)}, bf16[4,16,704]{2,1,0:T(8,128)(2,1)S(1)}, u32[]{:S(2)}, u32[]{:S(2)}) collective-permute-start(bf16[4,16,704]{2,1,0:T(8,128)(2,1)S(1)} %get-tuple-element.30), channel_id=1, source_target_pairs={{2,0},{3,1},{4,2},{5,3},{6,4},{7,5},{0,6},{1,7},{10,8},{11,9},{12,... | collective-permute-start | bytes 270344 | tf_op jit(solution)/shard_map/ppermute | solution.py:564
  27.1 19.7 %collective-permute-start.3 = (bf16[4,16,704]{2,1,0:T(8,128)(2,1)S(1)}, bf16[4,16,704]{2,1,0:T(8,128)(2,1)S(1)}, u32[]{:S(2)}, u32[]{:S(2)}) collective-permute-start(bf16[4,16,704]{2,1,0:T(8,128)(2,1)S(1)} %get-tuple-element.31), channel_id=1, source_target_pairs={{2,32},{3,33},{4,34},{5,35},{6,36},{7,37},{0,38},{1,39},{10,40},{1... | collective-permute-start | bytes 270344 | tf_op jit(solution)/shard_map/ppermute | solution.py:564
  28.5 18.4 %collective-permute-start.4 = (bf16[4,16,704]{2,1,0:T(8,128)(2,1)S(1)}, bf16[4,16,704]{2,1,0:T(8,128)(2,1)S(1)}, u32[]{:S(2)}, u32[]{:S(2)}) collective-permute-start(bf16[4,16,704]{2,1,0:T(8,128)(2,1)S(1)} %get-tuple-element.32), channel_id=1, source_target_pairs={{2,68},{3,69},{4,70},{5,71},{6,72},{7,73},{0,74},{1,75},{10,76},{1... | collective-permute-start | bytes 270344 | tf_op jit(solution)/shard_map/ppermute | solution.py:564
  33.8 15.0 %collective-permute-start.5 = (bf16[4,16,704]{2,1,0:T(8,128)(2,1)S(1)}, bf16[4,16,704]{2,1,0:T(8,128)(2,1)S(1)}, u32[]{:S(2)}, u32[]{:S(2)}) collective-permute-start(bf16[4,16,704]{2,1,0:T(8,128)(2,1)S(1)} %get-tuple-element.33), channel_id=1, source_target_pairs={{2,100},{3,101},{4,102},{5,103},{6,104},{7,105},{0,106},{1,107},{1... | collective-permute-start | bytes 270344 | tf_op jit(solution)/shard_map/ppermute | solution.py:564
  34.5 14.3 %copy-start = (bf16[704,2112]{1,0:T(8,128)(2,1)S(1)}, bf16[704,2112]{1,0:T(8,128)(2,1)}, u32[]{:S(2)}) copy-start(bf16[704,2112]{1,0:T(8,128)(2,1)} %refs_7_.5) | copy-start | bytes 8921092
  34.5 14.3 %copy-start.1 = (bf16[704,704]{1,0:T(8,128)(2,1)S(1)}, bf16[704,704]{1,0:T(8,128)(2,1)}, u32[]{:S(2)}) copy-start(bf16[704,704]{1,0:T(8,128)(2,1)} %refs_8_.5) | copy-start | bytes 2973700
  34.5 14.3 %copy-start.6 = (f32[16,704]{1,0:T(8,128)S(1)}, f32[16,704]{1,0:T(8,128)}, u32[]{:S(2)}) copy-start(f32[16,704]{1,0:T(8,128)} %refs_5_.3) | copy-start | bytes 135172
  34.5 14.3 %copy-start.8 = (f32[704]{0:T(1024)S(1)}, f32[704]{0:T(1024)}, u32[]{:S(2)}) copy-start(f32[704]{0:T(1024)} %refs_6_.5) | copy-start | bytes 8452
  34.5 14.3 %copy-start.12 = (s32[16]{0:T(128)S(1)}, s32[16]{0:T(128)}, u32[]{:S(2)}) copy-start(s32[16]{0:T(128)} %rank.3) | copy-start | bytes 196
  43.0 13.5 %collective-permute-start.11 = (bf16[4,16,704]{2,1,0:T(8,128)(2,1)S(1)}, bf16[4,16,704]{2,1,0:T(8,128)(2,1)S(1)}, u32[]{:S(2)}, u32[]{:S(2)}) collective-permute-start(bf16[4,16,704]{2,1,0:T(8,128)(2,1)S(1)} %get-tuple-element.42), channel_id=1, source_target_pairs={{2,0},{3,1},{4,2},{5,3},{6,4},{7,5},{0,6},{1,7},{10,8},{11,9},{12,... | collective-permute-start | bytes 270344 | tf_op jit(solution)/shard_map/ppermute | solution.py:564
  46.8 13.6 %collective-permute-start.12 = (bf16[4,16,704]{2,1,0:T(8,128)(2,1)S(1)}, bf16[4,16,704]{2,1,0:T(8,128)(2,1)S(1)}, u32[]{:S(2)}, u32[]{:S(2)}) collective-permute-start(bf16[4,16,704]{2,1,0:T(8,128)(2,1)S(1)} %get-tuple-element.43), channel_id=1, source_target_pairs={{2,33},{3,34},{4,35},{5,32},{6,37},{7,38},{0,39},{1,36},{10,41},{1... | collective-permute-start | bytes 270344 | tf_op jit(solution)/shard_map/ppermute | solution.py:564
  46.9 14.9 %collective-permute-start.13 = (bf16[4,16,704]{2,1,0:T(8,128)(2,1)S(1)}, bf16[4,16,704]{2,1,0:T(8,128)(2,1)S(1)}, u32[]{:S(2)}, u32[]{:S(2)}) collective-permute-start(bf16[4,16,704]{2,1,0:T(8,128)(2,1)S(1)} %get-tuple-element.44), channel_id=1, source_target_pairs={{2,68},{3,69},{4,70},{5,71},{6,72},{7,73},{0,74},{1,75},{10,76},{1... | collective-permute-start | bytes 270344 | tf_op jit(solution)/shard_map/ppermute | solution.py:564
  46.9 14.8 %collective-permute-start.14 = (bf16[4,16,704]{2,1,0:T(8,128)(2,1)S(1)}, bf16[4,16,704]{2,1,0:T(8,128)(2,1)S(1)}, u32[]{:S(2)}, u32[]{:S(2)}) collective-permute-start(bf16[4,16,704]{2,1,0:T(8,128)(2,1)S(1)} %get-tuple-element.45), channel_id=1, source_target_pairs={{2,101},{3,102},{4,103},{5,100},{6,105},{7,106},{0,107},{1,104},{1... | collective-permute-start | bytes 270344 | tf_op jit(solution)/shard_map/ppermute | solution.py:564
  52.7 15.0 %collective-permute-start.8 = (bf16[4,16,704]{2,1,0:T(8,128)(2,1)S(1)}, bf16[4,16,704]{2,1,0:T(8,128)(2,1)S(1)}, u32[]{:S(2)}, u32[]{:S(2)}) collective-permute-start(bf16[4,16,704]{2,1,0:T(8,128)(2,1)S(1)} %get-tuple-element.39), channel_id=1, source_target_pairs={{0,96},{32,0},{64,32},{96,64},{1,97},{33,1},{65,33},{97,65},{2,98}... | collective-permute-start | bytes 270344 | tf_op jit(solution)/shard_map/ppermute | solution.py:570
  56.5 12.0 %collective-permute-start.9 = (bf16[4,16,704]{2,1,0:T(8,128)(2,1)S(1)}, bf16[4,16,704]{2,1,0:T(8,128)(2,1)S(1)}, u32[]{:S(2)}, u32[]{:S(2)}) collective-permute-start(bf16[4,16,704]{2,1,0:T(8,128)(2,1)S(1)} %get-tuple-element.40), channel_id=1, source_target_pairs={{0,64},{32,96},{64,0},{96,32},{1,65},{33,97},{65,1},{97,33},{2,66}... | collective-permute-start | bytes 270344 | tf_op jit(solution)/shard_map/ppermute | solution.py:570
  60.4 8.1 %collective-permute-start.10 = (bf16[4,16,704]{2,1,0:T(8,128)(2,1)S(1)}, bf16[4,16,704]{2,1,0:T(8,128)(2,1)S(1)}, u32[]{:S(2)}, u32[]{:S(2)}) collective-permute-start(bf16[4,16,704]{2,1,0:T(8,128)(2,1)S(1)} %get-tuple-element.41), channel_id=1, source_target_pairs={{0,32},{32,64},{64,96},{96,0},{1,33},{33,65},{65,97},{97,1},{2,34}... | collective-permute-start | bytes 270344 | tf_op jit(solution)/shard_map/ppermute | solution.py:570
  65.5 5.2 %collective-permute-start.15 = (bf16[4,16,704]{2,1,0:T(8,128)(2,1)S(1)}, bf16[4,16,704]{2,1,0:T(8,128)(2,1)S(1)}, u32[]{:S(2)}, u32[]{:S(2)}) collective-permute-start(bf16[4,16,704]{2,1,0:T(8,128)(2,1)S(1)} %get-tuple-element.48), channel_id=1, source_target_pairs={{0,96},{32,0},{64,32},{96,64},{1,97},{33,1},{65,33},{97,65},{2,98}... | collective-permute-start | bytes 270344 | tf_op jit(solution)/shard_map/ppermute | solution.py:570
  67.5 6.2 %collective-permute-start.16 = (bf16[4,16,704]{2,1,0:T(8,128)(2,1)S(1)}, bf16[4,16,704]{2,1,0:T(8,128)(2,1)S(1)}, u32[]{:S(2)}, u32[]{:S(2)}) collective-permute-start(bf16[4,16,704]{2,1,0:T(8,128)(2,1)S(1)} %get-tuple-element.49), channel_id=1, source_target_pairs={{0,64},{32,96},{64,0},{96,32},{1,65},{33,97},{65,1},{97,33},{2,66}... | collective-permute-start | bytes 270344 | tf_op jit(solution)/shard_map/ppermute | solution.py:570
  67.7 6.9 %collective-permute-start.17 = (bf16[4,16,704]{2,1,0:T(8,128)(2,1)S(1)}, bf16[4,16,704]{2,1,0:T(8,128)(2,1)S(1)}, u32[]{:S(2)}, u32[]{:S(2)}) collective-permute-start(bf16[4,16,704]{2,1,0:T(8,128)(2,1)S(1)} %get-tuple-element.50), channel_id=1, source_target_pairs={{0,32},{32,64},{64,96},{96,0},{1,33},{33,65},{65,97},{97,1},{2,34}... | collective-permute-start | bytes 270344 | tf_op jit(solution)/shard_map/ppermute | solution.py:570

commit v4 on v3

--- a/solution.py
+++ b/solution.py
@@ -235,23 +235,17 @@
     gain = attention_gain[...].reshape(1, features)
     resid = (tokens.astype(F32) + layer_norm(projected, gain)).astype(BF16)
 
-    total = up.shape[1]
-    raised, parts = [], []
+    parts = []
 
     def raise_block(span):
         return dot(resid, up[:, slice(*span)])
 
-    def lower_block(span, block):
-        raised.append(gelu(block).astype(BF16))
-        if len(raised) == 2 or span[1] == total:
-            start = span[1] - 256 * len(raised)
-            hidden = jnp.concatenate(raised, axis=1)
-            parts.append(dot_last(hidden, down[:, start : span[1]]))
-            raised.clear()
-            if len(parts) > 1:
-                parts[:] = [parts[0] + parts[1]]
-
-    staggered(column_blocks(total, 256), raise_block, lower_block)
+    def lower_block(span, raised):
+        parts.append(dot_last(gelu(raised).astype(BF16), down[:, slice(*span)]))
+        if len(parts) > 1:
+            parts[:] = [parts[0] + parts[1]]
+
+    staggered(column_blocks(up.shape[1], 512), raise_block, lower_block)
     (lowered,) = parts
     return resid.astype(F32) + layer_norm(lowered, forward_gain[...].reshape(1, features))
 

time: 75.9 us -> 76.2 us (level)
  transfers between devices with their start and end apart: 18 -> 18, of which waited for: 5 -> 5; matrix products, arithmetic and copies ran while one was open for 0% -> 0% of each run, Pallas kernels for 35% -> 36%
where the time goes in v4:
time: 76.2 us; the launch traced here: 76 us
  starting transfers between devices  34.4 us (45%)
  Pallas kernels  29.4 us (39%)
  waiting for transfers between devices  10.8 us (14%)
  local copies, waits for them, and re-layouts  1.35 us (2%)
    ppermute x8, starting transfers between devices, to_dates(): lax.ppermute(piece, space, routes[kind][k])  16 us
    ppermute x6, starting transfers between devices, to_home(): lax.ppermute(piece, 'date', [(i, (i - k) % date_axis) for i in range(date...  12 us
    pallas_call x1, Pallas kernels, straddle_layer(): call(straddle_window, [part_shape] * 4 + [token_shape], [SMEM] * 4 + [VME...  8.42 us
    pallas_call x2, Pallas kernels, time_layer(): call(functools.partial(time_kernel, features // heads), [part_shape] * 4...  7.62 us
    ppermute x4, starting transfers between devices, local(): lax.ppermute(piece, plane, routes[name])  6.43 us
    ppermute x6, waiting for transfers between devices, to_home(): lax.ppermute(piece, 'date', [(i, (i - k) % date_axis) for i in range(date...  6.1 us
    pallas_call x1, Pallas kernels, inner_layer(): call(inner_settle, [part_shape] * 4 + [token_shape], [SMEM] + [VMEM] * 8,...  4.99 us
    ppermute x4, waiting for transfers between devices, local(): lax.ppermute(piece, plane, routes[name])  4.65 us
  transfers between devices with their start and end apart: 18, of which 5 were waited for; matrix products, arithmetic and copies ran while one was open for 0% of the time, Pallas kernels for 36%

profile of v4, /device:TPU:0, one launch (start us, length us, event | category | flops | bytes accessed | tf_op | source)
XLA Modules:
  0.0 76.0 jit_solution(7793776987398894467)
XLA Ops:
  0.0 1.3 %copy-done.13 = bf16[4,8,16,704]{3,2,1,0:T(8,128)(2,1)S(1)} copy-done((bf16[4,8,16,704]{3,2,1,0:T(8,128)(2,1)S(1)}, bf16[4,8,16,704]{3,2,1,0:T(8,128)(2,1)}, u32[]{:S(2)}) %copy-start.13) | copy-done | bytes 720920
  1.3 1.1 %pack.1 = (bf16[4,48,704]{2,1,0:T(8,128)(2,1)}, bf16[4,48,704]{2,1,0:T(8,128)(2,1)}, bf16[4,16,704]{2,1,0:T(8,128)(2,1)}, bf16[4,16,704]{2,1,0:T(8,128)(2,1)}) custom-call(bf16[4,8,16,704]{3,2,1,0:T(8,128)(2,1)S(1)} %copy-done.13), custom_call_target="tpu_custom_call" | custom-call | flops 10000000000 | bytes 1441792 | tf_op jit(solution)/shard_map/pack/pallas_call | solution.py:449
  2.4 1.7 %collective-permute-start = (bf16[4,48,704]{2,1,0:T(8,128)(2,1)}, bf16[4,48,704]{2,1,0:T(8,128)(2,1)S(1)}, u32[]{:S(2)}, u32[]{:S(2)}) collective-permute-start(bf16[4,48,704]{2,1,0:T(8,128)(2,1)} %get-tuple-element.28), channel_id=1, source_target_pairs={{0,2},{1,3},{2,4},{3,5},{4,6},{5,7},{6,0},{7,1},{8,10},{9,11},{10,... | collective-permute-start | bytes 811016 | tf_op jit(solution)/shard_map/ppermute | solution.py:460
  4.0 3.9 %collective-permute-start.1 = (bf16[4,48,704]{2,1,0:T(8,128)(2,1)}, bf16[4,48,704]{2,1,0:T(8,128)(2,1)}, u32[]{:S(2)}, u32[]{:S(2)}) collective-permute-start(bf16[4,48,704]{2,1,0:T(8,128)(2,1)} %get-tuple-element.29), channel_id=1, source_target_pairs={{4,2},{5,3},{6,4},{7,5},{8,6},{9,7},{10,0},{11,1},{12,10},{13,11},... | collective-permute-start | bytes 811016 | tf_op jit(solution)/shard_map/ppermute | solution.py:460
  7.9 0.0 collective-permute-start.6
  7.9 0.9 %collective-permute-start.7 = (bf16[4,16,704]{2,1,0:T(8,128)(2,1)}, bf16[4,16,704]{2,1,0:T(8,128)(2,1)}, u32[]{:S(2)}, u32[]{:S(2)}) collective-permute-start(bf16[4,16,704]{2,1,0:T(8,128)(2,1)} %get-tuple-element.35), channel_id=1, source_target_pairs={{5,2},{6,3},{7,4},{4,5},{9,6},{10,7},{11,0},{8,1},{13,10},{14,11},... | collective-permute-start | bytes 270344 | tf_op jit(solution)/shard_map/ppermute | solution.py:460
  8.8 0.0 copy-done.9
  8.8 0.0 copy-done.7
  8.8 0.0 copy-done.4
  8.8 1.8 %position_bias.1.bias.refs_5_ = f32[22,64,128]{2,1,0:T(8,128)S(1)} custom-call(f32[2,512]{1,0:T(2,128)S(1)} %copy-done.9, f32[22,512]{1,0:T(8,128)S(1)} %bitcast.7, bf16[704,2112]{1,0:T(8,128)(2,1)S(1)} %copy-done.4), custom_call_target="tpu_custom_call" | custom-call | flops 1000000000 | bytes 1000000 | tf_op jit(solution)/shard_map/position_bias/pallas_call | solution.py:463
  10.7 0.0 copy-start.2
  10.7 0.0 copy-start.5
  10.7 0.0 copy-start.10
  10.7 0.0 copy-start.11
  10.7 2.3 %collective-permute-done.low.refs_0_ = bf16[4,48,704]{2,1,0:T(8,128)(2,1)S(1)} collective-permute-done((bf16[4,48,704]{2,1,0:T(8,128)(2,1)}, bf16[4,48,704]{2,1,0:T(8,128)(2,1)S(1)}, u32[]{:S(2)}, u32[]{:S(2)}) %collective-permute-start) | collective-permute-done | bytes 270368 | tf_op jit(solution)/shard_map/ppermute | solution.py:460
  13.0 2.3 %collective-permute-done.1.high.refs_1_ = bf16[4,48,704]{2,1,0:T(8,128)(2,1)} collective-permute-done((bf16[4,48,704]{2,1,0:T(8,128)(2,1)}, bf16[4,48,704]{2,1,0:T(8,128)(2,1)}, u32[]{:S(2)}, u32[]{:S(2)}) %collective-permute-start.1) | collective-permute-done | bytes 270368 | tf_op jit(solution)/shard_map/ppermute | solution.py:460
  15.3 0.0 copy-done.14
  15.3 4.3 %inner_attention.1.mixed_heads = bf16[704,256]{1,0:T(8,128)(2,1)S(1)} custom-call(bf16[4,48,704]{2,1,0:T(8,128)(2,1)S(1)} %collective-permute-done.low.refs_0_, bf16[4,48,704]{2,1,0:T(8,128)(2,1)} %collective-permute-done.1.high.refs_1_, s32[1]{0:T(128)} %bitcast.1.last_row, f32[22]{0:T(128)S(1)} %copy-done.14, ...), custom_call_target="tpu_custom_call" | custom-call | flops 1522532352 | bytes 4000000 | tf_op jit(solution)/shard_map/inner_attention/pallas_call | solution.py:493
  19.6 0.0 copy-done.3
  19.6 0.0 copy-done.2
  19.6 0.0 copy-done.5
  19.7 0.0 copy-done.10
  19.7 0.0 copy-done.11
  19.7 5.0 %inner_settle.1 = (bf16[4,16,704]{2,1,0:T(8,128)(2,1)S(1)}, bf16[4,16,704]{2,1,0:T(8,128)(2,1)S(1)}, bf16[4,16,704]{2,1,0:T(8,128)(2,1)S(1)}, bf16[4,16,704]{2,1,0:T(8,128)(2,1)S(1)}, f32[8,128]{1,0:T(8,128)S(1)}) custom-call(s32[1]{0:T(128)} %bitcast.place, bf16[4,48,704]{2,1,0:T(8,128)(2,1)S(1)} %collective-permute-done.low.refs_0_, ...), custom_call_target="tpu_custom_call" | custom-call | flops 2283798528 | bytes 9000000 | tf_op jit(solution)/shard_map/inner_settle/pallas_call | solution.py:503
  24.7 2.8 %collective-permute-start.2 = (bf16[4,16,704]{2,1,0:T(8,128)(2,1)S(1)}, bf16[4,16,704]{2,1,0:T(8,128)(2,1)S(1)}, u32[]{:S(2)}, u32[]{:S(2)}) collective-permute-start(bf16[4,16,704]{2,1,0:T(8,128)(2,1)S(1)} %get-tuple-element.30), channel_id=1, source_target_pairs={{2,0},{3,1},{4,2},{5,3},{6,4},{7,5},{0,6},{1,7},{10,8},{11,9},{12,... | collective-permute-start | bytes 270344 | tf_op jit(solution)/shard_map/ppermute | solution.py:558
  27.4 1.4 %collective-permute-start.3 = (bf16[4,16,704]{2,1,0:T(8,128)(2,1)S(1)}, bf16[4,16,704]{2,1,0:T(8,128)(2,1)S(1)}, u32[]{:S(2)}, u32[]{:S(2)}) collective-permute-start(bf16[4,16,704]{2,1,0:T(8,128)(2,1)S(1)} %get-tuple-element.31), channel_id=1, source_target_pairs={{2,32},{3,33},{4,34},{5,35},{6,36},{7,37},{0,38},{1,39},{10,40},{1... | collective-permute-start | bytes 270344 | tf_op jit(solution)/shard_map/ppermute | solution.py:558
  28.9 5.3 %collective-permute-start.4 = (bf16[4,16,704]{2,1,0:T(8,128)(2,1)S(1)}, bf16[4,16,704]{2,1,0:T(8,128)(2,1)S(1)}, u32[]{:S(2)}, u32[]{:S(2)}) collective-permute-start(bf16[4,16,704]{2,1,0:T(8,128)(2,1)S(1)} %get-tuple-element.32), channel_id=1, source_target_pairs={{2,68},{3,69},{4,70},{5,71},{6,72},{7,73},{0,74},{1,75},{10,76},{1... | collective-permute-start | bytes 270344 | tf_op jit(solution)/shard_map/ppermute | solution.py:558
  34.2 0.0 collective-permute-done.6.refs_2_
  34.2 0.7 collective-permute-start.5
  34.8 0.0 collective-permute-done.7.refs_3_
  34.8 0.0 copy-start.8
  34.8 0.0 copy-start.12
  34.9 8.4 %straddle_window.1 = (bf16[4,16,704]{2,1,0:T(8,128)(2,1)S(1)}, bf16[4,16,704]{2,1,0:T(8,128)(2,1)S(1)}, bf16[4,16,704]{2,1,0:T(8,128)(2,1)S(1)}, bf16[4,16,704]{2,1,0:T(8,128)(2,1)S(1)}, f32[8,128]{1,0:T(8,128)S(1)}) custom-call(s32[1]{0:T(128)} %bitcast.place, s32[1]{0:T(128)} %bitcast.1.last_row, s32[1]{0:T(128)} %bitcast.4.last_col, f32[22]{0:T(128)S(1)} %copy-done.14, ...), custom_call_target="tpu_custom_call" | custom-call | flops 3806330880 | bytes 13000000 | tf_op jit(solution)/shard_map/straddle_window/pallas_call | solution.py:515
  43.3 3.9 %collective-permute-start.11 = (bf16[4,16,704]{2,1,0:T(8,128)(2,1)S(1)}, bf16[4,16,704]{2,1,0:T(8,128)(2,1)S(1)}, u32[]{:S(2)}, u32[]{:S(2)}) collective-permute-start(bf16[4,16,704]{2,1,0:T(8,128)(2,1)S(1)} %get-tuple-element.42), channel_id=1, source_target_pairs={{2,0},{3,1},{4,2},{5,3},{6,4},{7,5},{0,6},{1,7},{10,8},{11,9},{12,... | collective-permute-start | bytes 270344 | tf_op jit(solution)/shard_map/ppermute | solution.py:558
  47.2 0.0 collective-permute-done.2.refs_0_
  47.2 0.0 collective-permute-start.12
  47.2 0.0 collective-permute-done.3.refs_1_
  47.2 0.1 collective-permute-start.13
  47.2 0.0 collective-permute-done.4.refs_2_
  47.3 1.9 %collective-permute-start.14 = (bf16[4,16,704]{2,1,0:T(8,128)(2,1)S(1)}, bf16[4,16,704]{2,1,0:T(8,128)(2,1)S(1)}, u32[]{:S(2)}, u32[]{:S(2)}) collective-permute-start(bf16[4,16,704]{2,1,0:T(8,128)(2,1)S(1)} %get-tuple-element.45), channel_id=1, source_target_pairs={{2,101},{3,102},{4,103},{5,100},{6,105},{7,106},{0,107},{1,104},{1... | collective-permute-start | bytes 270344 | tf_op jit(solution)/shard_map/ppermute | solution.py:558
  49.1 0.0 collective-permute-done.5.refs_3_
  49.1 0.0 copy-done.1
  49.1 0.0 copy-done.6
  49.2 0.0 copy-done.8
  49.2 0.0 copy-done.12
  49.2 3.8 %time_layer.2 = (bf16[4,16,704]{2,1,0:T(8,128)(2,1)S(1)}, bf16[4,16,704]{2,1,0:T(8,128)(2,1)S(1)}, bf16[4,16,704]{2,1,0:T(8,128)(2,1)S(1)}, bf16[4,16,704]{2,1,0:T(8,128)(2,1)S(1)}, f32[8,128]{1,0:T(8,128)S(1)}) custom-call(s32[1]{0:T(128)} %bitcast.place, s32[16]{0:T(128)S(1)} %copy-done.12, bf16[4,16,704]{2,1,0:T(8,128)(2,1)S(1)} %collective-permute-done.2.refs_0_, ...), custom_call_target="tpu_custom_call" | custom-call | flops 1015021568 | bytes 5000000 | tf_op jit(solution)/shard_map/time_layer/pallas_call | solution.py:537
  53.0 3.8 %collective-permute-start.8 = (bf16[4,16,704]{2,1,0:T(8,128)(2,1)S(1)}, bf16[4,16,704]{2,1,0:T(8,128)(2,1)S(1)}, u32[]{:S(2)}, u32[]{:S(2)}) collective-permute-start(bf16[4,16,704]{2,1,0:T(8,128)(2,1)S(1)} %get-tuple-element.39), channel_id=1, source_target_pairs={{0,96},{32,0},{64,32},{96,64},{1,97},{33,1},{65,33},{97,65},{2,98}... | collective-permute-start | bytes 270344 | tf_op jit(solution)/shard_map/ppermute | solution.py:564
  56.8 0.0 collective-permute-done.11.refs_0_
  56.8 3.9 %collective-permute-start.9 = (bf16[4,16,704]{2,1,0:T(8,128)(2,1)S(1)}, bf16[4,16,704]{2,1,0:T(8,128)(2,1)S(1)}, u32[]{:S(2)}, u32[]{:S(2)}) collective-permute-start(bf16[4,16,704]{2,1,0:T(8,128)(2,1)S(1)} %get-tuple-element.40), channel_id=1, source_target_pairs={{0,64},{32,96},{64,0},{96,32},{1,65},{33,97},{65,1},{97,33},{2,66}... | collective-permute-start | bytes 270344 | tf_op jit(solution)/shard_map/ppermute | solution.py:564
  60.7 0.0 collective-permute-done.12.refs_1_
  60.7 1.3 %collective-permute-start.10 = (bf16[4,16,704]{2,1,0:T(8,128)(2,1)S(1)}, bf16[4,16,704]{2,1,0:T(8,128)(2,1)S(1)}, u32[]{:S(2)}, u32[]{:S(2)}) collective-permute-start(bf16[4,16,704]{2,1,0:T(8,128)(2,1)S(1)} %get-tuple-element.41), channel_id=1, source_target_pairs={{0,32},{32,64},{64,96},{96,0},{1,33},{33,65},{65,97},{97,1},{2,34}... | collective-permute-start | bytes 270344 | tf_op jit(solution)/shard_map/ppermute | solution.py:564
  62.0 0.0 collective-permute-done.13.refs_2_
  62.0 0.0 collective-permute-done.14.refs_3_
  62.0 3.8 %time_layer.3 = (bf16[4,16,704]{2,1,0:T(8,128)(2,1)S(1)}, bf16[4,16,704]{2,1,0:T(8,128)(2,1)S(1)}, bf16[4,16,704]{2,1,0:T(8,128)(2,1)S(1)}, bf16[4,16,704]{2,1,0:T(8,128)(2,1)S(1)}, f32[8,128]{1,0:T(8,128)}) custom-call(s32[1]{0:T(128)} %bitcast.place, s32[16]{0:T(128)S(1)} %copy-done.12, bf16[4,16,704]{2,1,0:T(8,128)(2,1)S(1)} %collective-permute-done.11.refs_0_, ...), custom_call_target="tpu_custom_call" | custom-call | flops 1015021568 | bytes 5000000 | tf_op jit(solution)/shard_map/time_layer/pallas_call | solution.py:537
  65.9 2.0 %collective-permute-start.15 = (bf16[4,16,704]{2,1,0:T(8,128)(2,1)S(1)}, bf16[4,16,704]{2,1,0:T(8,128)(2,1)S(1)}, u32[]{:S(2)}, u32[]{:S(2)}) collective-permute-start(bf16[4,16,704]{2,1,0:T(8,128)(2,1)S(1)} %get-tuple-element.48), channel_id=1, source_target_pairs={{0,96},{32,0},{64,32},{96,64},{1,97},{33,1},{65,33},{97,65},{2,98}... | collective-permute-start | bytes 270344 | tf_op jit(solution)/shard_map/ppermute | solution.py:564
  67.8 0.2 collective-permute-start.16
  68.0 0.0 collective-permute-done.8.refs_1_
  68.0 0.8 %collective-permute-start.17 = (bf16[4,16,704]{2,1,0:T(8,128)(2,1)S(1)}, bf16[4,16,704]{2,1,0:T(8,128)(2,1)S(1)}, u32[]{:S(2)}, u32[]{:S(2)}) collective-permute-start(bf16[4,16,704]{2,1,0:T(8,128)(2,1)S(1)} %get-tuple-element.50), channel_id=1, source_target_pairs={{0,32},{32,64},{64,96},{96,0},{1,33},{33,65},{65,97},{97,1},{2,34}... | collective-permute-start | bytes 270344 | tf_op jit(solution)/shard_map/ppermute | solution.py:564
  68.8 0.0 collective-permute-done.9.refs_2_
  68.8 0.0 collective-permute-done.10.refs_3_
  68.8 2.3 %collective-permute-done.15.refs_5_ = bf16[4,16,704]{2,1,0:T(8,128)(2,1)S(1)} collective-permute-done((bf16[4,16,704]{2,1,0:T(8,128)(2,1)S(1)}, bf16[4,16,704]{2,1,0:T(8,128)(2,1)S(1)}, u32[]{:S(2)}, u32[]{:S(2)}) %collective-permute-start.15) | collective-permute-done | bytes 90144 | tf_op jit(solution)/shard_map/ppermute | solution.py:564
  71.1 3.0 %collective-permute-done.16.refs_6_ = bf16[4,16,704]{2,1,0:T(8,128)(2,1)S(1)} collective-permute-done((bf16[4,16,704]{2,1,0:T(8,128)(2,1)S(1)}, bf16[4,16,704]{2,1,0:T(8,128)(2,1)S(1)}, u32[]{:S(2)}, u32[]{:S(2)}) %collective-permute-start.16) | collective-permute-done | bytes 90144 | tf_op jit(solution)/shard_map/ppermute | solution.py:564
  74.1 0.8 %collective-permute-done.17.refs_7_ = bf16[4,16,704]{2,1,0:T(8,128)(2,1)S(1)} collective-permute-done((bf16[4,16,704]{2,1,0:T(8,128)(2,1)S(1)}, bf16[4,16,704]{2,1,0:T(8,128)(2,1)S(1)}, u32[]{:S(2)}, u32[]{:S(2)}) %collective-permute-start.17) | collective-permute-done | bytes 90144 | tf_op jit(solution)/shard_map/ppermute | solution.py:564
  74.9 1.1 %assemble.1 = bf16[4,8,16,704]{3,2,1,0:T(8,128)(2,1)} custom-call(s32[1]{0:T(128)} %bitcast.place, bf16[4,16,704]{2,1,0:T(8,128)(2,1)S(1)} %get-tuple-element.38.refs_0_, bf16[4,16,704]{2,1,0:T(8,128)(2,1)S(1)} %collective-permute-done.8.refs_1_, bf16[4,16,704]{2,1,0:T(8,128)(2,1)S(1)} %collective-permute-done.9.refs_2_, ...), custom_call_target="tpu_custom_call" | custom-call | bytes 1441792 | tf_op jit(solution)/shard_map/assemble/pallas_call | solution.py:576
  (10 shorter events, 0.0 us)
Async XLA Ops:
  0.0 8.8 %copy-start.9 = (f32[2,512]{1,0:T(2,128)S(1)}, f32[2,512]{1,0:T(2,128)}, u32[]{:S(2)}) copy-start(f32[2,512]{1,0:T(2,128)} %first.1) | copy-start | bytes 12292
  0.0 8.8 %copy-start.7 = (f32[512,22]{0,1:T(8,128)S(1)}, f32[512,22]{0,1:T(8,128)}, u32[]{:S(2)}) copy-start(f32[512,22]{0,1:T(8,128)} %param.19) | copy-start | bytes 135172
  0.0 8.8 %copy-start.4 = (bf16[704,2112]{1,0:T(8,128)(2,1)S(1)}, bf16[704,2112]{1,0:T(8,128)(2,1)}, u32[]{:S(2)}) copy-start(bf16[704,2112]{1,0:T(8,128)(2,1)} %refs_6_.3) | copy-start | bytes 8921092
  0.0 1.3 %copy-start.13 = (bf16[4,8,16,704]{3,2,1,0:T(8,128)(2,1)S(1)}, bf16[4,8,16,704]{3,2,1,0:T(8,128)(2,1)}, u32[]{:S(2)}) copy-start(bf16[4,8,16,704]{3,2,1,0:T(8,128)(2,1)} %pixels.1) | copy-start | bytes 2162692
  2.4 13.0 %copy-start.14 = (f32[22]{0:T(128)S(1)}, f32[22]{0:T(128)}, u32[]{:S(2)}) copy-start(f32[22]{0:T(128)} %scale.3) | copy-start | bytes 268
  2.4 10.6 %collective-permute-start = (bf16[4,48,704]{2,1,0:T(8,128)(2,1)}, bf16[4,48,704]{2,1,0:T(8,128)(2,1)S(1)}, u32[]{:S(2)}, u32[]{:S(2)}) collective-permute-start(bf16[4,48,704]{2,1,0:T(8,128)(2,1)} %get-tuple-element.28), channel_id=1, source_target_pairs={{0,2},{1,3},{2,4},{3,5},{4,6},{5,7},{6,0},{7,1},{8,10},{9,11},{10,... | collective-permute-start | bytes 811016 | tf_op jit(solution)/shard_map/ppermute | solution.py:460
  4.0 11.3 %collective-permute-start.1 = (bf16[4,48,704]{2,1,0:T(8,128)(2,1)}, bf16[4,48,704]{2,1,0:T(8,128)(2,1)}, u32[]{:S(2)}, u32[]{:S(2)}) collective-permute-start(bf16[4,48,704]{2,1,0:T(8,128)(2,1)} %get-tuple-element.29), channel_id=1, source_target_pairs={{4,2},{5,3},{6,4},{7,5},{8,6},{9,7},{10,0},{11,1},{12,10},{13,11},... | collective-permute-start | bytes 811016 | tf_op jit(solution)/shard_map/ppermute | solution.py:460
  7.9 26.3 %collective-permute-start.6 = (bf16[4,16,704]{2,1,0:T(8,128)(2,1)}, bf16[4,16,704]{2,1,0:T(8,128)(2,1)S(1)}, u32[]{:S(2)}, u32[]{:S(2)}) collective-permute-start(bf16[4,16,704]{2,1,0:T(8,128)(2,1)} %get-tuple-element.34), channel_id=1, source_target_pairs={{1,2},{2,3},{3,4},{0,5},{5,6},{6,7},{7,0},{4,1},{9,10},{10,11},{11... | collective-permute-start | bytes 270344 | tf_op jit(solution)/shard_map/ppermute | solution.py:460
  7.9 26.9 %collective-permute-start.7 = (bf16[4,16,704]{2,1,0:T(8,128)(2,1)}, bf16[4,16,704]{2,1,0:T(8,128)(2,1)}, u32[]{:S(2)}, u32[]{:S(2)}) collective-permute-start(bf16[4,16,704]{2,1,0:T(8,128)(2,1)} %get-tuple-element.35), channel_id=1, source_target_pairs={{5,2},{6,3},{7,4},{4,5},{9,6},{10,7},{11,0},{8,1},{13,10},{14,11},... | collective-permute-start | bytes 270344 | tf_op jit(solution)/shard_map/ppermute | solution.py:460
  8.8 10.8 %copy-start.3 = (bf16[2816,704]{0,1:T(8,128)(2,1)S(1)}, bf16[2816,704]{0,1:T(8,128)(2,1)}, u32[]{:S(2)}) copy-start(bf16[2816,704]{0,1:T(8,128)(2,1)} %param.23) | copy-start | bytes 11894788
  10.7 9.0 %copy-start.2 = (bf16[704,2816]{1,0:T(8,128)(2,1)S(1)}, bf16[704,2816]{1,0:T(8,128)(2,1)}, u32[]{:S(2)}) copy-start(bf16[704,2816]{1,0:T(8,128)(2,1)} %refs_8_.3) | copy-start | bytes 11894788
  10.7 9.0 %copy-start.5 = (bf16[704,704]{1,0:T(8,128)(2,1)S(1)}, bf16[704,704]{1,0:T(8,128)(2,1)}, u32[]{:S(2)}) copy-start(bf16[704,704]{1,0:T(8,128)(2,1)} %refs_7_.3) | copy-start | bytes 2973700
  10.7 9.0 %copy-start.10 = (f32[704]{0:T(1024)S(1)}, f32[704]{0:T(1024)}, u32[]{:S(2)}) copy-start(f32[704]{0:T(1024)} %refs_10_.1) | copy-start | bytes 8452
  10.7 9.0 %copy-start.11 = (f32[704]{0:T(1024)S(1)}, f32[704]{0:T(1024)}, u32[]{:S(2)}) copy-start(f32[704]{0:T(1024)} %refs_11_.1) | copy-start | bytes 8452
  24.7 22.5 %collective-permute-start.2 = (bf16[4,16,704]{2,1,0:T(8,128)(2,1)S(1)}, bf16[4,16,704]{2,1,0:T(8,128)(2,1)S(1)}, u32[]{:S(2)}, u32[]{:S(2)}) collective-permute-start(bf16[4,16,704]{2,1,0:T(8,128)(2,1)S(1)} %get-tuple-element.30), channel_id=1, source_target_pairs={{2,0},{3,1},{4,2},{5,3},{6,4},{7,5},{0,6},{1,7},{10,8},{11,9},{12,... | collective-permute-start | bytes 270344 | tf_op jit(solution)/shard_map/ppermute | solution.py:558
  27.4 19.7 %collective-permute-start.3 = (bf16[4,16,704]{2,1,0:T(8,128)(2,1)S(1)}, bf16[4,16,704]{2,1,0:T(8,128)(2,1)S(1)}, u32[]{:S(2)}, u32[]{:S(2)}) collective-permute-start(bf16[4,16,704]{2,1,0:T(8,128)(2,1)S(1)} %get-tuple-element.31), channel_id=1, source_target_pairs={{2,32},{3,33},{4,34},{5,35},{6,36},{7,37},{0,38},{1,39},{10,40},{1... | collective-permute-start | bytes 270344 | tf_op jit(solution)/shard_map/ppermute | solution.py:558
  28.9 18.4 %collective-permute-start.4 = (bf16[4,16,704]{2,1,0:T(8,128)(2,1)S(1)}, bf16[4,16,704]{2,1,0:T(8,128)(2,1)S(1)}, u32[]{:S(2)}, u32[]{:S(2)}) collective-permute-start(bf16[4,16,704]{2,1,0:T(8,128)(2,1)S(1)} %get-tuple-element.32), channel_id=1, source_target_pairs={{2,68},{3,69},{4,70},{5,71},{6,72},{7,73},{0,74},{1,75},{10,76},{1... | collective-permute-start | bytes 270344 | tf_op jit(solution)/shard_map/ppermute | solution.py:558
  34.2 15.0 %collective-permute-start.5 = (bf16[4,16,704]{2,1,0:T(8,128)(2,1)S(1)}, bf16[4,16,704]{2,1,0:T(8,128)(2,1)S(1)}, u32[]{:S(2)}, u32[]{:S(2)}) collective-permute-start(bf16[4,16,704]{2,1,0:T(8,128)(2,1)S(1)} %get-tuple-element.33), channel_id=1, source_target_pairs={{2,100},{3,101},{4,102},{5,103},{6,104},{7,105},{0,106},{1,107},{1... | collective-permute-start | bytes 270344 | tf_op jit(solution)/shard_map/ppermute | solution.py:558
  34.8 14.3 %copy-start = (bf16[704,2112]{1,0:T(8,128)(2,1)S(1)}, bf16[704,2112]{1,0:T(8,128)(2,1)}, u32[]{:S(2)}) copy-start(bf16[704,2112]{1,0:T(8,128)(2,1)} %refs_7_.5) | copy-start | bytes 8921092
  34.8 14.3 %copy-start.1 = (bf16[704,704]{1,0:T(8,128)(2,1)S(1)}, bf16[704,704]{1,0:T(8,128)(2,1)}, u32[]{:S(2)}) copy-start(bf16[704,704]{1,0:T(8,128)(2,1)} %refs_8_.5) | copy-start | bytes 2973700
  34.8 14.3 %copy-start.6 = (f32[16,704]{1,0:T(8,128)S(1)}, f32[16,704]{1,0:T(8,128)}, u32[]{:S(2)}) copy-start(f32[16,704]{1,0:T(8,128)} %refs_5_.3) | copy-start | bytes 135172
  34.8 14.3 %copy-start.8 = (f32[704]{0:T(1024)S(1)}, f32[704]{0:T(1024)}, u32[]{:S(2)}) copy-start(f32[704]{0:T(1024)} %refs_6_.5) | copy-start | bytes 8452
  34.8 14.3 %copy-start.12 = (s32[16]{0:T(128)S(1)}, s32[16]{0:T(128)}, u32[]{:S(2)}) copy-start(s32[16]{0:T(128)} %rank.3) | copy-start | bytes 196
  43.3 13.5 %collective-permute-start.11 = (bf16[4,16,704]{2,1,0:T(8,128)(2,1)S(1)}, bf16[4,16,704]{2,1,0:T(8,128)(2,1)S(1)}, u32[]{:S(2)}, u32[]{:S(2)}) collective-permute-start(bf16[4,16,704]{2,1,0:T(8,128)(2,1)S(1)} %get-tuple-element.42), channel_id=1, source_target_pairs={{2,0},{3,1},{4,2},{5,3},{6,4},{7,5},{0,6},{1,7},{10,8},{11,9},{12,... | collective-permute-start | bytes 270344 | tf_op jit(solution)/shard_map/ppermute | solution.py:558
  47.2 13.5 %collective-permute-start.12 = (bf16[4,16,704]{2,1,0:T(8,128)(2,1)S(1)}, bf16[4,16,704]{2,1,0:T(8,128)(2,1)S(1)}, u32[]{:S(2)}, u32[]{:S(2)}) collective-permute-start(bf16[4,16,704]{2,1,0:T(8,128)(2,1)S(1)} %get-tuple-element.43), channel_id=1, source_target_pairs={{2,33},{3,34},{4,35},{5,32},{6,37},{7,38},{0,39},{1,36},{10,41},{1... | collective-permute-start | bytes 270344 | tf_op jit(solution)/shard_map/ppermute | solution.py:558
  47.2 14.9 %collective-permute-start.13 = (bf16[4,16,704]{2,1,0:T(8,128)(2,1)S(1)}, bf16[4,16,704]{2,1,0:T(8,128)(2,1)S(1)}, u32[]{:S(2)}, u32[]{:S(2)}) collective-permute-start(bf16[4,16,704]{2,1,0:T(8,128)(2,1)S(1)} %get-tuple-element.44), channel_id=1, source_target_pairs={{2,68},{3,69},{4,70},{5,71},{6,72},{7,73},{0,74},{1,75},{10,76},{1... | collective-permute-start | bytes 270344 | tf_op jit(solution)/shard_map/ppermute | solution.py:558
  47.3 14.8 %collective-permute-start.14 = (bf16[4,16,704]{2,1,0:T(8,128)(2,1)S(1)}, bf16[4,16,704]{2,1,0:T(8,128)(2,1)S(1)}, u32[]{:S(2)}, u32[]{:S(2)}) collective-permute-start(bf16[4,16,704]{2,1,0:T(8,128)(2,1)S(1)} %get-tuple-element.45), channel_id=1, source_target_pairs={{2,101},{3,102},{4,103},{5,100},{6,105},{7,106},{0,107},{1,104},{1... | collective-permute-start | bytes 270344 | tf_op jit(solution)/shard_map/ppermute | solution.py:558
  53.0 15.0 %collective-permute-start.8 = (bf16[4,16,704]{2,1,0:T(8,128)(2,1)S(1)}, bf16[4,16,704]{2,1,0:T(8,128)(2,1)S(1)}, u32[]{:S(2)}, u32[]{:S(2)}) collective-permute-start(bf16[4,16,704]{2,1,0:T(8,128)(2,1)S(1)} %get-tuple-element.39), channel_id=1, source_target_pairs={{0,96},{32,0},{64,32},{96,64},{1,97},{33,1},{65,33},{97,65},{2,98}... | collective-permute-start | bytes 270344 | tf_op jit(solution)/shard_map/ppermute | solution.py:564
  56.8 12.0 %collective-permute-start.9 = (bf16[4,16,704]{2,1,0:T(8,128)(2,1)S(1)}, bf16[4,16,704]{2,1,0:T(8,128)(2,1)S(1)}, u32[]{:S(2)}, u32[]{:S(2)}) collective-permute-start(bf16[4,16,704]{2,1,0:T(8,128)(2,1)S(1)} %get-tuple-element.40), channel_id=1, source_target_pairs={{0,64},{32,96},{64,0},{96,32},{1,65},{33,97},{65,1},{97,33},{2,66}... | collective-permute-start | bytes 270344 | tf_op jit(solution)/shard_map/ppermute | solution.py:564
  60.7 8.1 %collective-permute-start.10 = (bf16[4,16,704]{2,1,0:T(8,128)(2,1)S(1)}, bf16[4,16,704]{2,1,0:T(8,128)(2,1)S(1)}, u32[]{:S(2)}, u32[]{:S(2)}) collective-permute-start(bf16[4,16,704]{2,1,0:T(8,128)(2,1)S(1)} %get-tuple-element.41), channel_id=1, source_target_pairs={{0,32},{32,64},{64,96},{96,0},{1,33},{33,65},{65,97},{97,1},{2,34}... | collective-permute-start | bytes 270344 | tf_op jit(solution)/shard_map/ppermute | solution.py:564
  65.9 5.2 %collective-permute-start.15 = (bf16[4,16,704]{2,1,0:T(8,128)(2,1)S(1)}, bf16[4,16,704]{2,1,0:T(8,128)(2,1)S(1)}, u32[]{:S(2)}, u32[]{:S(2)}) collective-permute-start(bf16[4,16,704]{2,1,0:T(8,128)(2,1)S(1)} %get-tuple-element.48), channel_id=1, source_target_pairs={{0,96},{32,0},{64,32},{96,64},{1,97},{33,1},{65,33},{97,65},{2,98}... | collective-permute-start | bytes 270344 | tf_op jit(solution)/shard_map/ppermute | solution.py:564
  67.8 6.2 %collective-permute-start.16 = (bf16[4,16,704]{2,1,0:T(8,128)(2,1)S(1)}, bf16[4,16,704]{2,1,0:T(8,128)(2,1)S(1)}, u32[]{:S(2)}, u32[]{:S(2)}) collective-permute-start(bf16[4,16,704]{2,1,0:T(8,128)(2,1)S(1)} %get-tuple-element.49), channel_id=1, source_target_pairs={{0,64},{32,96},{64,0},{96,32},{1,65},{33,97},{65,1},{97,33},{2,66}... | collective-permute-start | bytes 270344 | tf_op jit(solution)/shard_map/ppermute | solution.py:564
  68.0 6.9 %collective-permute-start.17 = (bf16[4,16,704]{2,1,0:T(8,128)(2,1)S(1)}, bf16[4,16,704]{2,1,0:T(8,128)(2,1)S(1)}, u32[]{:S(2)}, u32[]{:S(2)}) collective-permute-start(bf16[4,16,704]{2,1,0:T(8,128)(2,1)S(1)} %get-tuple-element.50), channel_id=1, source_target_pairs={{0,32},{32,64},{64,96},{96,0},{1,33},{33,65},{65,97},{97,1},{2,34}... | collective-permute-start | bytes 270344 | tf_op jit(solution)/shard_map/ppermute | solution.py:564

commit v5 on v4

--- a/solution.py
+++ b/solution.py
@@ -115,7 +115,7 @@
             right[d] = jnp.concatenate([work[i, :SHIFT, :] for i in lines], axis=0).astype(BF16)
 
 
-def bias_kernel(first, second, _, out, table):
+def bias_kernel(first, second, out, table):
     units = first.shape[1]
     heads = second.shape[0]
     layer = jnp.concatenate([first[...], jnp.zeros((6, units), F32)], axis=0).T
@@ -454,7 +454,6 @@
         10**10,
         tile_bytes * 2,
         "pack",
-        4,
     )(pixels)
     low, high, low_right, high_right = (
         lax.ppermute(piece, plane, routes[name])
@@ -463,13 +462,12 @@
     bias = call(
         bias_kernel,
         jax.ShapeDtypeStruct((heads, POSITIONS, PAIR), F32),
-        [VMEM] * 3,
+        [VMEM, VMEM],
         [pltpu.VMEM((WINDOW * 32, 128), F32)],
         10**9,
         10**6,
         "position_bias",
-        6,
-    )(bias_network_first, bias_network_second.T, window_query_key_value_weight)
+    )(bias_network_first, bias_network_second.T)
 
     projected = [
         pltpu.VMEM((features, token_total), BF16),

time: 76.2 us -> 75 us (0.984)
  Pallas kernels: 29.4 us -> 26.6 us
  local copies, waits for them, and re-layouts: 1.35 us -> 3.08 us
    unnamed x30 -> x32, local copies, waits for them, and re-layouts: 1.35 us -> 3.08 us
    pallas_call x1, Pallas kernels: 4.99 us -> 4.03 us  [inner_layer(): call(inner_settle, [part_shape] * 4 + [token_shape], [SMEM] + [VMEM] * 8,...]
  transfers between devices with their start and end apart: 18 -> 18, of which waited for: 5 -> 5; matrix products, arithmetic and copies ran while one was open for 0% -> 0% of each run, Pallas kernels for 36% -> 34%
where the time goes in v5:
time: 75 us; the launch traced here: 74.8 us
  starting transfers between devices  34.4 us (46%)
  Pallas kernels  26.6 us (35%)
  waiting for transfers between devices  10.5 us (14%)
  local copies, waits for them, and re-layouts  3.08 us (4%)
    ppermute x8, starting transfers between devices, to_dates(): lax.ppermute(piece, space, routes[kind][k])  16 us
    ppermute x6, starting transfers between devices, to_home(): lax.ppermute(piece, 'date', [(i, (i - k) % date_axis) for i in range(date...  11.9 us
    pallas_call x1, Pallas kernels, straddle_layer(): call(straddle_window, [part_shape] * 4 + [token_shape], [SMEM] * 4 + [VME...  7.83 us
    pallas_call x2, Pallas kernels, time_layer(): call(functools.partial(time_kernel, features // heads), [part_shape] * 4...  7.62 us
    ppermute x4, starting transfers between devices, local(): lax.ppermute(piece, plane, routes[name])  6.5 us
    ppermute x6, waiting for transfers between devices, to_home(): lax.ppermute(piece, 'date', [(i, (i - k) % date_axis) for i in range(date...  6.1 us
    ppermute x4, waiting for transfers between devices, local(): lax.ppermute(piece, plane, routes[name])  4.38 us
    pallas_call x1, Pallas kernels, inner_layer(): call(inner_settle, [part_shape] * 4 + [token_shape], [SMEM] + [VMEM] * 8,...  4.03 us
  transfers between devices with their start and end apart: 18, of which 5 were waited for; matrix products, arithmetic and copies ran while one was open for 0% of the time, Pallas kernels for 34%

profile of v5, /device:TPU:0, one launch (start us, length us, event | category | flops | bytes accessed | tf_op | source)
XLA Modules:
  0.0 74.8 jit_solution(13283002835771260307)
XLA Ops:
  0.0 1.1 %copy-done.12 = bf16[4,8,16,704]{3,2,1,0:T(8,128)(2,1)S(1)} copy-done((bf16[4,8,16,704]{3,2,1,0:T(8,128)(2,1)S(1)}, bf16[4,8,16,704]{3,2,1,0:T(8,128)(2,1)}, u32[]{:S(2)}) %copy-start.12) | copy-done | bytes 720920
  1.1 0.3 pack.1
  1.5 0.0 copy-start.15
  1.5 1.7 %collective-permute-start = (bf16[4,48,704]{2,1,0:T(8,128)(2,1)S(1)}, bf16[4,48,704]{2,1,0:T(8,128)(2,1)S(1)}, u32[]{:S(2)}, u32[]{:S(2)}) collective-permute-start(bf16[4,48,704]{2,1,0:T(8,128)(2,1)S(1)} %get-tuple-element.28), channel_id=1, source_target_pairs={{0,2},{1,3},{2,4},{3,5},{4,6},{5,7},{6,0},{7,1},{8,10},{9,11},{10,... | collective-permute-start | bytes 811016 | tf_op jit(solution)/shard_map/ppermute | solution.py:459
  3.2 3.9 %collective-permute-start.1 = (bf16[4,48,704]{2,1,0:T(8,128)(2,1)S(1)}, bf16[4,48,704]{2,1,0:T(8,128)(2,1)S(1)}, u32[]{:S(2)}, u32[]{:S(2)}) collective-permute-start(bf16[4,48,704]{2,1,0:T(8,128)(2,1)S(1)} %get-tuple-element.29), channel_id=1, source_target_pairs={{4,2},{5,3},{6,4},{7,5},{8,6},{9,7},{10,0},{11,1},{12,10},{13,11},... | collective-permute-start | bytes 811016 | tf_op jit(solution)/shard_map/ppermute | solution.py:459
  7.1 0.0 collective-permute-start.6
  7.1 0.9 %collective-permute-start.7 = (bf16[4,16,704]{2,1,0:T(8,128)(2,1)S(1)}, bf16[4,16,704]{2,1,0:T(8,128)(2,1)S(1)}, u32[]{:S(2)}, u32[]{:S(2)}) collective-permute-start(bf16[4,16,704]{2,1,0:T(8,128)(2,1)S(1)} %get-tuple-element.35), channel_id=1, source_target_pairs={{5,2},{6,3},{7,4},{4,5},{9,6},{10,7},{11,0},{8,1},{13,10},{14,11},... | collective-permute-start | bytes 270344 | tf_op jit(solution)/shard_map/ppermute | solution.py:459
  8.0 0.0 copy-done.13
  8.0 0.0 copy-done.14
  8.0 1.8 %position_bias.1.bias.refs_5_ = f32[22,64,128]{2,1,0:T(8,128)S(1)} custom-call(f32[2,512]{1,0:T(2,128)S(1)} %copy-done.14, f32[22,512]{1,0:T(8,128)S(1)} %bitcast.7), custom_call_target="tpu_custom_call" | custom-call | flops 1000000000 | bytes 1000000 | tf_op jit(solution)/shard_map/position_bias/pallas_call | solution.py:462
  9.8 0.0 copy-start.2
  9.8 0.0 copy-start.4
  9.8 0.0 copy-start.7
  9.9 0.0 copy-start.8
  9.9 2.1 %collective-permute-done.low.refs_0_ = bf16[4,48,704]{2,1,0:T(8,128)(2,1)S(1)} collective-permute-done((bf16[4,48,704]{2,1,0:T(8,128)(2,1)S(1)}, bf16[4,48,704]{2,1,0:T(8,128)(2,1)S(1)}, u32[]{:S(2)}, u32[]{:S(2)}) %collective-permute-start) | collective-permute-done | bytes 270368 | tf_op jit(solution)/shard_map/ppermute | solution.py:459
  12.0 2.3 %collective-permute-done.1.high.refs_1_ = bf16[4,48,704]{2,1,0:T(8,128)(2,1)S(1)} collective-permute-done((bf16[4,48,704]{2,1,0:T(8,128)(2,1)S(1)}, bf16[4,48,704]{2,1,0:T(8,128)(2,1)S(1)}, u32[]{:S(2)}, u32[]{:S(2)}) %collective-permute-start.1) | collective-permute-done | bytes 270368 | tf_op jit(solution)/shard_map/ppermute | solution.py:459
  14.2 0.0 copy-done.15
  14.2 1.9 %copy-done.10 = bf16[704,2112]{1,0:T(8,128)(2,1)S(1)} copy-done((bf16[704,2112]{1,0:T(8,128)(2,1)S(1)}, bf16[704,2112]{1,0:T(8,128)(2,1)}, u32[]{:S(2)}) %copy-start.10) | copy-done | bytes 2973720
  16.1 3.8 %inner_attention.1.mixed_heads = bf16[704,256]{1,0:T(8,128)(2,1)S(1)} custom-call(bf16[4,48,704]{2,1,0:T(8,128)(2,1)S(1)} %collective-permute-done.low.refs_0_, bf16[4,48,704]{2,1,0:T(8,128)(2,1)S(1)} %collective-permute-done.1.high.refs_1_, s32[1]{0:T(128)} %bitcast.1.last_row, f32[22]{0:T(128)S(1)} %copy-done.15, ...), custom_call_target="tpu_custom_call" | custom-call | flops 1522532352 | bytes 4000000 | tf_op jit(solution)/shard_map/inner_attention/pallas_call | solution.py:491
  20.0 0.0 copy-done.3
  20.0 0.0 copy-done.2
  20.0 0.0 copy-done.4
  20.0 0.0 copy-done.7
  20.0 0.0 copy-done.8
  20.0 0.0 copy-start.11
  20.0 4.0 %inner_settle.1 = (bf16[4,16,704]{2,1,0:T(8,128)(2,1)S(1)}, bf16[4,16,704]{2,1,0:T(8,128)(2,1)S(1)}, bf16[4,16,704]{2,1,0:T(8,128)(2,1)S(1)}, bf16[4,16,704]{2,1,0:T(8,128)(2,1)S(1)}, f32[8,128]{1,0:T(8,128)S(1)}) custom-call(s32[1]{0:T(128)} %bitcast.place, bf16[4,48,704]{2,1,0:T(8,128)(2,1)S(1)} %collective-permute-done.low.refs_0_, ...), custom_call_target="tpu_custom_call" | custom-call | flops 2283798528 | bytes 9000000 | tf_op jit(solution)/shard_map/inner_settle/pallas_call | solution.py:501
  24.1 2.8 %collective-permute-start.2 = (bf16[4,16,704]{2,1,0:T(8,128)(2,1)S(1)}, bf16[4,16,704]{2,1,0:T(8,128)(2,1)S(1)}, u32[]{:S(2)}, u32[]{:S(2)}) collective-permute-start(bf16[4,16,704]{2,1,0:T(8,128)(2,1)S(1)} %get-tuple-element.30), channel_id=1, source_target_pairs={{2,0},{3,1},{4,2},{5,3},{6,4},{7,5},{0,6},{1,7},{10,8},{11,9},{12,... | collective-permute-start | bytes 270344 | tf_op jit(solution)/shard_map/ppermute | solution.py:556
  26.9 1.4 %collective-permute-start.3 = (bf16[4,16,704]{2,1,0:T(8,128)(2,1)S(1)}, bf16[4,16,704]{2,1,0:T(8,128)(2,1)S(1)}, u32[]{:S(2)}, u32[]{:S(2)}) collective-permute-start(bf16[4,16,704]{2,1,0:T(8,128)(2,1)S(1)} %get-tuple-element.31), channel_id=1, source_target_pairs={{2,32},{3,33},{4,34},{5,35},{6,36},{7,37},{0,38},{1,39},{10,40},{1... | collective-permute-start | bytes 270344 | tf_op jit(solution)/shard_map/ppermute | solution.py:556
  28.3 5.3 %collective-permute-start.4 = (bf16[4,16,704]{2,1,0:T(8,128)(2,1)S(1)}, bf16[4,16,704]{2,1,0:T(8,128)(2,1)S(1)}, u32[]{:S(2)}, u32[]{:S(2)}) collective-permute-start(bf16[4,16,704]{2,1,0:T(8,128)(2,1)S(1)} %get-tuple-element.32), channel_id=1, source_target_pairs={{2,68},{3,69},{4,70},{5,71},{6,72},{7,73},{0,74},{1,75},{10,76},{1... | collective-permute-start | bytes 270344 | tf_op jit(solution)/shard_map/ppermute | solution.py:556
  33.6 0.0 collective-permute-done.6.refs_2_
  33.6 0.6 collective-permute-start.5
  34.2 0.0 collective-permute-done.7.refs_3_
  34.2 0.0 copy-start.5
  34.3 0.0 copy-start.6
  34.3 0.0 copy-start.9
  34.3 7.8 %straddle_window.1 = (bf16[4,16,704]{2,1,0:T(8,128)(2,1)S(1)}, bf16[4,16,704]{2,1,0:T(8,128)(2,1)S(1)}, bf16[4,16,704]{2,1,0:T(8,128)(2,1)S(1)}, bf16[4,16,704]{2,1,0:T(8,128)(2,1)S(1)}, f32[8,128]{1,0:T(8,128)S(1)}) custom-call(s32[1]{0:T(128)} %bitcast.place, s32[1]{0:T(128)} %bitcast.1.last_row, s32[1]{0:T(128)} %bitcast.4.last_col, f32[22]{0:T(128)S(1)} %copy-done.15, ...), custom_call_target="tpu_custom_call" | custom-call | flops 3806330880 | bytes 13000000 | tf_op jit(solution)/shard_map/straddle_window/pallas_call | solution.py:513
  42.1 3.8 %collective-permute-start.11 = (bf16[4,16,704]{2,1,0:T(8,128)(2,1)S(1)}, bf16[4,16,704]{2,1,0:T(8,128)(2,1)S(1)}, u32[]{:S(2)}, u32[]{:S(2)}) collective-permute-start(bf16[4,16,704]{2,1,0:T(8,128)(2,1)S(1)} %get-tuple-element.42), channel_id=1, source_target_pairs={{2,0},{3,1},{4,2},{5,3},{6,4},{7,5},{0,6},{1,7},{10,8},{11,9},{12,... | collective-permute-start | bytes 270344 | tf_op jit(solution)/shard_map/ppermute | solution.py:556
  45.9 0.0 collective-permute-done.2.refs_0_
  45.9 0.0 collective-permute-start.12
  45.9 0.0 collective-permute-done.3.refs_1_
  45.9 0.1 collective-permute-start.13
  46.0 0.0 collective-permute-done.4.refs_2_
  46.0 1.9 %collective-permute-start.14 = (bf16[4,16,704]{2,1,0:T(8,128)(2,1)S(1)}, bf16[4,16,704]{2,1,0:T(8,128)(2,1)S(1)}, u32[]{:S(2)}, u32[]{:S(2)}) collective-permute-start(bf16[4,16,704]{2,1,0:T(8,128)(2,1)S(1)} %get-tuple-element.45), channel_id=1, source_target_pairs={{2,101},{3,102},{4,103},{5,100},{6,105},{7,106},{0,107},{1,104},{1... | collective-permute-start | bytes 270344 | tf_op jit(solution)/shard_map/ppermute | solution.py:556
  48.0 0.0 collective-permute-done.5.refs_3_
  48.0 0.0 copy-done
  48.0 3.8 %time_layer.2 = (bf16[4,16,704]{2,1,0:T(8,128)(2,1)S(1)}, bf16[4,16,704]{2,1,0:T(8,128)(2,1)S(1)}, bf16[4,16,704]{2,1,0:T(8,128)(2,1)S(1)}, bf16[4,16,704]{2,1,0:T(8,128)(2,1)S(1)}, f32[8,128]{1,0:T(8,128)S(1)}) custom-call(s32[1]{0:T(128)} %bitcast.place, s32[16]{0:T(128)S(1)} %copy-done.9, bf16[4,16,704]{2,1,0:T(8,128)(2,1)S(1)} %collective-permute-done.2.refs_0_, ...), custom_call_target="tpu_custom_call" | custom-call | flops 1015021568 | bytes 5000000 | tf_op jit(solution)/shard_map/time_layer/pallas_call | solution.py:535
  51.8 3.7 %collective-permute-start.8 = (bf16[4,16,704]{2,1,0:T(8,128)(2,1)S(1)}, bf16[4,16,704]{2,1,0:T(8,128)(2,1)S(1)}, u32[]{:S(2)}, u32[]{:S(2)}) collective-permute-start(bf16[4,16,704]{2,1,0:T(8,128)(2,1)S(1)} %get-tuple-element.39), channel_id=1, source_target_pairs={{0,96},{32,0},{64,32},{96,64},{1,97},{33,1},{65,33},{97,65},{2,98}... | collective-permute-start | bytes 270344 | tf_op jit(solution)/shard_map/ppermute | solution.py:562
  55.6 0.0 collective-permute-done.11.refs_0_
  55.6 3.9 %collective-permute-start.9 = (bf16[4,16,704]{2,1,0:T(8,128)(2,1)S(1)}, bf16[4,16,704]{2,1,0:T(8,128)(2,1)S(1)}, u32[]{:S(2)}, u32[]{:S(2)}) collective-permute-start(bf16[4,16,704]{2,1,0:T(8,128)(2,1)S(1)} %get-tuple-element.40), channel_id=1, source_target_pairs={{0,64},{32,96},{64,0},{96,32},{1,65},{33,97},{65,1},{97,33},{2,66}... | collective-permute-start | bytes 270344 | tf_op jit(solution)/shard_map/ppermute | solution.py:562
  59.5 0.0 collective-permute-done.12.refs_1_
  59.5 1.3 %collective-permute-start.10 = (bf16[4,16,704]{2,1,0:T(8,128)(2,1)S(1)}, bf16[4,16,704]{2,1,0:T(8,128)(2,1)S(1)}, u32[]{:S(2)}, u32[]{:S(2)}) collective-permute-start(bf16[4,16,704]{2,1,0:T(8,128)(2,1)S(1)} %get-tuple-element.41), channel_id=1, source_target_pairs={{0,32},{32,64},{64,96},{96,0},{1,33},{33,65},{65,97},{97,1},{2,34}... | collective-permute-start | bytes 270344 | tf_op jit(solution)/shard_map/ppermute | solution.py:562
  60.8 0.0 collective-permute-done.13.refs_2_
  60.8 0.0 collective-permute-done.14.refs_3_
  60.8 3.8 %time_layer.3 = (bf16[4,16,704]{2,1,0:T(8,128)(2,1)S(1)}, bf16[4,16,704]{2,1,0:T(8,128)(2,1)S(1)}, bf16[4,16,704]{2,1,0:T(8,128)(2,1)S(1)}, bf16[4,16,704]{2,1,0:T(8,128)(2,1)S(1)}, f32[8,128]{1,0:T(8,128)}) custom-call(s32[1]{0:T(128)} %bitcast.place, s32[16]{0:T(128)S(1)} %copy-done.9, bf16[4,16,704]{2,1,0:T(8,128)(2,1)S(1)} %collective-permute-done.11.refs_0_, ...), custom_call_target="tpu_custom_call" | custom-call | flops 1015021568 | bytes 5000000 | tf_op jit(solution)/shard_map/time_layer/pallas_call | solution.py:535
  64.6 2.0 %collective-permute-start.15 = (bf16[4,16,704]{2,1,0:T(8,128)(2,1)S(1)}, bf16[4,16,704]{2,1,0:T(8,128)(2,1)S(1)}, u32[]{:S(2)}, u32[]{:S(2)}) collective-permute-start(bf16[4,16,704]{2,1,0:T(8,128)(2,1)S(1)} %get-tuple-element.48), channel_id=1, source_target_pairs={{0,96},{32,0},{64,32},{96,64},{1,97},{33,1},{65,33},{97,65},{2,98}... | collective-permute-start | bytes 270344 | tf_op jit(solution)/shard_map/ppermute | solution.py:562
  66.6 0.2 collective-permute-start.16
  66.8 0.0 collective-permute-done.8.refs_1_
  66.8 0.8 %collective-permute-start.17 = (bf16[4,16,704]{2,1,0:T(8,128)(2,1)S(1)}, bf16[4,16,704]{2,1,0:T(8,128)(2,1)S(1)}, u32[]{:S(2)}, u32[]{:S(2)}) collective-permute-start(bf16[4,16,704]{2,1,0:T(8,128)(2,1)S(1)} %get-tuple-element.50), channel_id=1, source_target_pairs={{0,32},{32,64},{64,96},{96,0},{1,33},{33,65},{65,97},{97,1},{2,34}... | collective-permute-start | bytes 270344 | tf_op jit(solution)/shard_map/ppermute | solution.py:562
  67.6 0.0 collective-permute-done.9.refs_2_
  67.6 0.0 collective-permute-done.10.refs_3_
  67.6 2.3 %collective-permute-done.15.refs_5_ = bf16[4,16,704]{2,1,0:T(8,128)(2,1)S(1)} collective-permute-done((bf16[4,16,704]{2,1,0:T(8,128)(2,1)S(1)}, bf16[4,16,704]{2,1,0:T(8,128)(2,1)S(1)}, u32[]{:S(2)}, u32[]{:S(2)}) %collective-permute-start.15) | collective-permute-done | bytes 90144 | tf_op jit(solution)/shard_map/ppermute | solution.py:562
  69.8 3.0 %collective-permute-done.16.refs_6_ = bf16[4,16,704]{2,1,0:T(8,128)(2,1)S(1)} collective-permute-done((bf16[4,16,704]{2,1,0:T(8,128)(2,1)S(1)}, bf16[4,16,704]{2,1,0:T(8,128)(2,1)S(1)}, u32[]{:S(2)}, u32[]{:S(2)}) %collective-permute-start.16) | collective-permute-done | bytes 90144 | tf_op jit(solution)/shard_map/ppermute | solution.py:562
  72.9 0.8 %collective-permute-done.17.refs_7_ = bf16[4,16,704]{2,1,0:T(8,128)(2,1)S(1)} collective-permute-done((bf16[4,16,704]{2,1,0:T(8,128)(2,1)S(1)}, bf16[4,16,704]{2,1,0:T(8,128)(2,1)S(1)}, u32[]{:S(2)}, u32[]{:S(2)}) %collective-permute-start.17) | collective-permute-done | bytes 90144 | tf_op jit(solution)/shard_map/ppermute | solution.py:562
  73.7 1.1 %assemble.1 = bf16[4,8,16,704]{3,2,1,0:T(8,128)(2,1)} custom-call(s32[1]{0:T(128)} %bitcast.place, bf16[4,16,704]{2,1,0:T(8,128)(2,1)S(1)} %get-tuple-element.38.refs_0_, bf16[4,16,704]{2,1,0:T(8,128)(2,1)S(1)} %collective-permute-done.8.refs_1_, bf16[4,16,704]{2,1,0:T(8,128)(2,1)S(1)} %collective-permute-done.9.refs_2_, ...), custom_call_target="tpu_custom_call" | custom-call | bytes 1441792 | tf_op jit(solution)/shard_map/assemble/pallas_call | solution.py:574
  (12 shorter events, 0.0 us)
Async XLA Ops:
  0.0 1.1 %copy-start.12 = (bf16[4,8,16,704]{3,2,1,0:T(8,128)(2,1)S(1)}, bf16[4,8,16,704]{3,2,1,0:T(8,128)(2,1)}, u32[]{:S(2)}) copy-start(bf16[4,8,16,704]{3,2,1,0:T(8,128)(2,1)} %pixels.1) | copy-start | bytes 2162692
  1.1 6.8 %copy-start.13 = (f32[512,22]{0,1:T(8,128)S(1)}, f32[512,22]{0,1:T(8,128)}, u32[]{:S(2)}) copy-start(f32[512,22]{0,1:T(8,128)} %param.19) | copy-start | bytes 135172
  1.1 6.8 %copy-start.14 = (f32[2,512]{1,0:T(2,128)S(1)}, f32[2,512]{1,0:T(2,128)}, u32[]{:S(2)}) copy-start(f32[2,512]{1,0:T(2,128)} %first.1) | copy-start | bytes 12292
  1.5 12.8 %copy-start.15 = (f32[22]{0:T(128)S(1)}, f32[22]{0:T(128)}, u32[]{:S(2)}) copy-start(f32[22]{0:T(128)} %scale.3) | copy-start | bytes 268
  1.5 10.5 %collective-permute-start = (bf16[4,48,704]{2,1,0:T(8,128)(2,1)S(1)}, bf16[4,48,704]{2,1,0:T(8,128)(2,1)S(1)}, u32[]{:S(2)}, u32[]{:S(2)}) collective-permute-start(bf16[4,48,704]{2,1,0:T(8,128)(2,1)S(1)} %get-tuple-element.28), channel_id=1, source_target_pairs={{0,2},{1,3},{2,4},{3,5},{4,6},{5,7},{6,0},{7,1},{8,10},{9,11},{10,... | collective-permute-start | bytes 811016 | tf_op jit(solution)/shard_map/ppermute | solution.py:459
  3.2 11.0 %collective-permute-start.1 = (bf16[4,48,704]{2,1,0:T(8,128)(2,1)S(1)}, bf16[4,48,704]{2,1,0:T(8,128)(2,1)S(1)}, u32[]{:S(2)}, u32[]{:S(2)}) collective-permute-start(bf16[4,48,704]{2,1,0:T(8,128)(2,1)S(1)} %get-tuple-element.29), channel_id=1, source_target_pairs={{4,2},{5,3},{6,4},{7,5},{8,6},{9,7},{10,0},{11,1},{12,10},{13,11},... | collective-permute-start | bytes 811016 | tf_op jit(solution)/shard_map/ppermute | solution.py:459
  7.1 26.5 %collective-permute-start.6 = (bf16[4,16,704]{2,1,0:T(8,128)(2,1)S(1)}, bf16[4,16,704]{2,1,0:T(8,128)(2,1)S(1)}, u32[]{:S(2)}, u32[]{:S(2)}) collective-permute-start(bf16[4,16,704]{2,1,0:T(8,128)(2,1)S(1)} %get-tuple-element.34), channel_id=1, source_target_pairs={{1,2},{2,3},{3,4},{0,5},{5,6},{6,7},{7,0},{4,1},{9,10},{10,11},{11... | collective-permute-start | bytes 270344 | tf_op jit(solution)/shard_map/ppermute | solution.py:459
  7.1 27.2 %collective-permute-start.7 = (bf16[4,16,704]{2,1,0:T(8,128)(2,1)S(1)}, bf16[4,16,704]{2,1,0:T(8,128)(2,1)S(1)}, u32[]{:S(2)}, u32[]{:S(2)}) collective-permute-start(bf16[4,16,704]{2,1,0:T(8,128)(2,1)S(1)} %get-tuple-element.35), channel_id=1, source_target_pairs={{5,2},{6,3},{7,4},{4,5},{9,6},{10,7},{11,0},{8,1},{13,10},{14,11},... | collective-permute-start | bytes 270344 | tf_op jit(solution)/shard_map/ppermute | solution.py:459
  8.0 12.0 %copy-start.3 = (bf16[2816,704]{0,1:T(8,128)(2,1)S(1)}, bf16[2816,704]{0,1:T(8,128)(2,1)}, u32[]{:S(2)}) copy-start(bf16[2816,704]{0,1:T(8,128)(2,1)} %param.23) | copy-start | bytes 11894788
  9.8 10.2 %copy-start.2 = (bf16[704,2816]{1,0:T(8,128)(2,1)S(1)}, bf16[704,2816]{1,0:T(8,128)(2,1)}, u32[]{:S(2)}) copy-start(bf16[704,2816]{1,0:T(8,128)(2,1)} %refs_8_.3) | copy-start | bytes 11894788
  9.8 10.1 %copy-start.4 = (bf16[704,704]{1,0:T(8,128)(2,1)S(1)}, bf16[704,704]{1,0:T(8,128)(2,1)}, u32[]{:S(2)}) copy-start(bf16[704,704]{1,0:T(8,128)(2,1)} %refs_7_.3) | copy-start | bytes 2973700
  9.8 10.1 %copy-start.7 = (f32[704]{0:T(1024)S(1)}, f32[704]{0:T(1024)}, u32[]{:S(2)}) copy-start(f32[704]{0:T(1024)} %refs_10_.1) | copy-start | bytes 8452
  9.9 10.1 %copy-start.8 = (f32[704]{0:T(1024)S(1)}, f32[704]{0:T(1024)}, u32[]{:S(2)}) copy-start(f32[704]{0:T(1024)} %refs_11_.1) | copy-start | bytes 8452
  14.2 1.9 %copy-start.10 = (bf16[704,2112]{1,0:T(8,128)(2,1)S(1)}, bf16[704,2112]{1,0:T(8,128)(2,1)}, u32[]{:S(2)}) copy-start(bf16[704,2112]{1,0:T(8,128)(2,1)} %refs_6_.3) | copy-start | bytes 8921092
  20.0 14.2 %copy-start.11 = (bf16[704,2112]{1,0:T(8,128)(2,1)S(1)}, bf16[704,2112]{1,0:T(8,128)(2,1)}, u32[]{:S(2)}) copy-start(bf16[704,2112]{1,0:T(8,128)(2,1)} %refs_6_.3) | copy-start | bytes 8921092
  24.1 21.9 %collective-permute-start.2 = (bf16[4,16,704]{2,1,0:T(8,128)(2,1)S(1)}, bf16[4,16,704]{2,1,0:T(8,128)(2,1)S(1)}, u32[]{:S(2)}, u32[]{:S(2)}) collective-permute-start(bf16[4,16,704]{2,1,0:T(8,128)(2,1)S(1)} %get-tuple-element.30), channel_id=1, source_target_pairs={{2,0},{3,1},{4,2},{5,3},{6,4},{7,5},{0,6},{1,7},{10,8},{11,9},{12,... | collective-permute-start | bytes 270344 | tf_op jit(solution)/shard_map/ppermute | solution.py:556
  26.9 19.1 %collective-permute-start.3 = (bf16[4,16,704]{2,1,0:T(8,128)(2,1)S(1)}, bf16[4,16,704]{2,1,0:T(8,128)(2,1)S(1)}, u32[]{:S(2)}, u32[]{:S(2)}) collective-permute-start(bf16[4,16,704]{2,1,0:T(8,128)(2,1)S(1)} %get-tuple-element.31), channel_id=1, source_target_pairs={{2,32},{3,33},{4,34},{5,35},{6,36},{7,37},{0,38},{1,39},{10,40},{1... | collective-permute-start | bytes 270344 | tf_op jit(solution)/shard_map/ppermute | solution.py:556
  28.3 17.7 %collective-permute-start.4 = (bf16[4,16,704]{2,1,0:T(8,128)(2,1)S(1)}, bf16[4,16,704]{2,1,0:T(8,128)(2,1)S(1)}, u32[]{:S(2)}, u32[]{:S(2)}) collective-permute-start(bf16[4,16,704]{2,1,0:T(8,128)(2,1)S(1)} %get-tuple-element.32), channel_id=1, source_target_pairs={{2,68},{3,69},{4,70},{5,71},{6,72},{7,73},{0,74},{1,75},{10,76},{1... | collective-permute-start | bytes 270344 | tf_op jit(solution)/shard_map/ppermute | solution.py:556
  33.6 14.4 %collective-permute-start.5 = (bf16[4,16,704]{2,1,0:T(8,128)(2,1)S(1)}, bf16[4,16,704]{2,1,0:T(8,128)(2,1)S(1)}, u32[]{:S(2)}, u32[]{:S(2)}) collective-permute-start(bf16[4,16,704]{2,1,0:T(8,128)(2,1)S(1)} %get-tuple-element.33), channel_id=1, source_target_pairs={{2,100},{3,101},{4,102},{5,103},{6,104},{7,105},{0,106},{1,107},{1... | collective-permute-start | bytes 270344 | tf_op jit(solution)/shard_map/ppermute | solution.py:556
  34.2 13.8 %copy-start = (bf16[704,2112]{1,0:T(8,128)(2,1)S(1)}, bf16[704,2112]{1,0:T(8,128)(2,1)}, u32[]{:S(2)}) copy-start(bf16[704,2112]{1,0:T(8,128)(2,1)} %refs_7_.5) | copy-start | bytes 8921092
  34.2 13.8 %copy-start.1 = (bf16[704,704]{1,0:T(8,128)(2,1)S(1)}, bf16[704,704]{1,0:T(8,128)(2,1)}, u32[]{:S(2)}) copy-start(bf16[704,704]{1,0:T(8,128)(2,1)} %refs_8_.5) | copy-start | bytes 2973700
  34.2 13.8 %copy-start.5 = (f32[16,704]{1,0:T(8,128)S(1)}, f32[16,704]{1,0:T(8,128)}, u32[]{:S(2)}) copy-start(f32[16,704]{1,0:T(8,128)} %refs_5_.3) | copy-start | bytes 135172
  34.3 13.8 %copy-start.6 = (f32[704]{0:T(1024)S(1)}, f32[704]{0:T(1024)}, u32[]{:S(2)}) copy-start(f32[704]{0:T(1024)} %refs_6_.5) | copy-start | bytes 8452
  34.3 13.8 %copy-start.9 = (s32[16]{0:T(128)S(1)}, s32[16]{0:T(128)}, u32[]{:S(2)}) copy-start(s32[16]{0:T(128)} %rank.3) | copy-start | bytes 196
  42.1 13.4 %collective-permute-start.11 = (bf16[4,16,704]{2,1,0:T(8,128)(2,1)S(1)}, bf16[4,16,704]{2,1,0:T(8,128)(2,1)S(1)}, u32[]{:S(2)}, u32[]{:S(2)}) collective-permute-start(bf16[4,16,704]{2,1,0:T(8,128)(2,1)S(1)} %get-tuple-element.42), channel_id=1, source_target_pairs={{2,0},{3,1},{4,2},{5,3},{6,4},{7,5},{0,6},{1,7},{10,8},{11,9},{12,... | collective-permute-start | bytes 270344 | tf_op jit(solution)/shard_map/ppermute | solution.py:556
  45.9 13.6 %collective-permute-start.12 = (bf16[4,16,704]{2,1,0:T(8,128)(2,1)S(1)}, bf16[4,16,704]{2,1,0:T(8,128)(2,1)S(1)}, u32[]{:S(2)}, u32[]{:S(2)}) collective-permute-start(bf16[4,16,704]{2,1,0:T(8,128)(2,1)S(1)} %get-tuple-element.43), channel_id=1, source_target_pairs={{2,33},{3,34},{4,35},{5,32},{6,37},{7,38},{0,39},{1,36},{10,41},{1... | collective-permute-start | bytes 270344 | tf_op jit(solution)/shard_map/ppermute | solution.py:556
  45.9 14.9 %collective-permute-start.13 = (bf16[4,16,704]{2,1,0:T(8,128)(2,1)S(1)}, bf16[4,16,704]{2,1,0:T(8,128)(2,1)S(1)}, u32[]{:S(2)}, u32[]{:S(2)}) collective-permute-start(bf16[4,16,704]{2,1,0:T(8,128)(2,1)S(1)} %get-tuple-element.44), channel_id=1, source_target_pairs={{2,68},{3,69},{4,70},{5,71},{6,72},{7,73},{0,74},{1,75},{10,76},{1... | collective-permute-start | bytes 270344 | tf_op jit(solution)/shard_map/ppermute | solution.py:556
  46.0 14.8 %collective-permute-start.14 = (bf16[4,16,704]{2,1,0:T(8,128)(2,1)S(1)}, bf16[4,16,704]{2,1,0:T(8,128)(2,1)S(1)}, u32[]{:S(2)}, u32[]{:S(2)}) collective-permute-start(bf16[4,16,704]{2,1,0:T(8,128)(2,1)S(1)} %get-tuple-element.45), channel_id=1, source_target_pairs={{2,101},{3,102},{4,103},{5,100},{6,105},{7,106},{0,107},{1,104},{1... | collective-permute-start | bytes 270344 | tf_op jit(solution)/shard_map/ppermute | solution.py:556
  51.8 14.9 %collective-permute-start.8 = (bf16[4,16,704]{2,1,0:T(8,128)(2,1)S(1)}, bf16[4,16,704]{2,1,0:T(8,128)(2,1)S(1)}, u32[]{:S(2)}, u32[]{:S(2)}) collective-permute-start(bf16[4,16,704]{2,1,0:T(8,128)(2,1)S(1)} %get-tuple-element.39), channel_id=1, source_target_pairs={{0,96},{32,0},{64,32},{96,64},{1,97},{33,1},{65,33},{97,65},{2,98}... | collective-permute-start | bytes 270344 | tf_op jit(solution)/shard_map/ppermute | solution.py:562
  55.6 12.0 %collective-permute-start.9 = (bf16[4,16,704]{2,1,0:T(8,128)(2,1)S(1)}, bf16[4,16,704]{2,1,0:T(8,128)(2,1)S(1)}, u32[]{:S(2)}, u32[]{:S(2)}) collective-permute-start(bf16[4,16,704]{2,1,0:T(8,128)(2,1)S(1)} %get-tuple-element.40), channel_id=1, source_target_pairs={{0,64},{32,96},{64,0},{96,32},{1,65},{33,97},{65,1},{97,33},{2,66}... | collective-permute-start | bytes 270344 | tf_op jit(solution)/shard_map/ppermute | solution.py:562
  59.5 8.1 %collective-permute-start.10 = (bf16[4,16,704]{2,1,0:T(8,128)(2,1)S(1)}, bf16[4,16,704]{2,1,0:T(8,128)(2,1)S(1)}, u32[]{:S(2)}, u32[]{:S(2)}) collective-permute-start(bf16[4,16,704]{2,1,0:T(8,128)(2,1)S(1)} %get-tuple-element.41), channel_id=1, source_target_pairs={{0,32},{32,64},{64,96},{96,0},{1,33},{33,65},{65,97},{97,1},{2,34}... | collective-permute-start | bytes 270344 | tf_op jit(solution)/shard_map/ppermute | solution.py:562
  64.6 5.2 %collective-permute-start.15 = (bf16[4,16,704]{2,1,0:T(8,128)(2,1)S(1)}, bf16[4,16,704]{2,1,0:T(8,128)(2,1)S(1)}, u32[]{:S(2)}, u32[]{:S(2)}) collective-permute-start(bf16[4,16,704]{2,1,0:T(8,128)(2,1)S(1)} %get-tuple-element.48), channel_id=1, source_target_pairs={{0,96},{32,0},{64,32},{96,64},{1,97},{33,1},{65,33},{97,65},{2,98}... | collective-permute-start | bytes 270344 | tf_op jit(solution)/shard_map/ppermute | solution.py:562
  66.6 6.2 %collective-permute-start.16 = (bf16[4,16,704]{2,1,0:T(8,128)(2,1)S(1)}, bf16[4,16,704]{2,1,0:T(8,128)(2,1)S(1)}, u32[]{:S(2)}, u32[]{:S(2)}) collective-permute-start(bf16[4,16,704]{2,1,0:T(8,128)(2,1)S(1)} %get-tuple-element.49), channel_id=1, source_target_pairs={{0,64},{32,96},{64,0},{96,32},{1,65},{33,97},{65,1},{97,33},{2,66}... | collective-permute-start | bytes 270344 | tf_op jit(solution)/shard_map/ppermute | solution.py:562
  66.8 6.9 %collective-permute-start.17 = (bf16[4,16,704]{2,1,0:T(8,128)(2,1)S(1)}, bf16[4,16,704]{2,1,0:T(8,128)(2,1)S(1)}, u32[]{:S(2)}, u32[]{:S(2)}) collective-permute-start(bf16[4,16,704]{2,1,0:T(8,128)(2,1)S(1)} %get-tuple-element.50), channel_id=1, source_target_pairs={{0,32},{32,64},{64,96},{96,0},{1,33},{33,65},{65,97},{97,1},{2,34}... | collective-permute-start | bytes 270344 | tf_op jit(solution)/shard_map/ppermute | solution.py:562
